TPU v7x, 32 devices: a whole 2x2x4 slice. The times are simulated.
32 devices in a mesh: dp: 4 (over z), section: 2 (over core), head: 4 (over y, x).
Axes of the slice: x: 2, y: 2, z: 4, core: 2. Of those that a mesh axis runs over, the one named last changes fastest.
Arguments:
- text_in: bfloat16 [512, 16, 768], P(('dp', 'section')), may hold values from -6 to 6
- lengths: int32 [512], P(('dp', 'section')), may hold values from 4 to 16, as said below
- image_embed: bfloat16 [512, 768], P(('dp', 'section')), may hold values from -6 to 6
- base_gain_one: float32 [768], replicated, may hold values from 0.25 to 1.75
- base_bias_one: float32 [768], replicated, may hold values from -1.75 to 1.75
- base_w_qkv: bfloat16 [768, 3, 768], P(None, None, 'head'), may hold values from -0.21875 to 0.21875
- base_b_qv: float32 [2, 768], P(None, 'head'), may hold values from -1.75 to 1.75
- base_w_out: bfloat16 [768, 768], P('head'), may hold values from -0.4375 to 0.4375
- base_b_out: float32 [768], replicated, may hold values from -1.75 to 1.75
- base_gain_two: float32 [768], replicated, may hold values from 0.25 to 1.75
- base_bias_two: float32 [768], replicated, may hold values from -1.75 to 1.75
- base_w_up: bfloat16 [768, 3072], P(None, 'head'), may hold values from -0.21875 to 0.21875
- base_b_up: float32 [3072], P('head'), may hold values from -1.75 to 1.75
- base_w_down: bfloat16 [3072, 768], P('head'), may hold values from -0.109375 to 0.109375
- base_b_down: float32 [768], replicated, may hold values from -1.75 to 1.75
- gain_one: float32 [768], replicated, may hold values from 0.25 to 1.75
- bias_one: float32 [768], replicated, may hold values from -1.75 to 1.75
- w_qkv: bfloat16 [768, 3, 768], P(None, None, 'head'), may hold values from -0.21875 to 0.21875
- b_qv: float32 [2, 768], P(None, 'head'), may hold values from -1.75 to 1.75
- output_weight: bfloat16 [768, 768], P('head'), may hold values from -0.4375 to 0.4375
- b_out: float32 [768], replicated, may hold values from -1.75 to 1.75
- gain_two: float32 [768], replicated, may hold values from 0.25 to 1.75
- bias_two: float32 [768], replicated, may hold values from -1.75 to 1.75
- w_up: bfloat16 [768, 3072], P(None, 'head'), may hold values from -0.21875 to 0.21875
- b_up: float32 [3072], P('head'), may hold values from -1.75 to 1.75
- w_down: bfloat16 [3072, 768], P('head'), may hold values from -0.109375 to 0.109375
- b_down: float32 [768], replicated, may hold values from -1.75 to 1.75
Outputs:
- loss: float32 [], replicated
- grad_text: float32 [512, 16, 768], P(('dp', 'section'))
- grad_base_gain_one: float32 [768], replicated
- grad_base_bias_one: float32 [768], replicated
- grad_base_w_qkv: float32 [768, 3, 768], P(None, None, 'head')
- grad_base_b_qv: float32 [2, 768], P(None, 'head')
- grad_base_w_out: float32 [768, 768], P('head')
- grad_base_b_out: float32 [768], replicated
- grad_base_gain_two: float32 [768], replicated
- grad_base_bias_two: float32 [768], replicated
- grad_base_w_up: float32 [768, 3072], P(None, 'head')
- grad_base_b_up: float32 [3072], P('head')
- grad_base_w_down: float32 [3072, 768], P('head')
- grad_base_b_down: float32 [768], replicated
- grad_gain_one: float32 [768], replicated
- grad_bias_one: float32 [768], replicated
- grad_w_qkv: float32 [768, 3, 768], P(None, None, 'head')
- grad_b_qv: float32 [2, 768], P(None, 'head')
- grad_w_out: float32 [768, 768], P('head')
- grad_b_out: float32 [768], replicated
- grad_gain_two: float32 [768], replicated
- grad_bias_two: float32 [768], replicated
- grad_w_up: float32 [768, 3072], P(None, 'head')
- grad_b_up: float32 [3072], P('head')
- grad_w_down: float32 [3072, 768], P('head')
- grad_b_down: float32 [768], replicated
Inputs may be any that keep to these rules, and one draw needn't show every extreme that they name: `lengths`: slots from a caption's length on are padding; some caption has 16 tokens and some 4.
All inputs are finite; a program needn't handle non-finite values.
Results may differ from a plain program's by a relative error of at most 0.029.
Values may be sent and summed in bfloat16 or wider, within the bound.
A program may use at most 128 MiB of HBM per device.

v0:
```python
import jax
import jax.numpy as jnp
from jax import lax
from jax.sharding import PartitionSpec as P

HEAD_DIM = 64


norm_eps = 1e-06
logit_scale = 50.0


def layer_norm(values, gain_vec, bias_vec):
    center = jnp.mean(values, -1, keepdims=True)
    shifted = values - center
    spread = jnp.mean(shifted * shifted, -1, keepdims=True)
    return shifted * lax.rsqrt(spread + norm_eps) * gain_vec + bias_vec


def unit_rows(values):
    return (
        values
        * lax.rsqrt(jnp.mean(values * values, -1, keepdims=True) + norm_eps)
        * values.shape[-1] ** (-0.5)
    )


def base_forward(inputs, valid, params):
    (
        gain_one,
        bias_one,
        w_qkv,
        b_qv,
        output_weight,
        b_out,
        gain_two,
        bias_two,
        w_up,
        b_up,
        w_down,
        b_down,
    ) = params
    bf_type = jnp.bfloat16
    float_kind = jnp.float32
    captions, slots, width = inputs.shape
    local_dim = w_qkv.shape[2]
    local_heads = local_dim // HEAD_DIM
    head_scale = HEAD_DIM ** (-0.5)
    normed_one, norm_one_back = jax.vjp(layer_norm, inputs, gain_one, bias_one)
    normed_low = normed_one.astype(bf_type)
    project = jnp.einsum("cld,dkh->clkh", normed_low, w_qkv, preferred_element_type=float_kind)
    query_heads = (
        (project[:, :, 0] + b_qv[0]).astype(bf_type).reshape(captions, slots, local_heads, HEAD_DIM)
    )
    key_heads = project[:, :, 1].astype(bf_type).reshape(captions, slots, local_heads, HEAD_DIM)
    value_heads = (
        (project[:, :, 2] + b_qv[1]).astype(bf_type).reshape(captions, slots, local_heads, HEAD_DIM)
    )
    scores = (
        jnp.einsum("cihe,cjhe->chij", query_heads, key_heads, preferred_element_type=float_kind)
        * head_scale
    )
    scores = jnp.where(valid[:, None, None, :], scores, -1000000000.0)
    probs = jax.nn.softmax(scores, -1)
    probs_low = probs.astype(bf_type)
    mixed_heads = (
        jnp.einsum("chij,cjhe->cihe", probs_low, value_heads, preferred_element_type=float_kind)
        .astype(bf_type)
        .reshape(captions, slots, local_dim)
    )
    attended_output = lax.psum(
        jnp.einsum(
            "umg,ge->ume", mixed_heads, output_weight, preferred_element_type=float_kind
        ).astype(jnp.bfloat16),
        "head",
    ).astype(jnp.float32)
    resid_one = inputs + attended_output + b_out
    normed_two, norm_two_back = jax.vjp(layer_norm, resid_one, gain_two, bias_two)
    normed_two_low = normed_two.astype(bf_type)
    upper = (
        jnp.einsum("cld,df->clf", normed_two_low, w_up, preferred_element_type=float_kind) + b_up
    )
    activated, gelu_back = jax.vjp(jax.nn.gelu, upper)
    hidden = activated.astype(bf_type)
    branch = lax.psum(
        jnp.einsum("clf,fd->cld", hidden, w_down, preferred_element_type=float_kind).astype(
            jnp.bfloat16
        ),
        "head",
    ).astype(jnp.float32)
    result = resid_one + branch + b_down
    saved = (
        norm_one_back,
        normed_low,
        query_heads,
        key_heads,
        value_heads,
        probs,
        probs_low,
        mixed_heads,
        norm_two_back,
        normed_two_low,
        gelu_back,
        hidden,
    )
    return (result, saved)


def base_backward(grad_result, saved, params):
    (
        gain_one,
        bias_one,
        w_qkv,
        b_qv,
        output_weight,
        b_out,
        gain_two,
        bias_two,
        w_up,
        b_up,
        w_down,
        b_down,
    ) = params
    (
        norm_one_back,
        normed_low,
        query_heads,
        key_heads,
        value_heads,
        probs,
        probs_low,
        mixed_heads,
        norm_two_back,
        normed_two_low,
        gelu_back,
        hidden,
    ) = saved
    bf_type = jnp.bfloat16
    float_kind = jnp.float32
    captions, slots, width = grad_result.shape
    local_dim = w_qkv.shape[2]
    local_heads = local_dim // HEAD_DIM
    head_scale = HEAD_DIM ** (-0.5)
    branch_grad = grad_result.astype(bf_type)
    grad_down = jnp.einsum("clf,cld->fd", hidden, branch_grad, preferred_element_type=float_kind)
    grad_down_bias = jnp.sum(grad_result, (0, 1))
    d_hidden = jnp.einsum("cld,fd->clf", branch_grad, w_down, preferred_element_type=float_kind)
    (d_upper,) = gelu_back(d_hidden)
    upper_grad = d_upper.astype(bf_type)
    grad_up = jnp.einsum(
        "cld,clf->df", normed_two_low, upper_grad, preferred_element_type=float_kind
    )
    grad_up_bias = jnp.sum(upper_grad.astype(float_kind), (0, 1))
    d_normed_two = lax.psum(
        jnp.einsum("clf,df->cld", upper_grad, w_up, preferred_element_type=float_kind).astype(
            jnp.bfloat16
        ),
        "head",
    ).astype(jnp.float32)
    d_resid_one, grad_gain_two, grad_bias_two = norm_two_back(d_normed_two)
    d_resid_one = d_resid_one + grad_result
    grad_out_bias = jnp.sum(d_resid_one, (0, 1))
    attended_gradient = d_resid_one.astype(bf_type)
    output_gradient = jnp.einsum(
        "zja,zjy->ay", mixed_heads, attended_gradient, preferred_element_type=float_kind
    )
    d_mixed = (
        jnp.einsum(
            "iob,jb->ioj", attended_gradient, output_weight, preferred_element_type=float_kind
        )
        .astype(bf_type)
        .reshape(captions, slots, local_heads, HEAD_DIM)
    )
    d_probs = jnp.einsum("cihe,cjhe->chij", d_mixed, value_heads, preferred_element_type=float_kind)
    d_scores = probs * (d_probs - jnp.sum(probs * d_probs, -1, keepdims=True))
    scores_grad = d_scores.astype(bf_type)
    d_query = (
        (
            jnp.einsum("chij,cjhe->cihe", scores_grad, key_heads, preferred_element_type=float_kind)
            * head_scale
        )
        .astype(bf_type)
        .reshape(captions, slots, local_dim)
    )
    d_keys = (
        (
            jnp.einsum(
                "chij,cihe->cjhe", scores_grad, query_heads, preferred_element_type=float_kind
            )
            * head_scale
        )
        .astype(bf_type)
        .reshape(captions, slots, local_dim)
    )
    d_values = (
        jnp.einsum("chij,cihe->cjhe", probs_low, d_mixed, preferred_element_type=float_kind)
        .astype(bf_type)
        .reshape(captions, slots, local_dim)
    )
    stacked = jnp.stack([d_query, d_keys, d_values], 2)
    grad_qkv = jnp.einsum("cld,clkh->dkh", normed_low, stacked, preferred_element_type=float_kind)
    grad_qv_bias = jnp.stack(
        [jnp.sum(d_query.astype(float_kind), (0, 1)), jnp.sum(d_values.astype(float_kind), (0, 1))],
        0,
    )
    d_normed_one = lax.psum(
        jnp.einsum("clkh,dkh->cld", stacked, w_qkv, preferred_element_type=float_kind).astype(
            jnp.bfloat16
        ),
        "head",
    ).astype(jnp.float32)
    d_input, grad_gain_one, grad_bias_one = norm_one_back(d_normed_one)
    d_input = d_input + d_resid_one
    grads = (
        grad_gain_one,
        grad_bias_one,
        grad_qkv,
        grad_qv_bias,
        output_gradient,
        grad_out_bias,
        grad_gain_two,
        grad_bias_two,
        grad_up,
        grad_up_bias,
        grad_down,
        grad_down_bias,
    )
    return (d_input, grads)


def on_device(
    text_in,
    lengths,
    image_embed,
    base_gain_one,
    base_bias_one,
    base_w_qkv,
    base_b_qv,
    base_w_out,
    base_b_out,
    base_gain_two,
    base_bias_two,
    base_w_up,
    base_b_up,
    base_w_down,
    base_b_down,
    gain_one,
    bias_one,
    w_qkv,
    b_qv,
    output_weight,
    b_out,
    gain_two,
    bias_two,
    w_up,
    b_up,
    w_down,
    b_down,
):
    bf_type = jnp.bfloat16
    float_kind = jnp.float32
    captions, slots, width = text_in.shape
    local_dim = w_qkv.shape[2]
    local_heads = local_dim // HEAD_DIM
    everyone = captions * lax.axis_size(("dp", "section"))
    head_scale = HEAD_DIM ** (-0.5)
    positions = jnp.arange(slots, dtype=jnp.int32)
    valid = positions[None, :] < lengths[:, None]
    picker = (positions[None, :] == lengths[:, None] - 1).astype(float_kind)
    base_params = (
        base_gain_one,
        base_bias_one,
        base_w_qkv,
        base_b_qv,
        base_w_out,
        base_b_out,
        base_gain_two,
        base_bias_two,
        base_w_up,
        base_b_up,
        base_w_down,
        base_b_down,
    )
    inputs, base_saved = base_forward(text_in.astype(float_kind), valid, base_params)
    normed_one, norm_one_back = jax.vjp(layer_norm, inputs, gain_one, bias_one)
    normed_low = normed_one.astype(bf_type)
    key_value = jnp.einsum(
        "cld,dkh->clkh", normed_low, w_qkv[:, 1:], preferred_element_type=float_kind
    )
    keys_low = key_value[:, :, 0].astype(bf_type)
    values_low = (key_value[:, :, 1] + b_qv[1]).astype(bf_type)
    pooled_low = jnp.einsum(
        "cl,cld->cd", picker.astype(bf_type), normed_low, preferred_element_type=float_kind
    ).astype(bf_type)
    query_low = (
        jnp.dot(pooled_low, w_qkv[:, 0], preferred_element_type=float_kind) + b_qv[0]
    ).astype(bf_type)
    query_heads = query_low.reshape(captions, local_heads, HEAD_DIM)
    key_heads = keys_low.reshape(captions, slots, local_heads, HEAD_DIM)
    value_heads = values_low.reshape(captions, slots, local_heads, HEAD_DIM)
    scores = (
        jnp.einsum("che,clhe->chl", query_heads, key_heads, preferred_element_type=float_kind)
        * head_scale
    )
    scores = jnp.where(valid[:, None, :], scores, -1000000000.0)
    probs = jax.nn.softmax(scores, -1)
    probs_low = probs.astype(bf_type)
    mixed_heads = (
        jnp.einsum("chl,clhe->che", probs_low, value_heads, preferred_element_type=float_kind)
        .astype(bf_type)
        .reshape(captions, local_dim)
    )
    attended_output = lax.psum(
        jnp.dot(mixed_heads, output_weight, preferred_element_type=float_kind).astype(jnp.bfloat16),
        "head",
    ).astype(jnp.float32)
    input_pool = jnp.sum(picker[:, :, None] * inputs, 1)
    resid_one = input_pool + attended_output + b_out
    normed_two, norm_two_back = jax.vjp(layer_norm, resid_one, gain_two, bias_two)
    normed_two_low = normed_two.astype(bf_type)
    upper = jnp.dot(normed_two_low, w_up, preferred_element_type=float_kind) + b_up
    activated, gelu_back = jax.vjp(jax.nn.gelu, upper)
    hidden = activated.astype(bf_type)
    branch = lax.psum(
        jnp.dot(hidden, w_down, preferred_element_type=float_kind).astype(jnp.bfloat16), "head"
    ).astype(jnp.float32)
    pooled = resid_one + branch + b_down
    text_unit, unit_back = jax.vjp(unit_rows, pooled)
    text_low = text_unit.astype(bf_type)
    image_low = unit_rows(image_embed.astype(float_kind)).astype(bf_type)
    all_images = lax.all_gather(image_low, ("dp", "section"), axis=0, tiled=True)
    first_row = lax.axis_index(("dp", "section")) * captions
    own_rows = jnp.arange(captions, dtype=jnp.int32) + first_row
    own_mask = jnp.arange(everyone, dtype=jnp.int32)[None, :] == own_rows[:, None]
    logits = logit_scale * jnp.einsum(
        "cd,bd->cb", text_low, all_images, preferred_element_type=float_kind
    )
    row_lse = jax.nn.logsumexp(logits, 1)
    diagonal = jnp.sum(jnp.where(own_mask, logits, 0.0), 1)
    row_grad = (
        (jnp.exp(logits - row_lse[:, None]) - own_mask.astype(float_kind)) / (2 * everyone)
    ).astype(bf_type)
    text_grad = logit_scale * jnp.dot(row_grad, all_images, preferred_element_type=float_kind)
    all_texts = lax.all_gather(text_low, ("dp", "section"), axis=0, tiled=True)
    column_logits = logit_scale * jnp.einsum(
        "bd,cd->bc", all_texts, image_low, preferred_element_type=float_kind
    )
    column_lse = jax.nn.logsumexp(column_logits, 0)
    column_mask = own_mask.T
    column_diag = jnp.sum(jnp.where(column_mask, column_logits, 0.0), 0)
    column_loss = jnp.sum(column_lse - column_diag)
    column_grad = (
        (jnp.exp(column_logits - column_lse[None, :]) - column_mask.astype(float_kind))
        / (2 * everyone)
    ).astype(bf_type)
    column_term = logit_scale * jnp.dot(column_grad, image_low, preferred_element_type=float_kind)
    text_grad = text_grad + lax.psum_scatter(
        column_term, ("dp", "section"), scatter_dimension=0, tiled=True
    )
    loss = lax.psum(jnp.sum(row_lse - diagonal) + column_loss, ("dp", "section")) / (2 * everyone)
    (d_pooled,) = unit_back(text_grad)
    branch_grad = d_pooled.astype(bf_type)
    grad_down = jnp.einsum("cf,cd->fd", hidden, branch_grad, preferred_element_type=float_kind)
    grad_down_bias = jnp.sum(d_pooled, 0)
    d_hidden = jnp.einsum("cd,fd->cf", branch_grad, w_down, preferred_element_type=float_kind)
    (d_upper,) = gelu_back(d_hidden)
    upper_grad = d_upper.astype(bf_type)
    grad_up = jnp.einsum("cd,cf->df", normed_two_low, upper_grad, preferred_element_type=float_kind)
    grad_up_bias = jnp.sum(upper_grad.astype(float_kind), 0)
    d_normed_two = lax.psum(
        jnp.einsum("cf,df->cd", upper_grad, w_up, preferred_element_type=float_kind).astype(
            jnp.bfloat16
        ),
        "head",
    ).astype(jnp.float32)
    d_resid_one, grad_gain_two, grad_bias_two = norm_two_back(d_normed_two)
    d_resid_one = d_resid_one + d_pooled
    grad_out_bias = jnp.sum(d_resid_one, 0)
    attended_gradient = d_resid_one.astype(bf_type)
    output_gradient = jnp.einsum(
        "ck,cd->kd", mixed_heads, attended_gradient, preferred_element_type=float_kind
    )
    d_mixed = (
        jnp.einsum("cd,kd->ck", attended_gradient, output_weight, preferred_element_type=float_kind)
        .astype(bf_type)
        .reshape(captions, local_heads, HEAD_DIM)
    )
    d_probs = jnp.einsum("che,clhe->chl", d_mixed, value_heads, preferred_element_type=float_kind)
    d_scores = probs * (d_probs - jnp.sum(probs * d_probs, -1, keepdims=True))
    scores_grad = d_scores.astype(bf_type)
    d_query = (
        (
            jnp.einsum("chl,clhe->che", scores_grad, key_heads, preferred_element_type=float_kind)
            * head_scale
        )
        .astype(bf_type)
        .reshape(captions, local_dim)
    )
    d_keys = (
        (
            jnp.einsum("chl,che->clhe", scores_grad, query_heads, preferred_element_type=float_kind)
            * head_scale
        )
        .astype(bf_type)
        .reshape(captions, slots, local_dim)
    )
    d_values = (
        jnp.einsum("chl,che->clhe", probs_low, d_mixed, preferred_element_type=float_kind)
        .astype(bf_type)
        .reshape(captions, slots, local_dim)
    )
    key_value_grad = jnp.stack([d_keys, d_values], 2)
    grad_query = jnp.einsum("cd,ck->dk", pooled_low, d_query, preferred_element_type=float_kind)
    grad_key_value = jnp.einsum(
        "cld,clkh->dkh", normed_low, key_value_grad, preferred_element_type=float_kind
    )
    grad_qkv = jnp.concatenate([grad_query[:, None, :], grad_key_value], 1)
    grad_qv_bias = jnp.stack(
        [jnp.sum(d_query.astype(float_kind), 0), jnp.sum(d_values.astype(float_kind), (0, 1))], 0
    )
    query_back = jnp.einsum("ck,dk->cd", d_query, w_qkv[:, 0], preferred_element_type=float_kind)
    d_normed_part = (
        jnp.einsum("clkh,dkh->cld", key_value_grad, w_qkv[:, 1:], preferred_element_type=float_kind)
        + picker[:, :, None] * query_back[:, None, :]
    )
    d_normed_one = lax.psum(d_normed_part.astype(jnp.bfloat16), "head").astype(jnp.float32)
    d_middle, grad_gain_one, grad_bias_one = norm_one_back(d_normed_one)
    d_middle = d_middle + picker[:, :, None] * d_resid_one[:, None, :]
    top_grads = (
        grad_gain_one,
        grad_bias_one,
        grad_qkv,
        grad_qv_bias,
        output_gradient,
        grad_out_bias,
        grad_gain_two,
        grad_bias_two,
        grad_up,
        grad_up_bias,
        grad_down,
        grad_down_bias,
    )
    d_text, base_grads = base_backward(d_middle, base_saved, base_params)
    summed = lax.psum(
        (
            base_grads[0],
            base_grads[1],
            base_grads[2],
            base_grads[3],
            base_grads[4],
            base_grads[5],
            base_grads[6],
            base_grads[7],
            base_grads[8],
            base_grads[9],
            base_grads[10],
            base_grads[11],
            top_grads[0],
            top_grads[1],
            top_grads[2],
            top_grads[3],
            top_grads[4],
            top_grads[5],
            top_grads[6],
            top_grads[7],
            top_grads[8],
            top_grads[9],
            top_grads[10],
            top_grads[11],
        ),
        ("dp", "section"),
    )
    return (loss, d_text) + tuple(summed)


def solution(mesh):
    placed = (
        P(("dp", "section"), None, None),
        P(("dp", "section")),
        P(("dp", "section"), None),
        P(),
        P(),
        P(None, None, "head"),
        P(None, "head"),
        P("head", None),
        P(),
        P(),
        P(),
        P(None, "head"),
        P("head"),
        P("head", None),
        P(),
        P(),
        P(),
        P(None, None, "head"),
        P(None, "head"),
        P("head", None),
        P(),
        P(),
        P(),
        P(None, "head"),
        P("head"),
        P("head", None),
        P(),
    )
    return jax.shard_map(
        on_device,
        mesh=mesh,
        in_specs=placed,
        out_specs=(
            P(),
            P(("dp", "section"), None, None),
            P(),
            P(),
            P(None, None, "head"),
            P(None, "head"),
            P("head", None),
            P(),
            P(),
            P(),
            P(None, "head"),
            P("head"),
            P("head", None),
            P(),
            P(),
            P(),
            P(None, None, "head"),
            P(None, "head"),
            P("head", None),
            P(),
            P(),
            P(),
            P(None, "head"),
            P("head"),
            P("head", None),
            P(),
        ),
        check_vma=False,
    )
```

profile of v0, /device:TPU:0, one launch (start us, length us, event | category | flops | bytes accessed | tf_op | source)
XLA Modules:
  0.0 985.1 jit_solution(11584092945271950507)
XLA Ops:
  19.4 2.9 copy.74
  25.4 3.0 copy.73
  28.5 2.5 add_convert_fusion.4
  31.0 2.6 copy.78
  33.6 3.9 fusion.151
  37.5 2.9 fusion.50
  44.0 2.8 convolution_convert_fusion.2
  47.1 63.5 %all-reduce.12.cloned.1.call-done = bf16[64,16,768]{2,1,0:T(8,128)(2,1)} async-done(((bf16[64,16,768]{2,1,0:T(8,128)(2,1)}), bf16[64,16,768]{2,1,0:T(8,128)(2,1)}) %all-reduce.12.cloned.1.call-update) | async-done | bytes 1572880 | tf_op jit(solution)/shard_map/psum | solution.py:71
  110.6 2.1 fusion.33
  117.3 3.3 convolution_convert_fusion.1
  122.3 59.4 %all-reduce.14.cloned.1.call-done = bf16[64,16,768]{2,1,0:T(8,128)(2,1)} async-done(((bf16[64,16,768]{2,1,0:T(8,128)(2,1)}), bf16[64,16,768]{2,1,0:T(8,128)(2,1)}) %all-reduce.14.cloned.1.call-update) | async-done | bytes 1572880 | tf_op jit(solution)/shard_map/psum | solution.py:85
  181.7 2.7 fusion.149
  201.5 2.9 copy.84
  208.6 17.2 %all_gather.6 = bf16[512,768]{1,0:T(8,128)(2,1)} all-gather(bf16[64,768]{1,0:T(8,128)(2,1)} %fusion.95), channel_id=1, replica_groups=mesh['dp'=4,'section'=2,'head'=4] {'dp','section'}, dimensions={0}, use_global_device_ids=true | all-gather | bytes 884736 | tf_op jit(solution)/shard_map/all_gather | solution.py:331
  225.8 24.8 %all-reduce.16.cloned.1.call-done = bf16[64,768]{1,0:T(8,128)(2,1)} async-done(((bf16[64,768]{1,0:T(8,128)(2,1)}), bf16[64,768]{1,0:T(8,128)(2,1)}) %all-reduce.16.cloned.1.call-update) | async-done | bytes 98320 | tf_op jit(solution)/shard_map/psum | solution.py:313
  253.7 2.2 convolution_convert_fusion.7
  256.0 41.9 %all-reduce.18.cloned.1.call-done = bf16[64,768]{1,0:T(8,128)(2,1)} async-done(((bf16[64,768]{1,0:T(8,128)(2,1)}), bf16[64,768]{1,0:T(8,128)(2,1)}) %all-reduce.18.cloned.1.call-update) | async-done | bytes 98320 | tf_op jit(solution)/shard_map/psum | solution.py:324
  300.0 15.6 %all_gather.7 = bf16[512,768]{1,0:T(8,128)(2,1)S(1)} all-gather(bf16[64,768]{1,0:T(8,128)(2,1)S(1)} %multiply_convert_fusion.6), channel_id=1, replica_groups=mesh['dp'=4,'section'=2,'head'=4] {'dp','section'}, dimensions={0}, use_global_device_ids=true | all-gather | bytes 884736 | tf_op jit(solution)/shard_map/all_gather | solution.py:344
  315.6 2.2 fusion.152
  322.6 32.9 %reduce-scatter.2.cloned.1.call-done = f32[64,768]{1,0:T(8,128)} async-done(((f32[512,768]{1,0:T(8,128)}), f32[64,768]{1,0:T(8,128)}) %reduce-scatter.2.cloned.1.call-update) | async-done | bytes 196624 | tf_op jit(solution)/shard_map/reduce_scatter | solution.py:357
  358.0 2.4 convert_reduce_fusion.9
  362.3 39.2 %all-reduce.20.cloned.1.call-done = bf16[64,768]{1,0:T(8,128)(2,1)} async-done(((bf16[64,768]{1,0:T(8,128)(2,1)}), bf16[64,768]{1,0:T(8,128)(2,1)}) %all-reduce.20.cloned.1.call-update) | async-done | bytes 98320 | tf_op jit(solution)/shard_map/psum | solution.py:370
  411.9 3.3 multiply_convert_fusion.4
  415.2 2.6 copy.90
  427.3 2.3 fusion.74
  429.6 2.7 copy.87
  432.3 2.6 copy.89
  434.9 3.7 fusion.31
  438.9 3.1 fusion.143
  447.4 52.2 %all-reduce.22.cloned.1.call-done = bf16[64,16,768]{2,1,0:T(8,128)(2,1)} async-done(((bf16[64,16,768]{2,1,0:T(8,128)(2,1)}), bf16[64,16,768]{2,1,0:T(8,128)(2,1)}) %all-reduce.22.cloned.1.call-update) | async-done | bytes 1572880 | tf_op jit(solution)/shard_map/psum | solution.py:426
  499.7 4.3 fusion.28
  506.0 4.1 convert_reduce_fusion.4
  511.2 2.6 convolution_convert_fusion
  513.9 6.5 convolution_bitcast_fusion
  520.4 54.5 %all-reduce.24.cloned.1.call-done = bf16[64,16,768]{2,1,0:T(8,128)(2,1)} async-done(((bf16[64,16,768]{2,1,0:T(8,128)(2,1)}), bf16[64,16,768]{2,1,0:T(8,128)(2,1)}) %all-reduce.24.cloned.1.call-update) | async-done | bytes 1572880 | tf_op jit(solution)/shard_map/psum | solution.py:154
  574.9 4.1 convert_reduce_fusion.1
  579.0 3.1 fusion.29
  582.1 2.4 fusion.146
  589.4 3.0 convert_reduce_fusion.6
  605.6 4.2 bitcast_convert_fusion
  610.2 5.3 convolution_bitcast_fusion.1
  617.2 2.8 convolution_bitcast_fusion.2
  622.1 48.8 %all-reduce.26.cloned.1.call-done = bf16[64,16,768]{2,1,0:T(8,128)(2,1)} async-done(((bf16[64,16,768]{2,1,0:T(8,128)(2,1)}), bf16[64,16,768]{2,1,0:T(8,128)(2,1)}) %all-reduce.26.cloned.1.call-update) | async-done | bytes 1572880 | tf_op jit(solution)/shard_map/psum | solution.py:206
  670.9 2.7 convert_reduce_fusion
  675.8 31.0 %all-reduce = (f32[]{:T(128)}, f32[768]{0:T(1024)}, f32[768]{0:T(1024)}, f32[2,192]{1,0:T(2,128)}, f32[768]{0:T(1024)}, /*index=5*/f32[768]{0:T(1024)}, f32[768]...) all-reduce(f32[]{:T(128)S(6)} %add.376, ...), channel_id=1, replica_groups=mesh['dp'=4,'section'=2,'head'=4] {'dp','section'}, use_global_device_ids=true, to_apply=%region_27.28 | all-reduce | flops 11521 | bytes 92168 | tf_op jit(solution)/shard_map/psum | solution.py:360
  707.4 4.1 add_add_fusion.3
  711.5 252.3 %all-reduce.28.cloned.1.call-done = (f32[768,3,192]{0,2,1:T(8,128)}, f32[192,768]{1,0:T(8,128)}, f32[768,768]{1,0:T(8,128)}, f32[768,768]{1,0:T(8,128)}, f32[768...) async-done(((f32[768,3,192]{0,2,1:T(8,128)}, f32[192,768]{1,0:T(8,128)}, f32[768,768]{1,0:T(8,128)}, f32[768,768]{1,0:T(8,128)}, ...) | async-done | bytes 14155792 | tf_op jit(solution)/shard_map/psum | solution.py:444
  963.8 2.9 copy.196
  (381 shorter events, 121.6 us)
Async XLA Ops:
  7.2 110.1 %copy-start = (bf16[768,768]{1,0:T(8,128)(2,1)S(1)}, bf16[768,768]{1,0:T(8,128)(2,1)}, u32[]{:S(2)}) copy-start(bf16[768,768]{1,0:T(8,128)(2,1)} %param.40) | copy-start | bytes 3538948
  7.3 103.3 %all-reduce.12.cloned.1.call-start = ((), (), s32[]{:S(2)}) async-start(), calls=%async_computation.1 | async-start | bytes 3145728 | tf_op jit(solution)/shard_map/psum | solution.py:71
  16.2 17.5 %copy-start.95 = (pred[64,16]{1,0:T(8,128)(4,1)}, pred[64,16]{1,0:T(8,128)(4,1)S(1)}, u32[]{:S(2)}) copy-start(pred[64,16]{1,0:T(8,128)(4,1)S(1)} %iota_compare_fusion.2) | copy-start | bytes 3076
  25.4 8.2 copy-start.19
  40.4 70.1 %copy-start.74 = (f32[768]{0:T(1024)S(1)}, f32[768]{0:T(1024)}, u32[]{:S(2)}) copy-start(f32[768]{0:T(1024)} %param.35) | copy-start | bytes 9220
  42.3 70.4 %copy-start.17 = (bf16[64,16,3,64]{0,3,2,1:T(8,128)(2,1)}, bf16[64,16,3,64]{0,3,2,1:T(8,128)(2,1)S(1)}, u32[]{:S(2)}) copy-start(bf16[64,16,3,64]{0,3,2,1:T(8,128)(2,1)S(1)} %copy.80) | copy-start | bytes 1179652
  46.8 66.8 %copy-start.82 = (f32[768]{0:T(1024)S(1)}, f32[768]{0:T(1024)}, u32[]{:S(2)}) copy-start(f32[768]{0:T(1024)} %param.36) | copy-start | bytes 9220
  46.8 66.8 %copy-start.112 = (f32[768]{0:T(1024)S(1)}, f32[768]{0:T(1024)}, u32[]{:S(2)}) copy-start(f32[768]{0:T(1024)} %param.37) | copy-start | bytes 9220
  46.8 134.8 %all-reduce.14.cloned.1.call-start = ((), (), s32[]{:S(2)}) async-start(), calls=%async_computation.2 | async-start | bytes 3145728 | tf_op jit(solution)/shard_map/psum | solution.py:85
  117.3 64.4 %copy-start.98 = (f32[768]{0:T(1024)S(1)}, f32[768]{0:T(1024)}, u32[]{:S(2)}) copy-start(f32[768]{0:T(1024)} %param.41) | copy-start | bytes 9220
  120.6 130.0 %all-reduce.16.cloned.1.call-start = ((), (), s32[]{:S(2)}) async-start(), calls=%async_computation.3 | async-start | bytes 196608 | tf_op jit(solution)/shard_map/psum | solution.py:313
  121.6 62.9 %copy-start.65 = (f32[64,16]{1,0:T(8,128)}, f32[64,16]{1,0:T(8,128)S(1)}, u32[]{:S(2)}) copy-start(f32[64,16]{1,0:T(8,128)S(1)} %get-tuple-element.102) | copy-start | bytes 12292
  189.3 8.8 copy-start.96
  194.6 11.5 %copy-start.12 = (bf16[64,16,1,192]{0,3,1,2:T(8,128)(2,1)}, bf16[64,16,1,192]{0,3,1,2:T(8,128)(2,1)S(1)}, u32[]{:S(2)}) copy-start(bf16[64,16,1,192]{0,3,1,2:T(8,128)(2,1)S(1)} %copy.159) | copy-start | bytes 1179652
  201.5 50.5 %copy-start.76 = (f32[768]{0:T(1024)S(1)}, f32[768]{0:T(1024)}, u32[]{:S(2)}) copy-start(f32[768]{0:T(1024)} %param.48) | copy-start | bytes 9220
  204.4 93.5 %copy-start.78 = (f32[768]{0:T(1024)S(1)}, f32[768]{0:T(1024)}, u32[]{:S(2)}) copy-start(f32[768]{0:T(1024)} %param.53) | copy-start | bytes 9220
  208.6 89.4 %all-reduce.18.cloned.1.call-start = ((), (), s32[]{:S(2)}) async-start(), calls=%async_computation.4 | async-start | bytes 196608 | tf_op jit(solution)/shard_map/psum | solution.py:324
  250.6 67.3 %copy-start.27 = (bf16[64,768]{1,0:T(8,128)(2,1)S(1)}, bf16[64,768]{1,0:T(8,128)(2,1)}, u32[]{:S(2)}) copy-start(bf16[64,768]{1,0:T(8,128)(2,1)} %fusion.95) | copy-start | bytes 294916
  251.8 47.2 %copy-start.84 = (f32[64]{0:T(128)}, f32[64]{0:T(128)S(1)}, u32[]{:S(2)}) copy-start(f32[64]{0:T(128)S(1)} %broadcast_multiply_fusion.4) | copy-start | bytes 772
  252.0 47.0 %copy-start.104 = (f32[64]{0:T(128)}, f32[64]{0:T(128)S(1)}, u32[]{:S(2)}) copy-start(f32[64]{0:T(128)S(1)} %multiply_reduce_fusion.10) | copy-start | bytes 772
  252.0 47.0 %copy-start.97 = (f32[64]{0:T(128)}, f32[64]{0:T(128)S(1)}, u32[]{:S(2)}) copy-start(f32[64]{0:T(128)S(1)} %fusion.132) | copy-start | bytes 772
  255.9 99.6 %reduce-scatter.2.cloned.1.call-start = ((), (), s32[]{:S(2)}) async-start(), calls=%async_computation.5 | async-start | bytes 1769472 | tf_op jit(solution)/shard_map/reduce_scatter | solution.py:357
  300.0 55.5 %copy-start.31 = (bf16[64,768]{1,0:T(8,128)(2,1)S(1)}, bf16[64,768]{1,0:T(8,128)(2,1)}, u32[]{:S(2)}) copy-start(bf16[64,768]{1,0:T(8,128)(2,1)} %all-reduce.18.cloned.1.call-done) | copy-start | bytes 294916
  320.8 40.8 %copy-start.58 = (bf16[64,192]{0,1:T(8,128)(2,1)S(1)}, bf16[64,192]{0,1:T(8,128)(2,1)}, u32[]{:S(2)}) copy-start(bf16[64,192]{0,1:T(8,128)(2,1)} %copy-done.57) | copy-start | bytes 73732
  320.8 80.7 %all-reduce.20.cloned.1.call-start = ((), (), s32[]{:S(2)}) async-start(), calls=%async_computation.6 | async-start | bytes 196608 | tf_op jit(solution)/shard_map/psum | solution.py:370
  360.4 45.1 %copy-start.59 = (bf16[64,768]{1,0:T(8,128)(2,1)}, bf16[64,768]{1,0:T(8,128)(2,1)S(1)}, u32[]{:S(2)}) copy-start(bf16[64,768]{1,0:T(8,128)(2,1)S(1)} %get-tuple-element.122) | copy-start | bytes 294916
  361.5 138.1 %all-reduce.22.cloned.1.call-start = ((), (), s32[]{:S(2)}) async-start(), calls=%async_computation.7 | async-start | bytes 3145728 | tf_op jit(solution)/shard_map/psum | solution.py:426
  438.6 136.2 %all-reduce.24.cloned.1.call-start = ((), (), s32[]{:S(2)}) async-start(), calls=%async_computation.8 | async-start | bytes 3145728 | tf_op jit(solution)/shard_map/psum | solution.py:154
  445.0 54.6 %copy-start.37 = (f32[64,16]{1,0:T(8,128)S(1)}, f32[64,16]{1,0:T(8,128)}, u32[]{:S(2)}) copy-start(f32[64,16]{1,0:T(8,128)} %copy-done.36) | copy-start | bytes 12292
  445.0 54.6 %copy-start.44 = (f32[64,16]{1,0:T(8,128)S(1)}, f32[64,16]{1,0:T(8,128)}, u32[]{:S(2)}) copy-start(f32[64,16]{1,0:T(8,128)} %copy-done.43) | copy-start | bytes 12292
  446.4 57.6 %copy-start.70 = (f32[64,16]{1,0:T(8,128)S(1)}, f32[64,16]{1,0:T(8,128)}, u32[]{:S(2)}) copy-start(f32[64,16]{1,0:T(8,128)} %copy-done.69) | copy-start | bytes 12292
  513.8 61.0 %copy-start.35 = (f32[64,16]{1,0:T(8,128)S(1)}, f32[64,16]{1,0:T(8,128)}, u32[]{:S(2)}) copy-start(f32[64,16]{1,0:T(8,128)} %copy-done.34) | copy-start | bytes 12292
  513.8 61.0 %copy-start.83 = (f32[768]{0:T(1024)S(1)}, f32[768]{0:T(1024)}, u32[]{:S(2)}) copy-start(f32[768]{0:T(1024)} %param.36) | copy-start | bytes 9220
  513.8 157.0 %all-reduce.26.cloned.1.call-start = ((), (), s32[]{:S(2)}) async-start(), calls=%async_computation.9 | async-start | bytes 3145728 | tf_op jit(solution)/shard_map/psum | solution.py:206
  520.4 58.6 %copy-start.68 = (f32[64,16]{1,0:T(8,128)S(1)}, f32[64,16]{1,0:T(8,128)}, u32[]{:S(2)}) copy-start(f32[64,16]{1,0:T(8,128)} %copy-done.67) | copy-start | bytes 12292
  520.4 58.6 %copy-start.64 = (f32[64,16]{1,0:T(8,128)S(1)}, f32[64,16]{1,0:T(8,128)}, u32[]{:S(2)}) copy-start(f32[64,16]{1,0:T(8,128)} %copy-done.63) | copy-start | bytes 12292
  609.8 353.9 %all-reduce.28.cloned.1.call-start = ((), (), s32[]{:S(2)}) async-start(), calls=%async_computation.10 | async-start | bytes 28311552 | tf_op jit(solution)/shard_map/psum | solution.py:444
  620.0 53.6 %copy-start.73 = (f32[64,16]{1,0:T(8,128)S(1)}, f32[64,16]{1,0:T(8,128)}, u32[]{:S(2)}) copy-start(f32[64,16]{1,0:T(8,128)} %copy-done.72) | copy-start | bytes 12292
  622.0 53.7 %copy-start.86 = (f32[768]{0:T(1024)S(1)}, f32[768]{0:T(1024)}, u32[]{:S(2)}) copy-start(f32[768]{0:T(1024)} %get-tuple-element.74) | copy-start | bytes 9220
  622.0 53.7 %copy-start.87 = (f32[768]{0:T(1024)S(1)}, f32[768]{0:T(1024)}, u32[]{:S(2)}) copy-start(f32[768]{0:T(1024)} %get-tuple-element.45) | copy-start | bytes 9220
  622.0 53.7 %copy-start.88 = (f32[768]{0:T(1024)S(1)}, f32[768]{0:T(1024)}, u32[]{:S(2)}) copy-start(f32[768]{0:T(1024)} %get-tuple-element.39) | copy-start | bytes 9220
  622.0 53.7 %copy-start.89 = (f32[768]{0:T(1024)S(1)}, f32[768]{0:T(1024)}, u32[]{:S(2)}) copy-start(f32[768]{0:T(1024)} %get-tuple-element.76) | copy-start | bytes 9220
  622.0 53.7 %copy-start.90 = (f32[768]{0:T(1024)S(1)}, f32[768]{0:T(1024)}, u32[]{:S(2)}) copy-start(f32[768]{0:T(1024)} %get-tuple-element.28) | copy-start | bytes 9220
  622.0 53.7 %copy-start.91 = (f32[768]{0:T(1024)S(1)}, f32[768]{0:T(1024)}, u32[]{:S(2)}) copy-start(f32[768]{0:T(1024)} %get-tuple-element.34) | copy-start | bytes 9220
  622.0 53.7 %copy-start.92 = (f32[768]{0:T(1024)S(1)}, f32[768]{0:T(1024)}, u32[]{:S(2)}) copy-start(f32[768]{0:T(1024)} %get-tuple-element.35) | copy-start | bytes 9220
  622.0 53.7 %copy-start.93 = (f32[768]{0:T(1024)S(1)}, f32[768]{0:T(1024)}, u32[]{:S(2)}) copy-start(f32[768]{0:T(1024)} %get-tuple-element.26) | copy-start | bytes 9220
  622.0 53.7 %copy-start.100 = (f32[768]{0:T(1024)S(1)}, f32[768]{0:T(1024)}, u32[]{:S(2)}) copy-start(f32[768]{0:T(1024)} %get-tuple-element.121) | copy-start | bytes 9220
  622.1 53.7 %copy-start.101 = (f32[768]{0:T(1024)S(1)}, f32[768]{0:T(1024)}, u32[]{:S(2)}) copy-start(f32[768]{0:T(1024)} %get-tuple-element.119) | copy-start | bytes 9220
  (81 other events, 230.1 us)
Sparse Core Ops, SparseCore 0:
  46.9 63.5 all-reduce.11
  120.7 60.8 all-reduce.13
  208.7 41.8 all-reduce.15
  256.0 41.8 all-reduce.17
  320.9 34.5 reduce-scatter.1
  361.7 39.8 all-reduce.19
  438.7 60.8 all-reduce.21
  513.9 60.8 all-reduce.23
  609.9 60.8 all-reduce.25
  676.0 287.7 all-reduce.27
where the time goes:
time: 994 us; the launch traced here: 985 us
  waiting for transfers between devices  670 us (67%)
  matrix products  80.9 us (8%)
  local copies, waits for them, and re-layouts  78.5 us (8%)
  other arithmetic  72 us (7%)
  blocking collectives  63.8 us (6%)
  between operations  19.2 us (2%)
    psum x1, waiting for transfers between devices, on_device(): lax.psum((base_grads[0], base_grads[1], base_grads[2], base_grads[3], bas...  252 us
    psum x1, waiting for transfers between devices, base_forward(): lax.psum(jnp.einsum('umg,ge->ume', mixed_heads, output_weight, preferred_...  63.5 us
    psum x1, waiting for transfers between devices, base_forward(): lax.psum(jnp.einsum('clf,fd->cld', hidden, w_down, preferred_element_type...  59.4 us
    psum x1, waiting for transfers between devices, base_backward(): lax.psum(jnp.einsum('clf,df->cld', upper_grad, w_up, preferred_element_ty...  54.5 us
    psum x1, waiting for transfers between devices, on_device(): lax.psum(d_normed_part.astype(jnp.bfloat16), 'head').astype(jnp.float32)  52.2 us
    psum x1, waiting for transfers between devices, base_backward(): lax.psum(jnp.einsum('clkh,dkh->cld', stacked, w_qkv, preferred_element_ty...  48.8 us
    psum x1, waiting for transfers between devices, on_device(): lax.psum(jnp.dot(hidden, w_down, preferred_element_type=float_kind).astyp...  41.9 us
    psum x1, waiting for transfers between devices, on_device(): lax.psum(jnp.einsum('cf,df->cd', upper_grad, w_up, preferred_element_type...  39.2 us
  transfers between devices with their start and end apart: 10, of which 10 were waited for; matrix products, arithmetic and copies ran while one was open for 4% of the time, Pallas kernels for 0%

commit v1 on v0

v1 whole, which is shorter than its diff:
```python
import functools

import jax
import jax.numpy as jnp
from jax import lax
from jax.experimental import pallas as pl
from jax.experimental.pallas import tpu as pltpu
from jax.sharding import PartitionSpec as P

HEAD_DIM = 64
NORM_EPS = 1e-06
LOGIT_SCALE = 50.0
NEG = -1e30
BF = jnp.bfloat16
F32 = jnp.float32
MESH = pl.DeviceIdType.MESH
VMEM_LIMIT = 56 * 2**20


def dot(a, b):
    return lax.dot_general(a, b, (((1,), (0,)), ((), ())), preferred_element_type=F32)


def dot_nt(a, b):
    return lax.dot_general(a, b, (((1,), (1,)), ((), ())), preferred_element_type=F32)


def dot_tn(a, b):
    return lax.dot_general(a, b, (((0,), (0,)), ((), ())), preferred_element_type=F32)


def norm_stats(values):
    center = jnp.mean(values, -1, keepdims=True)
    shifted = values - center
    spread = jnp.mean(shifted * shifted, -1, keepdims=True)
    rstd = lax.rsqrt(spread + NORM_EPS)
    return shifted * rstd, rstd


def norm_back(grad, hat, rstd, gain):
    scaled = grad * gain
    m1 = jnp.mean(scaled, -1, keepdims=True)
    m2 = jnp.mean(scaled * hat, -1, keepdims=True)
    return rstd * (scaled - m1 - hat * m2)


def rows_sum(values):
    return jnp.sum(values, 0, keepdims=True)


def gelu_pair(u):
    c = 0.7978845608028654
    u2 = u * u
    t = jnp.tanh(c * u * (1.0 + 0.044715 * u2))
    half = 0.5 * (1.0 + t)
    value = u * half
    slope = half + 0.5 * u * (1.0 - t * t) * (c * (1.0 + 3.0 * 0.044715 * u2))
    return value, slope


def head_masks(width, kind):
    lane = lax.broadcasted_iota(jnp.int32, (1, width), 1)
    return [
        jnp.where((lane >= i * HEAD_DIM) & (lane < (i + 1) * HEAD_DIM), 1.0, 0.0).astype(kind)
        for i in range(width // HEAD_DIM)
    ]


class Place:
    def __init__(self):
        self.z = lax.axis_index("dp")
        self.s = lax.axis_index("section")
        h = lax.axis_index("head")
        self.h = h
        self.hi = lax.div(h, 2)
        self.lo = lax.rem(h, 2)
        self.hx = self.block(0, 1)
        self.hy = self.block(1, 0)
        self.hd = self.block(1, 1)

    def block(self, flip_hi, flip_lo):
        return lax.rem(self.hi + flip_hi, 2) * 2 + lax.rem(self.lo + flip_lo, 2)

    def head(self, other):
        return (self.z, self.s, other)

    def greet(self, devices):
        barrier = pltpu.get_barrier_semaphore()
        for device in devices:
            pl.semaphore_signal(barrier, inc=1, device_id=device, device_id_type=MESH)
        pl.semaphore_wait(barrier, len(devices))


def remote(src, dst, send_sem, recv_sem, device):
    return pltpu.make_async_remote_copy(
        src_ref=src,
        dst_ref=dst,
        send_sem=send_sem,
        recv_sem=recv_sem,
        device_id=device,
        device_id_type=MESH,
    )


class Gather:
    def __init__(self, at, ref, send, recv, block):
        half = block // 2

        def rows(owner, part):
            return ref.at[pl.ds(pl.multiple_of(owner * block + part * half, half), half)]

        def copy(i, owner, part, target):
            piece = rows(owner, part)
            return remote(piece, piece, send.at[i], recv.at[i], at.head(target))

        self.c = [
            copy(0, at.h, 0, at.hx),
            copy(1, at.h, 1, at.hy),
            copy(2, at.h, 1, at.hx),
            copy(3, at.h, 0, at.hy),
            copy(4, at.hx, 0, at.hy),
            copy(5, at.hy, 1, at.hx),
        ]

    def start(self):
        for i in range(4):
            self.c[i].start()

    def forward(self):
        self.c[0].wait_recv()
        self.c[4].start()
        self.c[1].wait_recv()
        self.c[5].start()

    def wait_x(self):
        self.c[2].wait_recv()

    def wait_y(self):
        self.c[3].wait_recv()

    def wait_d(self):
        self.c[4].wait_recv()
        self.c[5].wait_recv()

    def finish(self):
        for copy in self.c:
            copy.wait_send()


class Scatter:
    def __init__(self, at, part, got, send, recv, block):
        half = block // 2
        self.at, self.part, self.got, self.half = at, part, got, half

        def piece(owner, side):
            return part.at[owner, pl.ds(side * half, half)]

        def copy(i, owner, side, target):
            return remote(piece(owner, side), got.at[i], send.at[i], recv.at[i], at.head(target))

        self.c = [
            copy(0, at.hd, 0, at.hx),
            copy(1, at.hd, 1, at.hy),
            copy(2, at.hx, 0, at.hx),
            copy(3, at.hy, 1, at.hy),
            copy(4, at.hy, 0, at.hy),
            copy(5, at.hx, 1, at.hx),
        ]

    def send_d(self):
        self.c[0].start()
        self.c[1].start()

    def send_x(self):
        self.c[2].start()

    def send_y(self):
        self.c[3].start()

    def second(self):
        half, part, got, at = self.half, self.part, self.got, self.at
        self.c[0].wait_recv()
        part[at.hy, :half] = (part[at.hy, :half].astype(F32) + got[0].astype(F32)).astype(BF)
        self.c[4].start()
        self.c[1].wait_recv()
        part[at.hx, half:] = (part[at.hx, half:].astype(F32) + got[1].astype(F32)).astype(BF)
        self.c[5].start()

    def wait(self):
        for i in (2, 3, 4, 5):
            self.c[i].wait_recv()

    def total(self):
        half, part, got, at = self.half, self.part, self.got, self.at
        top = part[at.h, :half].astype(F32) + got[2].astype(F32) + got[4].astype(F32)
        low = part[at.h, half:].astype(F32) + got[3].astype(F32) + got[5].astype(F32)
        return jnp.concatenate([top, low], 0)

    def finish(self):
        for copy in self.c:
            copy.wait_send()


def first_forward_kernel(
    dp,
    block,
    slots,
    x,
    kbias,
    image,
    g1,
    c1,
    wqkv,
    bqv,
    wo,
    bo,
    g2,
    c2,
    wu,
    bu,
    wd,
    bd,
    w2,
    b2,
    n1,
    q,
    k,
    v,
    p,
    o,
    n2,
    hid,
    slope,
    r1,
    z,
    w2all,
    b2all,
    images,
    part_a,
    got_a,
    part_b,
    got_b,
    unit,
    sa_send,
    sa_recv,
    ag_send,
    ag_recv,
    sb_send,
    sb_recv,
    w_send,
    w_recv,
    b_send,
    b_recv,
    i_send,
    i_recv,
    local_sem,
):
    at = Place()
    local = wo.shape[0]
    heads = local // HEAD_DIM
    sub = 128
    other_core = (at.z, 1 - at.s, at.h)
    zs = [(lax.rem(at.z + j, dp), at.s, at.h) for j in range(1, dp)]
    z_pair = (at.z + 1 - 2 * lax.rem(at.z, 2), at.s, at.h)
    head_peers = [at.hx, at.hy, at.hd]

    own_w = pltpu.make_async_copy(w2, w2all.at[at.h], local_sem.at[0])
    own_w.start()
    own_b = pltpu.make_async_copy(b2, b2all.at[at.h], local_sem.at[1])
    own_b.start()
    pic = image[...].astype(F32)
    width = pic.shape[1]
    pic = pic * lax.rsqrt(jnp.mean(pic * pic, -1, keepdims=True) + NORM_EPS) * width ** (-0.5)
    unit[...] = pic.astype(BF)
    own_i = pltpu.make_async_copy(unit, images.at[at.z, at.s], local_sem.at[2])
    own_i.start()

    at.greet([at.head(j) for j in head_peers] + zs + [other_core])

    quarter = w2.shape[1] // 4
    mine = lax.rem(at.z, 2) * 2 + at.s
    pair = (1 - lax.rem(at.z, 2)) * 2 + at.s

    def span(which):
        return pl.ds(pl.multiple_of(which * quarter, quarter), quarter)

    hop1 = []
    for i, j in enumerate(head_peers):
        hop1.append(
            remote(
                w2.at[:, span(mine)],
                w2all.at[at.h, :, span(mine)],
                w_send.at[i],
                w_recv.at[i],
                at.head(j),
            )
        )
        hop1.append(remote(b2, b2all.at[at.h], b_send.at[i], b_recv.at[i], at.head(j)))
    hop2, hop3 = [], []
    for i, j in enumerate(head_peers):
        piece = w2all.at[j, :, span(mine)]
        hop2.append(remote(piece, piece, w_send.at[3 + i], w_recv.at[3 + i], z_pair))
        hop3.append(remote(piece, piece, w_send.at[6 + i], w_recv.at[6 + i], other_core))
        piece = w2all.at[j, :, span(pair)]
        hop3.append(remote(piece, piece, w_send.at[9 + i], w_recv.at[9 + i], other_core))
    for copy in hop1:
        copy.start()
    pics = [
        remote(unit, images.at[at.z, at.s], i_send.at[i], i_recv.at[i], device)
        for i, device in enumerate(zs)
    ]
    for copy in pics:
        copy.start()
    core_pics = remote(
        images.at[:, at.s], images.at[:, at.s], i_send.at[dp - 1], i_recv.at[dp - 1], other_core
    )

    scatter = Scatter(at, part_a, got_a, sa_send, sa_recv, block)
    masks_low = head_masks(local, BF)
    masks = head_masks(local, F32)
    row_id = lax.broadcasted_iota(jnp.int32, (sub, sub), 0) // slots
    col_id = lax.broadcasted_iota(jnp.int32, (sub, sub), 1) // slots
    same = row_id == col_id

    def attend(t, carry):
        blk = lax.rem(at.hi + lax.rem(t + 1, 2), 2) * 2 + lax.rem(at.lo + lax.div(3 - t, 2), 2)
        first = pl.multiple_of(blk * block, block)
        rows = pl.ds(first, block)
        hat, _ = norm_stats(x[rows].astype(F32))
        normed = (hat * g1[...] + c1[...]).astype(BF)
        n1[rows] = normed
        query = (dot(normed, wqkv[0]) + bqv[0]).astype(BF)
        keys = dot(normed, wqkv[1]).astype(BF)
        values = (dot(normed, wqkv[2]) + bqv[1]).astype(BF)
        q[rows] = query
        k[rows] = keys
        v[rows] = values
        mixed = []
        for m in range(block // sub):
            cut = slice(m * sub, (m + 1) * sub)
            index = blk * (block // sub) + m
            bias = jnp.where(same, kbias[index], NEG)
            total = jnp.zeros((sub, local), F32)
            for i in range(heads):
                scores = dot_nt(query[cut] * masks_low[i], keys[cut]) * HEAD_DIM ** (-0.5) + bias
                scores = jnp.exp(scores - jnp.max(scores, -1, keepdims=True))
                probs = (scores * (1.0 / jnp.sum(scores, -1, keepdims=True))).astype(BF)
                p[index, i] = probs
                total = total + dot(probs, values[cut]) * masks[i]
            mixed.append(total.astype(BF))
        mixed = jnp.concatenate(mixed, 0)
        o[rows] = mixed
        part_a[blk] = dot(mixed, wo[...]).astype(BF)
        pl.when(t == 0)(scatter.send_d)
        pl.when(t == 1)(scatter.send_x)
        pl.when(t == 2)(scatter.send_y)
        return carry

    lax.fori_loop(0, 4, attend, 0)
    scatter.second()
    for i in range(3):
        hop1[2 * i].wait_recv()
        hop2[i].start()
    scatter.wait()
    own = pl.ds(pl.multiple_of(at.h * block, block), block)
    resid = x[own].astype(F32) + scatter.total() + bo[...]
    r1[...] = resid
    hat, _ = norm_stats(resid)
    n2[own] = (hat * g2[...] + c2[...]).astype(BF)

    gather = Gather(at, n2, ag_send, ag_recv, block)
    gather.start()
    spread = Scatter(at, part_b, got_b, sb_send, sb_recv, block)

    def feed(t, carry):
        @pl.when(t == 1)
        def _():
            gather.forward()
            gather.wait_x()

        pl.when(t == 2)(gather.wait_y)
        pl.when(t == 3)(gather.wait_d)
        blk = lax.rem(at.hi + lax.div(t, 2), 2) * 2 + lax.rem(at.lo + lax.rem(t, 2), 2)
        rows = pl.ds(pl.multiple_of(blk * block, block), block)
        value, steep = gelu_pair(dot(n2[rows], wu[...]) + bu[...])
        value = value.astype(BF)
        hid[rows] = value
        slope[rows] = steep.astype(BF)
        part_b[blk] = dot(value, wd[...]).astype(BF)
        pl.when(t == 1)(spread.send_x)
        pl.when(t == 2)(spread.send_y)
        pl.when(t == 3)(spread.send_d)
        return carry

    lax.fori_loop(0, 4, feed, 0)
    for i in range(3):
        hop2[i].wait_recv()
        hop3[2 * i].start()
        hop3[2 * i + 1].start()
    own_i.wait()
    for copy in pics:
        copy.wait_recv()
    core_pics.start()
    spread.second()
    spread.wait()
    z[...] = r1[...] + spread.total() + bd[...]
    own_w.wait()
    own_b.wait()
    for i in range(3):
        hop1[2 * i + 1].wait_recv()
    for copy in hop3:
        copy.wait_recv()
    core_pics.wait_recv()
    for copy in hop1 + hop2 + hop3 + pics + [core_pics]:
        copy.wait_send()
    scatter.finish()
    gather.finish()
    spread.finish()


def first_forward(dp, section, x, kbias, image, base, w2, b2):
    g1, c1, wqkv, bqv, wo, bo, g2, c2, wu, bu, wd, bd = base
    tokens, width = x.shape
    local = wo.shape[0]
    ff = wu.shape[1]
    block = tokens // 4
    heads = local // HEAD_DIM
    captions = image.shape[0]
    slots = tokens // captions
    vmem = pl.BlockSpec(memory_space=pltpu.VMEM)
    hbm = pl.BlockSpec(memory_space=pl.ANY)
    shape = jax.ShapeDtypeStruct
    outs = [
        shape((tokens, width), BF),
        shape((tokens, local), BF),
        shape((tokens, local), BF),
        shape((tokens, local), BF),
        shape((tokens // 128, heads, 128, 128), BF),
        shape((tokens, local), BF),
        shape((tokens, width), BF),
        shape((tokens, ff), BF),
        shape((tokens, ff), BF),
        shape((block, width), F32),
        shape((block, width), F32),
        shape((4,) + w2.shape, BF),
        shape((4,) + b2.shape, F32),
        shape((dp, section, captions, width), BF),
    ]
    sems = pltpu.SemaphoreType.DMA
    return pl.pallas_call(
        functools.partial(first_forward_kernel, dp, block, slots),
        out_shape=outs,
        in_specs=[vmem] * 15 + [hbm] * 2,
        out_specs=[vmem] * 11 + [hbm] * 3,
        scratch_shapes=[
            pltpu.VMEM((4, block, width), BF),
            pltpu.VMEM((6, block // 2, width), BF),
            pltpu.VMEM((4, block, width), BF),
            pltpu.VMEM((6, block // 2, width), BF),
            pltpu.VMEM((captions, width), BF),
            sems((6,)),
            sems((6,)),
            sems((6,)),
            sems((6,)),
            sems((6,)),
            sems((6,)),
            sems((12,)),
            sems((12,)),
            sems((3,)),
            sems((3,)),
            sems((dp,)),
            sems((dp,)),
            sems((3,)),
        ],
        compiler_params=pltpu.CompilerParams(
            collective_id=0, has_side_effects=True, vmem_limit_bytes=VMEM_LIMIT
        ),
        cost_estimate=pl.CostEstimate(
            flops=4 * 10**9, bytes_accessed=20 * 10**6, transcendentals=10**6
        ),
    )(x, kbias, image, g1, c1, wqkv, bqv, wo, bo, g2, c2, wu, bu, wd, bd, w2, b2)


def second_kernel(
    dp,
    section,
    slots,
    z,
    kbias,
    pick,
    pcol,
    images,
    w2,
    b2,
    g1,
    c1,
    bo,
    g2,
    c2,
    wu,
    bu,
    wd,
    bd,
    dz,
    loss,
    g_qkv,
    g_wo,
    g_wu,
    g_wd,
    g_vec,
    g_bqv,
    g_bu,
    ring,
    arb,
    stats,
    dpool,
    dn2b,
    rsb,
    f_out,
    f_in,
    s_out,
    s_in,
    a_in,
    send,
    recv,
    st_send,
    st_recv,
):
    at = Place()
    head_peers = [at.hx, at.hy, at.hd]
    others = []
    for j in range(dp):
        for i in range(section):
            if i or j:
                others.append((lax.rem(at.z + j, dp), lax.rem(at.s + i, section), at.h))
    at.greet([at.head(j) for j in head_peers] + others)

    block, width = z.shape
    own_caps = block // slots
    caps = 4 * own_caps
    local = w2.shape[3]
    heads = local // HEAD_DIM
    scale = HEAD_DIM ** (-0.5)
    low_masks = head_masks(local, BF)
    masks = head_masks(local, F32)

    def stack(values):
        return jnp.concatenate([values * low_masks[i] for i in range(heads)], 0)

    def pick_heads(values):
        total = values[:own_caps] * masks[0]
        for i in range(1, heads):
            total = total + values[i * own_caps : (i + 1) * own_caps] * masks[i]
        return total

    zv = z[...]
    hat1, rstd1 = norm_stats(zv)
    normed = (hat1 * g1[...] + c1[...]).astype(BF)
    pooled_low = dot(pick[...], normed).astype(BF)
    a_in[at.h, 0] = pooled_low
    z_pool = jnp.sum((zv * pcol[...]).reshape(own_caps, slots, width), 1)
    us = []
    for j in range(4):
        query = (dot(pooled_low, w2[j, 0]) + b2[j, 0:1]).astype(BF)
        s_out[j, 0] = query
        us.append(dot_nt(stack(query), w2[j, 1]).astype(BF))
    u_all = jnp.concatenate(us, 0)
    rows_n = 4 * heads * own_caps
    row_cap = lax.rem(lax.broadcasted_iota(jnp.int32, (rows_n, block), 0), own_caps)
    col_cap = lax.broadcasted_iota(jnp.int32, (rows_n, block), 1) // slots
    bias = jnp.where(row_cap == col_cap, kbias[...], NEG)
    scores = dot_nt(u_all, normed) * scale + bias
    scores = jnp.exp(scores - jnp.max(scores, -1, keepdims=True))
    probs = scores * (1.0 / jnp.sum(scores, -1, keepdims=True))
    probs_low = probs.astype(BF)
    mix = dot(probs_low, normed).astype(BF)
    attended = jnp.zeros((own_caps, width), F32)
    per = heads * own_caps
    for j in range(4):
        part = mix[j * per : (j + 1) * per]
        f_out[j, 0] = part
        out = (pick_heads(dot(part, w2[j, 2])) + b2[j, 1:2]).astype(BF)
        s_out[j, 3] = out
        attended = attended + dot_nt(out, w2[j, 3])
    r1 = z_pool + attended + bo[...]
    ring[at.h] = r1
    rings = [
        remote(ring.at[at.h], ring.at[at.h], send.at[i], recv.at[i], at.head(j))
        for i, j in enumerate(head_peers)
    ]
    for copy in rings:
        copy.start()
    for copy in rings:
        copy.wait_recv()

    r1_all = ring[...].reshape(caps, width)
    hat2_all, _ = norm_stats(r1_all)
    n2 = (hat2_all * g2[...] + c2[...]).astype(BF)
    value, slope = gelu_pair(dot(n2, wu[...]) + bu[...])
    value = value.astype(BF)
    arb[at.h] = dot(value, wd[...]).astype(BF)
    sums = [
        remote(arb.at[at.h], arb.at[at.h], send.at[3 + i], recv.at[3 + i], at.head(j))
        for i, j in enumerate(head_peers)
    ]
    for copy in sums:
        copy.start()
    for copy in sums:
        copy.wait_recv()
    pooled = r1_all + bd[...]
    for j in range(4):
        pooled = pooled + arb[j].astype(F32)
    unit_r = lax.rsqrt(jnp.mean(pooled * pooled, -1, keepdims=True) + NORM_EPS)
    text = (pooled * unit_r * width ** (-0.5)).astype(BF)

    everyone = dp * section * caps
    images_all = images[...].reshape(everyone, width)
    logits = LOGIT_SCALE * dot_nt(text, images_all)
    place = at.z * section + at.s
    col = lax.broadcasted_iota(jnp.int32, (caps, everyone), 1)
    row = lax.broadcasted_iota(jnp.int32, (caps, everyone), 0) + place * caps
    diag = col == row
    eye = jnp.where(diag, 1.0, 0.0)
    row_max = jnp.max(logits, 1, keepdims=True)
    row_exp = jnp.exp(logits - row_max)
    row_sum = jnp.sum(row_exp, 1, keepdims=True)
    diagonal = jnp.sum(jnp.where(diag, logits, 0.0), 1, keepdims=True)
    row_loss = jnp.sum(row_max + jnp.log(row_sum) - 2.0 * diagonal, 0, keepdims=True)
    col_max = jnp.max(logits, 0, keepdims=True)
    col_sum = jnp.sum(jnp.exp(logits - col_max), 0, keepdims=True)
    stats[place, 0:1] = col_max
    stats[place, 1:2] = col_sum
    stats[place, 2:3] = jnp.broadcast_to(row_loss, (1, everyone))
    tells = [
        remote(stats.at[place], stats.at[place], st_send.at[i], st_recv.at[i], device)
        for i, device in enumerate(others)
    ]
    for copy in tells:
        copy.start()
    row_grad = ((row_exp * (1.0 / row_sum) - eye) * (0.5 / everyone)).astype(BF)
    text_grad = dot(row_grad, images_all)
    for copy in tells:
        copy.wait_recv()
    told = stats[...]
    top = jnp.max(told[:, 0:1], 0)
    total = jnp.sum(told[:, 1:2] * jnp.exp(told[:, 0:1] - top[None]), 0)
    col_lse = top + jnp.log(total)
    whole_loss = jnp.sum(told[:, 2:3, 0:1], 0) + jnp.sum(col_lse, 1, keepdims=True)
    loss[...] = whole_loss * (0.5 / everyone)
    col_grad = ((jnp.exp(logits - col_lse) - eye) * (0.5 / everyone)).astype(BF)
    text_grad = LOGIT_SCALE * (text_grad + dot(col_grad, images_all))
    inner = jnp.mean(pooled * text_grad, -1, keepdims=True)
    d_pool = (unit_r * width ** (-0.5)) * (text_grad - pooled * (unit_r * unit_r * inner))
    dpool[...] = d_pool

    dm = d_pool.astype(BF)
    du = (dot_nt(dm, wd[...]) * slope).astype(BF)
    dn2b[...] = dot_nt(du, wu[...]).astype(BF)
    own_rows = pl.ds(pl.multiple_of(at.h * own_caps, own_caps), own_caps)
    backs = []
    for i, j in enumerate(head_peers):
        rows = pl.ds(pl.multiple_of(j * own_caps, own_caps), own_caps)
        backs.append(
            remote(dn2b.at[rows], rsb.at[at.h], send.at[6 + i], recv.at[6 + i], at.head(j))
        )
    for copy in backs:
        copy.start()
    g_wd[...] = dot_tn(value, dm).astype(BF)
    g_wu[...] = dot_tn(n2, du).astype(BF)
    g_bu[...] = rows_sum(du.astype(F32))
    rsb[at.h] = dn2b[own_rows]
    for copy in backs:
        copy.wait_recv()
    dn2 = rsb[0].astype(F32)
    for j in range(1, 4):
        dn2 = dn2 + rsb[j].astype(F32)
    hat2, rstd2 = norm_stats(ring[at.h])
    dpool_own = dpool[own_rows]
    dr1 = dpool_own + norm_back(dn2, hat2, rstd2, g2[...])
    g_vec[2:3] = rows_sum(dr1)
    g_vec[3:4] = rows_sum(dn2 * hat2)
    g_vec[4:5] = rows_sum(dn2)
    g_vec[5:6] = rows_sum(dpool_own)
    g_vec[6:8] = jnp.zeros((2, width), F32)

    da = dr1.astype(BF)
    a_in[at.h, 1] = da
    ws = []
    for j in range(4):
        d_out = dot(da, w2[j, 3]).astype(BF)
        s_out[j, 2] = d_out
        ws.append(dot_nt(stack(d_out), w2[j, 2]).astype(BF))
    w_all = jnp.concatenate(ws, 0)
    d_probs = dot_nt(w_all, normed)
    d_scores = probs * (d_probs - jnp.sum(probs * d_probs, -1, keepdims=True))
    scores_low = d_scores.astype(BF)
    g_rows = (dot(scores_low, normed) * scale).astype(BF)
    d_pooled_low = jnp.zeros((own_caps, width), F32)
    for j in range(4):
        part = g_rows[j * per : (j + 1) * per]
        f_out[j, 1] = part
        d_query = pick_heads(dot(part, w2[j, 1])).astype(BF)
        s_out[j, 1] = d_query
        d_pooled_low = d_pooled_low + dot_nt(d_query, w2[j, 0])
    facts = []
    for i, j in enumerate(head_peers):
        facts.append(remote(f_out.at[j], f_in.at[at.h], send.at[9 + i], recv.at[9 + i], at.head(j)))
        facts.append(
            remote(s_out.at[j], s_in.at[at.h], send.at[12 + i], recv.at[12 + i], at.head(j))
        )
        facts.append(
            remote(a_in.at[at.h], a_in.at[at.h], send.at[15 + i], recv.at[15 + i], at.head(j))
        )
    for copy in facts:
        copy.start()
    dn = dot_tn(scores_low, u_all) * scale + dot_tn(probs_low, w_all)
    spread = jnp.broadcast_to(
        jnp.stack([d_pooled_low, dr1], 0)[:, :, None, :], (2, own_caps, slots, width)
    ).reshape(2, block, width)
    dn = dn + pcol[...] * spread[0]
    dz[...] = norm_back(dn, hat1, rstd1, g1[...]) + pcol[...] * spread[1]
    g_vec[0:1] = rows_sum(dn * hat1)
    g_vec[1:2] = rows_sum(dn)

    f_in[at.h] = f_out[at.h]
    s_in[at.h] = s_out[at.h]
    for copy in facts:
        copy.wait_recv()
    pooled_all = jnp.concatenate([a_in[j, 0] for j in range(4)], 0)
    da_all = jnp.concatenate([a_in[j, 1] for j in range(4)], 0)
    dq_all = jnp.concatenate([s_in[j, 1] for j in range(4)], 0)
    do_all = jnp.concatenate([s_in[j, 2] for j in range(4)], 0)
    out_all = jnp.concatenate([s_in[j, 3] for j in range(4)], 0)
    g_qkv[0] = dot_tn(pooled_all, dq_all).astype(BF)
    g_qkv[1] = dot_tn(
        jnp.concatenate([f_in[j, 1] for j in range(4)], 0),
        jnp.concatenate([stack(s_in[j, 0]) for j in range(4)], 0),
    ).astype(BF)
    g_qkv[2] = dot_tn(
        jnp.concatenate([f_in[j, 0] for j in range(4)], 0),
        jnp.concatenate([stack(s_in[j, 2]) for j in range(4)], 0),
    ).astype(BF)
    g_wo[...] = dot_tn(out_all, da_all).astype(BF)
    g_bqv[0:1] = rows_sum(dq_all.astype(F32))
    g_bqv[1:2] = rows_sum(do_all.astype(F32))
    for copy in rings + sums + tells + backs + facts:
        copy.wait_send()


def second_layer(dp, section, slots, z, kbias, pick, pcol, images, w2, b2, top):
    g1, c1, bo, g2, c2, wu, bu, wd, bd = top
    block, width = z.shape
    own_caps = block // slots
    caps = 4 * own_caps
    local = w2.shape[3]
    ff = wu.shape[1]
    heads = local // HEAD_DIM
    per = heads * own_caps
    everyone = dp * section * caps
    vmem = pl.BlockSpec(memory_space=pltpu.VMEM)
    shape = jax.ShapeDtypeStruct
    outs = [
        shape((block, width), F32),
        shape((1, 1), F32),
        shape((3, width, local), BF),
        shape((local, width), BF),
        shape((width, ff), BF),
        shape((ff, width), BF),
        shape((8, width), F32),
        shape((2, local), F32),
        shape((1, ff), F32),
    ]
    sems = pltpu.SemaphoreType.DMA
    others = dp * section - 1
    return pl.pallas_call(
        functools.partial(second_kernel, dp, section, slots),
        out_shape=outs,
        in_specs=[vmem] * 16,
        out_specs=[vmem] * len(outs),
        scratch_shapes=[
            pltpu.VMEM((4, own_caps, width), F32),
            pltpu.VMEM((4, caps, width), BF),
            pltpu.VMEM((dp * section, 8, everyone), F32),
            pltpu.VMEM((caps, width), F32),
            pltpu.VMEM((caps, width), BF),
            pltpu.VMEM((4, own_caps, width), BF),
            pltpu.VMEM((4, 2, per, width), BF),
            pltpu.VMEM((4, 2, per, width), BF),
            pltpu.VMEM((4, 4, own_caps, local), BF),
            pltpu.VMEM((4, 4, own_caps, local), BF),
            pltpu.VMEM((4, 2, own_caps, width), BF),
            sems((18,)),
            sems((18,)),
            sems((others,)),
            sems((others,)),
        ],
        compiler_params=pltpu.CompilerParams(
            collective_id=1, has_side_effects=True, vmem_limit_bytes=VMEM_LIMIT
        ),
        cost_estimate=pl.CostEstimate(
            flops=2 * 10**9, bytes_accessed=20 * 10**6, transcendentals=10**6
        ),
    )(z, kbias, pick, pcol, images, w2, b2, g1, c1, bo, g2, c2, wu, bu, wd, bd)


def first_backward_kernel(
    block,
    dz,
    x,
    n1,
    q,
    k,
    v,
    p,
    o,
    n2,
    hid,
    slope,
    r1,
    g1,
    wqkv,
    wo,
    g2,
    wu,
    wd,
    dy,
    g_qkv,
    g_wo,
    g_wu,
    g_wd,
    g_vec,
    g_bqv,
    g_bu,
    dm,
    du,
    da,
    dqkv,
    dr1,
    part_a,
    got_a,
    part_b,
    got_b,
    ga_send,
    ga_recv,
    sa_send,
    sa_recv,
    gb_send,
    gb_recv,
    sb_send,
    sb_recv,
    gc_send,
    gc_recv,
):
    at = Place()
    at.greet([at.head(j) for j in (at.hx, at.hy, at.hd)])
    local = wo.shape[0]
    heads = local // HEAD_DIM
    width = x.shape[1]
    sub = 128
    own = pl.ds(pl.multiple_of(at.h * block, block), block)
    dm[own] = dz[...].astype(BF)
    gather = Gather(at, dm, ga_send, ga_recv, block)
    gather.start()
    scatter = Scatter(at, part_a, got_a, sa_send, sa_recv, block)

    def waits(t, gather):
        @pl.when(t == 1)
        def _():
            gather.forward()
            gather.wait_x()

        pl.when(t == 2)(gather.wait_y)
        pl.when(t == 3)(gather.wait_d)

    def sends(t, scatter):
        pl.when(t == 1)(scatter.send_x)
        pl.when(t == 2)(scatter.send_y)
        pl.when(t == 3)(scatter.send_d)

    def block_of(t):
        return lax.rem(at.hi + lax.div(t, 2), 2) * 2 + lax.rem(at.lo + lax.rem(t, 2), 2)

    def feed(t, carry):
        waits(t, gather)
        blk = block_of(t)
        rows = pl.ds(pl.multiple_of(blk * block, block), block)
        grad = (dot_nt(dm[rows], wd[...]) * slope[rows].astype(F32)).astype(BF)
        du[rows] = grad
        part_a[blk] = dot_nt(grad, wu[...]).astype(BF)
        sends(t, scatter)
        return carry

    lax.fori_loop(0, 4, feed, 0)
    g_wd[...] = dot_tn(hid[...], dm[...]).astype(BF)
    scatter.second()
    g_wu[...] = dot_tn(n2[...], du[...]).astype(BF)
    g_bu[...] = rows_sum(du[...].astype(F32))
    scatter.wait()
    dn2 = scatter.total()
    hat, rstd = norm_stats(r1[...])
    upper = dz[...]
    back = upper + norm_back(dn2, hat, rstd, g2[...])
    dr1[...] = back
    da[own] = back.astype(BF)
    gather_a = Gather(at, da, gb_send, gb_recv, block)
    gather_a.start()
    g_vec[2:3] = rows_sum(back)
    g_vec[3:4] = rows_sum(dn2 * hat)
    g_vec[4:5] = rows_sum(dn2)
    g_vec[5:6] = rows_sum(upper)
    g_vec[6:8] = jnp.zeros((2, width), F32)

    scatter_b = Scatter(at, part_b, got_b, sb_send, sb_recv, block)
    low_masks = head_masks(local, BF)
    masks = head_masks(local, F32)
    scale = HEAD_DIM ** (-0.5)

    def attend(t, carry):
        waits(t, gather_a)
        blk = block_of(t)
        rows = pl.ds(pl.multiple_of(blk * block, block), block)
        d_out = dot_nt(da[rows], wo[...]).astype(BF)
        query, keys, values = q[rows], k[rows], v[rows]
        parts = [[], [], []]
        for m in range(block // sub):
            cut = slice(m * sub, (m + 1) * sub)
            index = blk * (block // sub) + m
            dq = jnp.zeros((sub, local), F32)
            dk = jnp.zeros((sub, local), F32)
            dv = jnp.zeros((sub, local), F32)
            for i in range(heads):
                probs_low = p[index, i]
                probs = probs_low.astype(F32)
                d_probs = dot_nt(d_out[cut] * low_masks[i], values[cut])
                d_scores = probs * (d_probs - jnp.sum(probs * d_probs, -1, keepdims=True))
                d_scores = d_scores.astype(BF)
                dq = dq + dot(d_scores, keys[cut]) * masks[i]
                dk = dk + dot_tn(d_scores, query[cut]) * masks[i]
                dv = dv + dot_tn(probs_low, d_out[cut]) * masks[i]
            parts[0].append((dq * scale).astype(BF))
            parts[1].append((dk * scale).astype(BF))
            parts[2].append(dv.astype(BF))
        total = None
        for i in range(3):
            whole = jnp.concatenate(parts[i], 0)
            dqkv[i, rows] = whole
            term = dot_nt(whole, wqkv[i])
            total = term if total is None else total + term
        part_b[blk] = total.astype(BF)
        sends(t, scatter_b)
        return carry

    lax.fori_loop(0, 4, attend, 0)
    g_wo[...] = dot_tn(o[...], da[...]).astype(BF)
    g_qkv[0] = dot_tn(n1[...], dqkv[0]).astype(BF)
    scatter_b.second()
    g_qkv[1] = dot_tn(n1[...], dqkv[1]).astype(BF)
    g_qkv[2] = dot_tn(n1[...], dqkv[2]).astype(BF)
    g_bqv[0:1] = rows_sum(dqkv[0].astype(F32))
    g_bqv[1:2] = rows_sum(dqkv[2].astype(F32))
    scatter_b.wait()
    dn1 = scatter_b.total()
    hat, rstd = norm_stats(x[own].astype(F32))
    dy[own] = (dr1[...] + norm_back(dn1, hat, rstd, g1[...])).astype(BF)
    gather_y = Gather(at, dy, gc_send, gc_recv, block)
    gather_y.start()
    g_vec[0:1] = rows_sum(dn1 * hat)
    g_vec[1:2] = rows_sum(dn1)
    gather_y.forward()
    gather_y.wait_x()
    gather_y.wait_y()
    gather_y.wait_d()
    for group in (gather, scatter, gather_a, scatter_b, gather_y):
        group.finish()


def first_backward(dz, x, saved, weights):
    tokens, width = x.shape
    block = tokens // 4
    g1, wqkv, wo, g2, wu, wd = weights
    local = wo.shape[0]
    ff = wu.shape[1]
    vmem = pl.BlockSpec(memory_space=pltpu.VMEM)
    shape = jax.ShapeDtypeStruct
    outs = [
        shape((tokens, width), BF),
        shape((3, width, local), BF),
        shape((local, width), BF),
        shape((width, ff), BF),
        shape((ff, width), BF),
        shape((8, width), F32),
        shape((2, local), F32),
        shape((1, ff), F32),
    ]
    sems = pltpu.SemaphoreType.DMA
    return pl.pallas_call(
        functools.partial(first_backward_kernel, block),
        out_shape=outs,
        in_specs=[vmem] * 18,
        out_specs=[vmem] * len(outs),
        scratch_shapes=[
            pltpu.VMEM((tokens, width), BF),
            pltpu.VMEM((tokens, ff), BF),
            pltpu.VMEM((tokens, width), BF),
            pltpu.VMEM((3, tokens, local), BF),
            pltpu.VMEM((block, width), F32),
            pltpu.VMEM((4, block, width), BF),
            pltpu.VMEM((6, block // 2, width), BF),
            pltpu.VMEM((4, block, width), BF),
            pltpu.VMEM((6, block // 2, width), BF),
        ]
        + [sems((6,))] * 10,
        compiler_params=pltpu.CompilerParams(
            collective_id=2, has_side_effects=True, vmem_limit_bytes=VMEM_LIMIT
        ),
        cost_estimate=pl.CostEstimate(
            flops=8 * 10**9, bytes_accessed=30 * 10**6, transcendentals=10**6
        ),
    )(dz, x, *saved, g1, wqkv, wo, g2, wu, wd)


def on_device(dp, section, text_in, lengths, image_embed, *params):
    base, top = params[:12], params[12:]
    captions, slots, width = text_in.shape
    tokens = captions * slots
    block = tokens // 4
    own_caps = captions // 4

    def line(vector):
        return vector.reshape(1, -1)

    def layout(layer):
        g1, c1, wqkv, bqv, wo, bo, g2, c2, wu, bu, wd, bd = layer
        return (
            line(g1),
            line(c1),
            wqkv.transpose(1, 0, 2),
            bqv,
            wo,
            line(bo),
            line(g2),
            line(c2),
            wu,
            line(bu),
            wd,
            line(bd),
        )

    base, top = layout(base), layout(top)
    x = text_in.reshape(tokens, width)
    positions = jnp.arange(slots, dtype=jnp.int32)
    kbias = jnp.where(positions[None, :] < lengths[:, None], 0.0, NEG).astype(F32)
    head = lax.axis_index("head")
    own_lengths = lax.dynamic_slice_in_dim(lengths, head * own_caps, own_caps)
    kbias_own = lax.dynamic_slice_in_dim(kbias, head * own_caps, own_caps).reshape(1, block)
    picker = positions[None, :] == own_lengths[:, None] - 1
    pick = (
        jnp.where(jnp.eye(own_caps, dtype=bool)[:, :, None], picker[None], False)
        .reshape(own_caps, block)
        .astype(BF)
    )
    pcol = picker.reshape(block, 1).astype(F32)

    w2 = jnp.concatenate([top[2], top[4].T[None]], 0)
    outs = first_forward(
        dp,
        section,
        x,
        kbias.reshape(tokens // 128, 1, 128),
        image_embed,
        base[:3] + (base[3].reshape(2, 1, -1),) + base[4:],
        w2,
        top[3],
    )
    n1, q, k, v, p, o, n2, hid, slope, r1, z, w2all, b2all, images = outs
    seconds = second_layer(
        dp,
        section,
        slots,
        z,
        kbias_own,
        pick,
        pcol,
        images,
        w2all,
        b2all,
        (top[0], top[1], top[5], top[6], top[7], top[8], top[9], top[10], top[11]),
    )
    dz, loss = seconds[0], seconds[1]
    firsts = first_backward(
        dz,
        x,
        (n1, q, k, v, p, o, n2, hid, slope, r1),
        (base[0], base[2], base[4], base[6], base[8], base[10]),
    )
    dy = firsts[0]
    axes = ("dp", "section")
    top_big = lax.psum(tuple(seconds[2:6]), axes)
    base_big = lax.psum(tuple(firsts[1:5]), axes)
    vec = lax.psum(jnp.stack([firsts[5], seconds[6]], 0), axes + ("head",))
    small = lax.psum((firsts[6], firsts[7], seconds[7], seconds[8]), axes)

    def grads(big, vec, bqv, bu):
        g_qkv, g_wo, g_wu, g_wd = (item.astype(F32) for item in big)
        return (
            vec[0],
            vec[1],
            g_qkv.transpose(1, 0, 2),
            bqv,
            g_wo,
            vec[2],
            vec[3],
            vec[4],
            g_wu,
            bu.reshape(-1),
            g_wd,
            vec[5],
        )

    return (
        (loss[0, 0], dy.astype(F32).reshape(captions, slots, width))
        + grads(base_big, vec[0], small[0], small[1])
        + grads(top_big, vec[1], small[2], small[3])
    )


def solution(mesh):
    layer_in = (
        P(),
        P(),
        P(None, None, "head"),
        P(None, "head"),
        P("head", None),
        P(),
        P(),
        P(),
        P(None, "head"),
        P("head"),
        P("head", None),
        P(),
    )
    rows = P(("dp", "section"), None, None)
    return jax.shard_map(
        functools.partial(on_device, mesh.shape["dp"], mesh.shape["section"]),
        mesh=mesh,
        in_specs=(rows, P(("dp", "section")), P(("dp", "section"), None)) + layer_in * 2,
        out_specs=(P(), rows) + layer_in * 2,
        check_vma=False,
    )
```

time: 994 us -> 421 us (0.42)
  waiting for transfers between devices: 670 us -> 94.9 us
  Pallas kernels: 0 us -> 198 us
  matrix products: 80.9 us -> 0 us
  other arithmetic: 72 us -> 13.6 us
  local copies, waits for them, and re-layouts: 78.5 us -> 31.5 us
    psum x9 -> x1, waiting for transfers between devices: 637 us -> 94.9 us  [on_device(): base_big = lax.psum(tuple(firsts[1:5]), axes)]
    pallas_call x0 -> x3, Pallas kernels: none -> 198 us  [the longest x1 78.8 us: first_backward(): pl.pallas_call(functools.partial(first_backward_kernel, block), out_shape...]
    dot_general x37 -> x0, matrix products: 77 us -> none  [the longest x1 6.48 us: base_backward(): jnp.einsum('clf,cld->fd', hidden, branch_grad, preferred_element_type=flo...]
    reduce_sum x27 -> x0, other arithmetic: 42.7 us -> none  [the longest x7 19.5 us: layer_norm(): return shifted * lax.rsqrt(spread + norm_eps) * gain_vec + bias_vec]
    psum x1 -> x2, blocking collectives: 31 us -> 66.2 us  [the longest x1 38.8 us: on_device(): vec = lax.psum(jnp.stack([firsts[5], seconds[6]], 0), axes + ('head',))]
    reduce_scatter x1 -> x0, waiting for transfers between devices: 32.9 us -> none  [on_device(): lax.psum_scatter(column_term, ('dp', 'section'), scatter_dimension=0, til...]
    all_gather x2 -> x0, blocking collectives: 32.8 us -> none  [the longest x1 17.2 us: on_device(): lax.all_gather(image_low, ('dp', 'section'), axis=0, tiled=True)]
    unnamed x249 -> x37, local copies, waits for them, and re-layouts: 29.3 us -> 8.91 us
  transfers between devices with their start and end apart: 10 -> 1, of which waited for: 10 -> 1; matrix products, arithmetic and copies ran while one was open for 4% -> 1% of each run, Pallas kernels for 0% -> 0%
where the time goes in v1:
time: 421 us; the launch traced here: 420 us
  Pallas kernels  198 us (47%)
  waiting for transfers between devices  94.9 us (23%)
  blocking collectives  66.2 us (16%)
  local copies, waits for them, and re-layouts  31.5 us (7%)
  between operations  16 us (4%)
  other arithmetic  13.6 us (3%)
    psum x1, waiting for transfers between devices, on_device(): base_big = lax.psum(tuple(firsts[1:5]), axes)  94.9 us
    pallas_call x1, Pallas kernels, first_backward(): pl.pallas_call(functools.partial(first_backward_kernel, block), out_shape...  78.8 us
    pallas_call x1, Pallas kernels, first_forward(): pl.pallas_call(functools.partial(first_forward_kernel, dp, block, slots),...  71.7 us
    pallas_call x1, Pallas kernels, second_layer(): pl.pallas_call(functools.partial(second_kernel, dp, section, slots), out_...  47.2 us
    psum x1, blocking collectives, on_device(): vec = lax.psum(jnp.stack([firsts[5], seconds[6]], 0), axes + ('head',))  38.8 us
    psum x1, blocking collectives, on_device(): small = lax.psum((firsts[6], firsts[7], seconds[7], seconds[8]), axes)  27.4 us
    reshape x14, local copies, waits for them, and re-layouts, line(): return vector.reshape(1, -1)  17.7 us
    unnamed x37, local copies, waits for them, and re-layouts  8.91 us
  transfers between devices with their start and end apart: 1, of which 1 were waited for; matrix products, arithmetic and copies ran while one was open for 1% of the time, Pallas kernels for 0%

profile of v1, /device:TPU:0, one launch (start us, length us, event | category | flops | bytes accessed | tf_op | source)
XLA Modules:
  0.0 420.0 jit_solution(9790577037037517927)
XLA Ops:
  7.3 0.8 lt.41
  8.1 0.7 broadcast_add_fusion
  8.9 0.1 broadcast_reduce_fusion
  9.0 1.3 reshape.243.bqv
  10.2 1.3 reshape.241.g1
  11.5 1.3 reshape.245.g2
  12.8 1.3 reshape.242.c1
  14.1 1.3 reshape.244.bo
  15.3 1.3 reshape.246.c2
  16.6 1.3 reshape.247.bu
  17.9 1.3 reshape.248.bd
  19.1 1.3 reshape.250.g1
  20.4 1.3 reshape.251.c1
  21.7 1.3 reshape.252.bo
  22.9 1.3 reshape.253.g2
  24.2 1.3 reshape.254.c2
  25.5 1.3 reshape.255.bu
  26.7 1.3 reshape.256.bd
  28.1 0.7 reshape.249.kbias
  29.1 0.1 broadcast_in_dim.48
  29.2 0.1 broadcast_in_dim.49
  29.4 0.8 reshape.264.pcol
  30.1 1.1 copy.60
  31.3 1.4 copy.58
  32.7 0.6 copy.59
  33.3 0.6 compare_select_fusion.kbias
  33.9 0.6 select_convert_fusion.pick
  34.5 1.4 pad_maximum_fusion.w2
  35.9 71.7 %shard_map.458 = (bf16[1024,768]{1,0:T(8,128)(2,1)}, bf16[1024,192]{1,0:T(8,128)(2,1)}, bf16[1024,192]{1,0:T(8,128)(2,1)}, bf16[1024,192]{1,0:T(8,128)(2,1)}, bf...) custom-call(bf16[1024,768]{1,0:T(8,128)(2,1)} %bitcast.22, ...), custom_call_target="tpu_custom_call" | custom-call | flops 4000000000 | bytes 20000000 | tf_op jit(solution)/shard_map/pallas_call | solution.py:450
  107.7 47.2 %shard_map.459 = (f32[256,768]{1,0:T(8,128)}, f32[1,1]{1,0:T(1,128)}, bf16[3,768,192]{2,1,0:T(8,128)(2,1)}, bf16[192,768]{1,0:T(8,128)(2,1)}, bf16[768,768]{1,0:...) custom-call(f32[256,768]{1,0:T(8,128)} %get-tuple-element.57.z, ...), custom_call_target="tpu_custom_call" | custom-call | flops 2000000000 | bytes 20000000 | tf_op jit(solution)/shard_map/pallas_call | solution.py:775
  154.9 78.8 %shard_map.460 = (bf16[1024,768]{1,0:T(8,128)(2,1)}, bf16[3,768,192]{2,1,0:T(8,128)(2,1)}, bf16[192,768]{1,0:T(8,128)(2,1)}, bf16[768,768]{1,0:T(8,128)(2,1)}, b...) custom-call(f32[256,768]{1,0:T(8,128)} %get-tuple-element.62.dz, ...), custom_call_target="tpu_custom_call" | custom-call | flops 8000000000 | bytes 30000000 | tf_op jit(solution)/shard_map/pallas_call | solution.py:996
  233.7 0.6 copy-done.13
  234.4 0.7 copy-done
  235.1 2.1 convert.4
  237.2 27.4 %all-reduce = (f32[2,192]{1,0:T(2,128)}, f32[768]{0:T(1024)}, f32[2,192]{1,0:T(2,128)}, f32[768]{0:T(1024)}) all-reduce(f32[2,192]{1,0:T(2,128)S(1)} %copy-done.15, f32[768]{0:T(1024)S(1)} %reduce.6, f32[2,192]{1,0:T(2,128)S(1)} %copy-done.14, f32[768]{0:T(1024)S(1)} %reduce.13), channel_id=1, replica_groups=mesh['dp'=4,'section'=2,'head'=4] {'dp','section'}, use_global_device_ids=true, to_apply=%region_2.3 | all-reduce | flops 2304 | bytes 18432 | tf_op jit(solution)/shard_map/psum | solution.py:1101
  264.6 38.8 %psum.91 = f32[2,8,768]{2,1,0:T(8,128)S(1)} all-reduce(f32[2,8,768]{2,1,0:T(8,128)S(1)} %pad_maximum_fusion.1), channel_id=1, replica_groups=mesh['dp'=4,'section'=2,'head'=4] {'dp','section','head'}, use_global_device_ids=true, to_apply=%region_0.1 | all-reduce | flops 12288 | bytes 98304 | tf_op jit(solution)/shard_map/psum | solution.py:1100
  303.4 0.7 slice_reduce_fusion
  304.1 94.9 %all-reduce.4.cloned.1.call-done = (bf16[768,3,192]{2,0,1:T(8,128)(2,1)}, bf16[768,3,192]{2,0,1:T(8,128)(2,1)}, bf16[192,768]{1,0:T(8,128)(2,1)}, bf16[768,768]{...) async-done(((bf16[768,3,192]{2,0,1:T(8,128)(2,1)}, ...) | async-done | bytes 7077904 | tf_op jit(solution)/shard_map/psum | solution.py:1099
  399.0 2.6 copy.62
  401.6 0.9 convert_element_type.32
  402.4 0.9 convert_element_type.35
  403.3 1.5 copy.63
  404.8 1.6 convert_element_type.33
  406.5 1.6 convert_element_type.34
  408.0 0.1 copy-done.2
  408.1 1.6 convert_element_type.36
  409.7 0.1 copy-done.1
  409.8 1.6 convert_element_type.37
  (44 shorter events, 0.8 us)
Async XLA Ops:
  7.2 24.0 %copy-start.6 = (bf16[768,3,192]{0,2,1:T(8,128)(2,1)S(1)}, bf16[768,3,192]{0,2,1:T(8,128)(2,1)}, u32[]{:S(2)}) copy-start(bf16[768,3,192]{0,2,1:T(8,128)(2,1)} %param.32) | copy-start | bytes 2654212
  7.2 391.8 %all-reduce.4.cloned.1.call-start = ((), (), s32[]{:S(2)}) async-start(), calls=%async_computation | async-start | bytes 15335424 | tf_op jit(solution)/shard_map/psum | solution.py:1099
  31.3 1.4 copy-start.7
  233.7 0.7 copy-start.13
  233.7 0.7 copy-start.12
  233.7 1.4 copy-start
  235.1 2.1 copy-start.14
  235.1 2.1 copy-start.15
  235.1 29.5 %copy-start.10 = (f32[8,768]{1,0:T(8,128)S(1)}, f32[8,768]{1,0:T(8,128)}, u32[]{:S(2)}) copy-start(f32[8,768]{1,0:T(8,128)} %get-tuple-element.75) | copy-start | bytes 73732
  235.1 29.5 %copy-start.11 = (f32[8,768]{1,0:T(8,128)S(1)}, f32[8,768]{1,0:T(8,128)}, u32[]{:S(2)}) copy-start(f32[8,768]{1,0:T(8,128)} %get-tuple-element.74) | copy-start | bytes 73732
  399.0 2.6 copy-start.9
  399.0 3.4 copy-start.8
  401.5 1.7 copy-start.5
  403.3 1.5 copy-start.4
  404.8 1.7 copy-start.3
  406.5 1.7 copy-start.2
  408.1 1.7 copy-start.1
Sparse Core Ops, SparseCore 0:
  233.9 165.0 all-reduce.3

commit v2 on v1

v2 whole, which is shorter than its diff:
```python
import functools

import jax
import jax.numpy as jnp
from jax import lax
from jax.experimental import pallas as pl
from jax.experimental.pallas import tpu as pltpu
from jax.sharding import PartitionSpec as P

HEAD_DIM = 64
NORM_EPS = 1e-06
LOGIT_SCALE = 50.0
NEG = -1e30
BF = jnp.bfloat16
F32 = jnp.float32
MESH = pl.DeviceIdType.MESH
VMEM_LIMIT = 63 * 2**20


def dot(a, b):
    return lax.dot_general(a, b, (((1,), (0,)), ((), ())), preferred_element_type=F32)


def dot_nt(a, b):
    return lax.dot_general(a, b, (((1,), (1,)), ((), ())), preferred_element_type=F32)


def dot_tn(a, b):
    return lax.dot_general(a, b, (((0,), (0,)), ((), ())), preferred_element_type=F32)


def norm_stats(values):
    center = jnp.mean(values, -1, keepdims=True)
    shifted = values - center
    spread = jnp.mean(shifted * shifted, -1, keepdims=True)
    rstd = lax.rsqrt(spread + NORM_EPS)
    return shifted * rstd, rstd


def norm_back(grad, hat, rstd, gain):
    scaled = grad * gain
    m1 = jnp.mean(scaled, -1, keepdims=True)
    m2 = jnp.mean(scaled * hat, -1, keepdims=True)
    return rstd * (scaled - m1 - hat * m2)


def rows_sum(values):
    return jnp.sum(values, 0, keepdims=True)


def gelu_pair(u):
    c = 0.7978845608028654
    u2 = u * u
    t = jnp.tanh(c * u * (1.0 + 0.044715 * u2))
    half = 0.5 * (1.0 + t)
    value = u * half
    slope = half + 0.5 * u * (1.0 - t * t) * (c * (1.0 + 3.0 * 0.044715 * u2))
    return value, slope


def head_masks(width, kind):
    lane = lax.broadcasted_iota(jnp.int32, (1, width), 1)
    return [
        jnp.where((lane >= i * HEAD_DIM) & (lane < (i + 1) * HEAD_DIM), 1.0, 0.0).astype(kind)
        for i in range(width // HEAD_DIM)
    ]


class Place:
    def __init__(self):
        self.z = lax.axis_index("dp")
        self.s = lax.axis_index("section")
        h = lax.axis_index("head")
        self.h = h
        self.hi = lax.div(h, 2)
        self.lo = lax.rem(h, 2)
        self.hx = self.block(0, 1)
        self.hy = self.block(1, 0)
        self.hd = self.block(1, 1)

    def block(self, flip_hi, flip_lo):
        return lax.rem(self.hi + flip_hi, 2) * 2 + lax.rem(self.lo + flip_lo, 2)

    def head(self, other):
        return (self.z, self.s, other)

    def greet(self, devices):
        barrier = pltpu.get_barrier_semaphore()
        for device in devices:
            pl.semaphore_signal(barrier, inc=1, device_id=device, device_id_type=MESH)
        pl.semaphore_wait(barrier, len(devices))


def remote(src, dst, send_sem, recv_sem, device):
    return pltpu.make_async_remote_copy(
        src_ref=src,
        dst_ref=dst,
        send_sem=send_sem,
        recv_sem=recv_sem,
        device_id=device,
        device_id_type=MESH,
    )


class Gather:
    def __init__(self, at, ref, send, recv, block):
        half = block // 2

        def rows(owner, part):
            return ref.at[pl.ds(pl.multiple_of(owner * block + part * half, half), half)]

        def copy(i, owner, part, target):
            piece = rows(owner, part)
            return remote(piece, piece, send.at[i], recv.at[i], at.head(target))

        self.c = [
            copy(0, at.h, 0, at.hx),
            copy(1, at.h, 1, at.hy),
            copy(2, at.h, 1, at.hx),
            copy(3, at.h, 0, at.hy),
            copy(4, at.hx, 0, at.hy),
            copy(5, at.hy, 1, at.hx),
        ]

    def start(self):
        for i in range(4):
            self.c[i].start()

    def forward(self):
        self.c[0].wait_recv()
        self.c[4].start()
        self.c[1].wait_recv()
        self.c[5].start()

    def wait_x(self):
        self.c[2].wait_recv()

    def wait_y(self):
        self.c[3].wait_recv()

    def wait_d(self):
        self.c[4].wait_recv()
        self.c[5].wait_recv()

    def finish(self):
        for copy in self.c:
            copy.wait_send()


class Scatter:
    def __init__(self, at, part, got, send, recv, block):
        half = block // 2
        self.at, self.part, self.got, self.half = at, part, got, half

        def piece(owner, side):
            return part.at[owner, pl.ds(side * half, half)]

        def copy(i, owner, side, target):
            return remote(piece(owner, side), got.at[i], send.at[i], recv.at[i], at.head(target))

        self.c = [
            copy(0, at.hd, 0, at.hx),
            copy(1, at.hd, 1, at.hy),
            copy(2, at.hx, 0, at.hx),
            copy(3, at.hy, 1, at.hy),
            copy(4, at.hy, 0, at.hy),
            copy(5, at.hx, 1, at.hx),
        ]

    def send_d(self):
        self.c[0].start()
        self.c[1].start()

    def send_x(self):
        self.c[2].start()

    def send_y(self):
        self.c[3].start()

    def second(self):
        half, part, got, at = self.half, self.part, self.got, self.at
        self.c[0].wait_recv()
        part[at.hy, :half] = (part[at.hy, :half].astype(F32) + got[0].astype(F32)).astype(BF)
        self.c[4].start()
        self.c[1].wait_recv()
        part[at.hx, half:] = (part[at.hx, half:].astype(F32) + got[1].astype(F32)).astype(BF)
        self.c[5].start()

    def wait(self):
        for i in (2, 3, 4, 5):
            self.c[i].wait_recv()

    def total(self):
        half, part, got, at = self.half, self.part, self.got, self.at
        top = part[at.h, :half].astype(F32) + got[2].astype(F32) + got[4].astype(F32)
        low = part[at.h, half:].astype(F32) + got[3].astype(F32) + got[5].astype(F32)
        return jnp.concatenate([top, low], 0)

    def finish(self):
        for copy in self.c:
            copy.wait_send()


class Ledger:
    def __init__(self, at, dp, refs, sems):
        self.at = at
        self.pieces = refs
        self.cs, self.cr, self.ns, self.ar, self.br, self.os, self.fs, self.fr, self.free = sems
        left = at.z < dp // 2
        step = jnp.where(left, 1, -1)
        self.inner = (at.z + step, at.s, at.h)
        self.outer = (at.z - step, at.s, at.h)
        self.core = (at.z, 1 - at.s, at.h)
        self.mid = (at.z == dp // 2 - 1) | (at.z == dp // 2)
        self.outermost = (at.z == 0) | (at.z == dp - 1)

    def rows(self, i, side):
        ref, c, a, b = self.pieces[i]
        half = ref.shape[0] // 2
        return ref.at[pl.ds(pl.multiple_of(side * half, half), half)]

    def swap(self, i):
        c = self.pieces[i][1]
        return remote(self.rows(i, 1 - self.at.s), c, self.cs.at[i], self.cr.at[i], self.core)

    def inward(self, i):
        return remote(
            self.rows(i, self.at.s), self.pieces[i][2], self.ns.at[i], self.ar.at[i], self.inner
        )

    def across(self, i):
        return remote(
            self.rows(i, self.at.s), self.pieces[i][3], self.ns.at[i], self.br.at[i], self.inner
        )

    def outward(self, i):
        return remote(
            self.rows(i, self.at.s), self.pieces[i][3], self.os.at[i], self.br.at[i], self.outer
        )

    def last(self, i):
        mine = self.rows(i, self.at.s)
        return remote(mine, mine, self.fs.at[i], self.fr.at[i], self.core)

    def release(self, i):
        self.swap(i).wait_send()
        pl.semaphore_signal(
            self.free.at[i], inc=1, device_id=self.core, device_id_type=MESH
        )

    def finish(self, i):
        pl.semaphore_wait(self.free.at[i], 1)
        self.last(i).start()

    def add(self, i, *refs):
        mine = self.rows(i, self.at.s)
        total = mine[...].astype(F32)
        for ref in refs:
            total = total + ref[...].astype(F32)
        mine[...] = total.astype(mine.dtype)

    def open(self, *which):
        for i in which:
            self.swap(i).start()

    def step(self, ends=(), middles=(), turns=(), backs=()):
        for i in ends:

            @pl.when(self.outermost)
            def _():
                self.swap(i).wait_recv()
                self.add(i, self.pieces[i][1])
                self.release(i)
                pl.when(self.mid)(lambda: self.across(i).start())
                pl.when(jnp.logical_not(self.mid))(lambda: self.inward(i).start())

        for i in middles:

            @pl.when(jnp.logical_not(self.outermost))
            def _():
                self.swap(i).wait_recv()
                self.inward(i).wait_recv()
                self.add(i, self.pieces[i][1], self.pieces[i][2])
                self.release(i)
                pl.when(self.mid)(lambda: self.across(i).start())
                pl.when(jnp.logical_not(self.mid))(lambda: self.inward(i).start())

        for i in turns:

            @pl.when(self.mid)
            def _():
                self.across(i).wait_recv()
                self.across(i).wait_send()
                self.add(i, self.pieces[i][3])
                pl.when(jnp.logical_not(self.outermost))(lambda: self.outward(i).start())
                self.finish(i)

        for i in backs:

            @pl.when(jnp.logical_not(self.mid))
            def _():
                self.outward(i).wait_recv()
                self.inward(i).wait_send()
                mine = self.rows(i, self.at.s)
                mine[...] = self.pieces[i][3][...]
                pl.when(jnp.logical_not(self.outermost))(lambda: self.outward(i).start())
                self.finish(i)

    def close(self):
        for i in range(len(self.pieces)):
            self.last(i).wait_recv()
            self.last(i).wait_send()
            pl.when(jnp.logical_not(self.outermost))(lambda: self.outward(i).wait_send())


def kernel(dp, section, slots, *refs):
    refs = list(refs)

    def take(count):
        out = refs[:count]
        del refs[:count]
        return out

    x, lens, image = take(3)
    g1, c1, wqkv, bqv, wo, bo, g2, c2, wu, bu, wd, bd = take(12)
    tg1, tc1, tqkv, tbqv, two, tbo, tg2, tc2, twu, tbu, twd, tbd = take(12)
    dy, grads, vec = take(3)
    n1, q, k, v, p, o, n2, hid, slope, r1, z = take(11)
    w2, b2, images = take(3)
    part, got = take(2)
    ring, arb, stats, scored, dpool, dn2b, rsb = take(7)
    f_out, f_in, s_out, s_in, a_in = take(5)
    (da,) = take(1)
    dm = dy
    c_in, l_in, b_in, vh_in, vc_in, vl_in, vb_in = take(7)
    ag_sems, rs_sems, w_sems, h_sems, i_sems, st_sems, sm_sems, v_sems = (
        take(2) for _ in range(8)
    )
    ledger_sems = take(9)
    assert not refs

    at = Place()
    tokens, width = x.shape
    block = tokens // 4
    local = wo.shape[0]
    heads = local // HEAD_DIM
    sub = 128
    captions = tokens // slots
    own_caps = block // slots
    caps = captions
    scale = HEAD_DIM ** (-0.5)
    low_masks = head_masks(local, BF)
    masks = head_masks(local, F32)
    other_core = (at.z, 1 - at.s, at.h)
    zs = [(lax.rem(at.z + j, dp), at.s, at.h) for j in range(1, dp)]
    z_pair = (at.z + 1 - 2 * lax.rem(at.z, 2), at.s, at.h)
    head_peers = [at.hx, at.hy, at.hd]
    others = []
    for j in range(dp):
        for i in range(section):
            if i or j:
                others.append((lax.rem(at.z + j, dp), lax.rem(at.s + i, section), at.h))
    own = pl.ds(pl.multiple_of(at.h * block, block), block)

    def vector(ref):
        return ref[...].reshape(1, -1)

    pic = image[...].astype(F32)
    pic = pic * lax.rsqrt(jnp.mean(pic * pic, -1, keepdims=True) + NORM_EPS) * width ** (-0.5)
    images[at.z, at.s] = pic.astype(BF)
    w2[at.h, 0:3] = tqkv[...]
    w2[at.h, 3] = two[...]
    b2[at.h] = tbqv[...]

    at.greet([at.head(j) for j in head_peers] + others)

    quarter = local // 4
    mine = lax.rem(at.z, 2) * 2 + at.s
    pair = (1 - lax.rem(at.z, 2)) * 2 + at.s

    def shard_part(owner, which):
        return w2.at[owner, :, pl.ds(pl.multiple_of(which * quarter, quarter), quarter)]

    def same_place(ref, sems, i, device):
        return remote(ref, ref, sems[0].at[i], sems[1].at[i], device)

    hop1 = [
        same_place(shard_part(at.h, mine), w_sems, i, at.head(j)) for i, j in enumerate(head_peers)
    ]
    hop_b = [same_place(b2.at[at.h], h_sems, i, at.head(j)) for i, j in enumerate(head_peers)]
    hop2 = [
        same_place(shard_part(j, mine), w_sems, 3 + i, z_pair) for i, j in enumerate(head_peers)
    ]
    hop3 = [
        same_place(shard_part(j, which), w_sems, 6 + 3 * n + i, other_core)
        for i, j in enumerate(head_peers)
        for n, which in enumerate((mine, pair))
    ]
    pics = [
        same_place(images.at[at.z, at.s], i_sems, i, device) for i, device in enumerate(zs)
    ]
    core_pics = same_place(images.at[:, at.s], i_sems, dp - 1, other_core)
    for copy in hop1 + hop_b + pics:
        copy.start()

    scatters = [
        Scatter(at, part, got, rs_sems[0].at[i], rs_sems[1].at[i], block) for i in range(4)
    ]
    gathers = [
        Gather(at, ref, ag_sems[0].at[i], ag_sems[1].at[i], block)
        for i, ref in enumerate((n2, dm, da, dy))
    ]

    def block_of(t):
        return lax.rem(at.hi + lax.div(t, 2), 2) * 2 + lax.rem(at.lo + lax.rem(t, 2), 2)

    def limits(first, count):
        cap = lax.broadcasted_iota(jnp.int32, (captions, count), 0)
        slot = lax.broadcasted_iota(jnp.int32, (captions, count), 1)
        chosen = jnp.where(cap == first + slot // slots, 1.0, 0.0).astype(BF)
        row = jnp.broadcast_to(vector(lens).astype(F32), (8, captions)).astype(BF)
        return dot(row, chosen)[:1]

    def key_bias(first, count):
        slot = lax.broadcasted_iota(jnp.int32, (1, count), 1)
        inside = lax.rem(slot, slots).astype(F32) < limits(first, count)
        return jnp.where(inside, 0.0, NEG)

    row_id = lax.broadcasted_iota(jnp.int32, (sub, sub), 0) // slots
    col_id = lax.broadcasted_iota(jnp.int32, (sub, sub), 1) // slots
    same = row_id == col_id
    scatter = scatters[0]

    def attend(t, carry):
        blk = block_of(3 - t)
        rows = pl.ds(pl.multiple_of(blk * block, block), block)
        hat, _ = norm_stats(x[rows].astype(F32))
        normed = (hat * vector(g1) + vector(c1)).astype(BF)
        n1[rows] = normed
        query = (dot_nt(normed, wqkv[0]) + bqv[0:1]).astype(BF)
        keys = dot_nt(normed, wqkv[1]).astype(BF)
        values = (dot_nt(normed, wqkv[2]) + bqv[1:2]).astype(BF)
        q[rows] = query
        k[rows] = keys
        v[rows] = values
        mixed = []
        for m in range(block // sub):
            cut = slice(m * sub, (m + 1) * sub)
            index = blk * (block // sub) + m
            bias = jnp.where(same, key_bias(index * (sub // slots), sub), NEG)
            total = jnp.zeros((sub, local), F32)
            for i in range(heads):
                scores = dot_nt(query[cut] * low_masks[i], keys[cut]) * scale + bias
                scores = jnp.exp(scores - jnp.max(scores, -1, keepdims=True))
                probs = (scores * (1.0 / jnp.sum(scores, -1, keepdims=True))).astype(BF)
                p[index, i] = probs
                total = total + dot(probs, values[cut]) * masks[i]
            mixed.append(total.astype(BF))
        mixed = jnp.concatenate(mixed, 0)
        o[rows] = mixed
        part[blk] = dot(mixed, wo[...]).astype(BF)
        pl.when(t == 0)(scatter.send_d)
        pl.when(t == 1)(scatter.send_y)
        pl.when(t == 2)(scatter.send_x)
        return carry

    lax.fori_loop(0, 4, attend, 0)
    scatter.second()
    for i in range(3):
        hop1[i].wait_recv()
        hop2[i].start()
    scatter.wait()
    resid = x[own].astype(F32) + scatter.total() + vector(bo)
    scatter.finish()
    r1[...] = resid
    hat, _ = norm_stats(resid)
    n2[own] = (hat * vector(g2) + vector(c2)).astype(BF)

    def waits(t, gather):
        @pl.when(t == 1)
        def _():
            gather.forward()
            gather.wait_x()

        pl.when(t == 2)(gather.wait_y)
        pl.when(t == 3)(gather.wait_d)

    def sends(t, scatter):
        pl.when(t == 1)(scatter.send_x)
        pl.when(t == 2)(scatter.send_y)
        pl.when(t == 3)(scatter.send_d)

    gathers[0].start()

    def feed(t, carry):
        waits(t, gathers[0])
        blk = block_of(t)
        rows = pl.ds(pl.multiple_of(blk * block, block), block)
        value, steep = gelu_pair(dot(n2[rows], wu[...]) + vector(bu))
        value = value.astype(BF)
        hid[rows] = value
        slope[rows] = steep.astype(BF)
        part[blk] = dot(value, wd[...]).astype(BF)
        sends(t, scatters[1])
        return carry

    lax.fori_loop(0, 4, feed, 0)
    for i in range(3):
        hop2[i].wait_recv()
        hop3[2 * i].start()
        hop3[2 * i + 1].start()
    for copy in pics:
        copy.wait_recv()
    core_pics.start()
    scatters[1].second()
    scatters[1].wait()
    zv = r1[...] + scatters[1].total() + vector(bd)
    scatters[1].finish()
    z[...] = zv
    for copy in hop_b + hop3 + [core_pics]:
        copy.wait_recv()

    per = heads * own_caps

    def stack(values):
        return jnp.concatenate([values * low_masks[i] for i in range(heads)], 0)

    def pick_heads(values):
        total = values[:own_caps] * masks[0]
        for i in range(1, heads):
            total = total + values[i * own_caps : (i + 1) * own_caps] * masks[i]
        return total

    first_cap = at.h * own_caps
    last_slot = limits(first_cap, block) - 1.0
    slot_row = lax.broadcasted_iota(jnp.int32, (own_caps, block), 1)
    cap_row = lax.broadcasted_iota(jnp.int32, (own_caps, block), 0)
    picked = (slot_row // slots == cap_row) & (lax.rem(slot_row, slots).astype(F32) == last_slot)
    pick = jnp.where(picked, 1.0, 0.0).astype(BF)
    cap_of = lax.broadcasted_iota(jnp.int32, (block, captions), 0)
    cap_at = lax.broadcasted_iota(jnp.int32, (block, captions), 1)
    length_col = jnp.sum(
        jnp.where(cap_at == first_cap + cap_of // slots, vector(lens).astype(F32), 0.0),
        1,
        keepdims=True,
    )
    slot_col = lax.rem(lax.broadcasted_iota(jnp.int32, (block, 1), 0), slots).astype(F32)
    pcol = jnp.where(slot_col == length_col - 1.0, 1.0, 0.0)

    hat1, rstd1 = norm_stats(zv)
    normed = (hat1 * vector(tg1) + vector(tc1)).astype(BF)
    pooled_low = dot(pick, normed).astype(BF)
    a_in[at.h, 0] = pooled_low
    z_pool = jnp.sum((zv * pcol).reshape(own_caps, slots, width), 1)
    us = []
    for j in range(4):
        query = (dot_nt(pooled_low, w2[j, 0]) + b2[j, 0:1]).astype(BF)
        s_out[j, 0] = query
        us.append(dot(stack(query), w2[j, 1]).astype(BF))
    u_all = jnp.concatenate(us, 0)
    rows_n = 4 * per
    row_cap = lax.rem(lax.broadcasted_iota(jnp.int32, (rows_n, block), 0), own_caps)
    col_cap = lax.broadcasted_iota(jnp.int32, (rows_n, block), 1) // slots
    bias = jnp.where(row_cap == col_cap, key_bias(first_cap, block), NEG)
    scores = dot_nt(u_all, normed) * scale + bias
    scores = jnp.exp(scores - jnp.max(scores, -1, keepdims=True))
    probs = scores * (1.0 / jnp.sum(scores, -1, keepdims=True))
    probs_low = probs.astype(BF)
    mix = dot(probs_low, normed).astype(BF)
    attended = jnp.zeros((own_caps, width), F32)
    for j in range(4):
        piece = mix[j * per : (j + 1) * per]
        f_out[j, 0] = piece
        out = (pick_heads(dot_nt(piece, w2[j, 2])) + b2[j, 1:2]).astype(BF)
        s_out[j, 3] = out
        attended = attended + dot(out, w2[j, 3])
    ring[at.h] = z_pool + attended + vector(tbo)

    def small(ref, i, j, target=None):
        return remote(
            ref,
            ref if target is None else target,
            sm_sems[0].at[i],
            sm_sems[1].at[i],
            at.head(j),
        )

    rings = [small(ring.at[at.h], i, j) for i, j in enumerate(head_peers)]
    for copy in rings:
        copy.start()
    for copy in rings:
        copy.wait_recv()

    r1_all = ring[...].reshape(caps, width)
    hat2_all, _ = norm_stats(r1_all)
    n2_top = (hat2_all * vector(tg2) + vector(tc2)).astype(BF)
    value, steep = gelu_pair(dot(n2_top, twu[...]) + vector(tbu))
    value = value.astype(BF)
    arb[at.h] = dot(value, twd[...]).astype(BF)
    sums = [small(arb.at[at.h], 3 + i, j) for i, j in enumerate(head_peers)]
    for copy in sums:
        copy.start()
    for copy in sums:
        copy.wait_recv()
    pooled = r1_all + vector(tbd)
    for j in range(4):
        pooled = pooled + arb[j].astype(F32)
    unit_r = lax.rsqrt(jnp.mean(pooled * pooled, -1, keepdims=True) + NORM_EPS)
    text = (pooled * unit_r * width ** (-0.5)).astype(BF)

    everyone = dp * section * caps
    batch = min(dp, 4)
    wide = batch * section * caps
    lanes = wide // 4
    place = at.z * section + at.s

    def chunk_images(n):
        return images[n * batch : (n + 1) * batch].reshape(wide, width)

    def own_columns(n):
        col = lax.broadcasted_iota(jnp.int32, (caps, wide), 1) + n * wide
        row = lax.broadcasted_iota(jnp.int32, (caps, wide), 0) + place * caps
        return col == row

    chunks = [slice(n * wide, (n + 1) * wide) for n in range(dp // batch)]
    row_max = diagonal = None
    for n, cols in enumerate(chunks):
        logits = LOGIT_SCALE * dot_nt(text, chunk_images(n))
        scored[:, cols] = logits
        found = jnp.max(logits, 1, keepdims=True)
        row_max = found if row_max is None else jnp.maximum(row_max, found)
        found = jnp.sum(jnp.where(own_columns(n), logits, 0.0), 1, keepdims=True)
        diagonal = found if diagonal is None else diagonal + found
        col_max = jnp.max(logits, 0, keepdims=True)
        col_sum = jnp.sum(jnp.exp(logits - col_max), 0, keepdims=True)
        for i in range(4):
            stats[place, n, i : i + 1] = col_max[:, i * lanes : (i + 1) * lanes]
            stats[place, n, 4 + i : 5 + i] = col_sum[:, i * lanes : (i + 1) * lanes]
    tells = [
        same_place(stats.at[place], st_sems, i, device) for i, device in enumerate(others)
    ]
    for copy in tells:
        copy.start()
    row_sum = None
    for n, cols in enumerate(chunks):
        found = jnp.sum(jnp.exp(scored[:, cols] - row_max), 1, keepdims=True)
        row_sum = found if row_sum is None else row_sum + found
    row_lse = row_max + jnp.log(row_sum)

    def pull(n, cols, lse):
        steep = jnp.exp(scored[:, cols] - lse) - jnp.where(own_columns(n), 1.0, 0.0)
        return dot((steep * (0.5 / everyone)).astype(BF), chunk_images(n))

    text_grad = None
    for n, cols in enumerate(chunks):
        term = pull(n, cols, row_lse)
        text_grad = term if text_grad is None else text_grad + term
    lost = jnp.sum(row_lse - 2.0 * diagonal, 0, keepdims=True)
    for copy in tells:
        copy.wait_recv()
    for n, cols in enumerate(chunks):
        told = stats[:, n]
        top = jnp.max(told[:, 0:4], 0)
        total = jnp.sum(told[:, 4:8] * jnp.exp(told[:, 0:4] - top[None]), 0)
        lse = top + jnp.log(total)
        col_lse = jnp.concatenate([lse[i : i + 1] for i in range(4)], 1)
        text_grad = text_grad + pull(n, cols, col_lse)
        found = jnp.sum(jnp.where(own_columns(n), col_lse, 0.0), 1, keepdims=True)
        lost = lost + jnp.sum(found, 0, keepdims=True)
    text_grad = LOGIT_SCALE * text_grad
    inner = jnp.mean(pooled * text_grad, -1, keepdims=True)
    d_pool = (unit_r * width ** (-0.5)) * (text_grad - pooled * (unit_r * unit_r * inner))
    dpool[...] = d_pool

    per_array = 2
    span = width // per_array
    pieces = []
    for a in range(6):
        for n in range(per_array):
            i = a * per_array + n
            pieces.append(
                (grads.at[a, pl.ds(n * span, span)], c_in.at[i], l_in.at[i], b_in.at[i])
            )
    pieces.append((vec, vc_in, vl_in, vb_in))
    ledger = Ledger(at, dp, pieces, ledger_sems)

    low = d_pool.astype(BF)
    du_top = (dot_nt(low, twd[...]) * steep).astype(BF)
    dn2b[...] = dot_nt(du_top, twu[...]).astype(BF)
    own_rows = pl.ds(pl.multiple_of(at.h * own_caps, own_caps), own_caps)
    backs = []
    for i, j in enumerate(head_peers):
        there = pl.ds(pl.multiple_of(j * own_caps, own_caps), own_caps)
        backs.append(small(dn2b.at[there], 6 + i, j, rsb.at[at.h]))
    for copy in backs:
        copy.start()
    grads[0] = dot_tn(value, low).astype(BF)
    ledger.open(0, 1)
    grads[1] = dot_tn(n2_top, du_top).astype(BF)
    ledger.open(2, 3)
    vec[...] = jnp.zeros_like(vec)
    vec[22:23, 0:128] = jnp.broadcast_to(lost, (1, 128))
    vec[17:18] = rows_sum(du_top.astype(F32))
    rsb[at.h] = dn2b[own_rows]
    ledger.step(ends=(0,))
    for copy in backs:
        copy.wait_recv()
    dn2 = rsb[0].astype(F32)
    for j in range(1, 4):
        dn2 = dn2 + rsb[j].astype(F32)
    hat2, rstd2 = norm_stats(ring[at.h])
    dpool_own = dpool[own_rows]
    dr1_top = dpool_own + norm_back(dn2, hat2, rstd2, vector(tg2))
    vec[8:9] = rows_sum(dr1_top)
    vec[9:10] = rows_sum(dn2 * hat2)
    vec[10:11] = rows_sum(dn2)
    vec[11:12] = rows_sum(dpool_own)

    da_top = dr1_top.astype(BF)
    a_in[at.h, 1] = da_top
    ws = []
    for j in range(4):
        d_out = dot_nt(da_top, w2[j, 3]).astype(BF)
        s_out[j, 2] = d_out
        ws.append(dot(stack(d_out), w2[j, 2]).astype(BF))
    w_all = jnp.concatenate(ws, 0)
    d_probs = dot_nt(w_all, normed)
    d_scores = probs * (d_probs - jnp.sum(probs * d_probs, -1, keepdims=True))
    scores_low = d_scores.astype(BF)
    g_rows = (dot(scores_low, normed) * scale).astype(BF)
    ledger.step(ends=(1,), middles=(0,))
    d_pooled_low = jnp.zeros((own_caps, width), F32)
    for j in range(4):
        piece = g_rows[j * per : (j + 1) * per]
        f_out[j, 1] = piece
        d_query = pick_heads(dot_nt(piece, w2[j, 1])).astype(BF)
        s_out[j, 1] = d_query
        d_pooled_low = d_pooled_low + dot(d_query, w2[j, 0])
    facts = []
    for i, j in enumerate(head_peers):
        facts.append(small(f_out.at[j], 9 + i, j, f_in.at[at.h]))
        facts.append(small(s_out.at[j], 12 + i, j, s_in.at[at.h]))
        facts.append(small(a_in.at[at.h], 15 + i, j))
    dn = dot_tn(scores_low, u_all) * scale + dot_tn(probs_low, w_all)

    def widen(values):
        values = jnp.broadcast_to(values[:, None, :], (own_caps, slots, width))
        return values.reshape(block, width)

    dn = dn + pcol * widen(d_pooled_low)
    dz = norm_back(dn, hat1, rstd1, vector(tg1)) + pcol * widen(dr1_top)
    dm[own] = dz.astype(BF)
    gathers[1].start()
    for copy in facts:
        copy.start()
    z[...] = dz
    vec[6:7] = rows_sum(dn * hat1)
    vec[7:8] = rows_sum(dn)
    vec[5:6] = rows_sum(dz)

    f_in[at.h] = f_out[at.h]
    s_in[at.h] = s_out[at.h]
    ledger.step(ends=(2,), middles=(1,), turns=(0,))
    scatter_a = scatters[2]

    def feed_back(t, carry):
        waits(t, gathers[1])
        blk = block_of(t)
        rows = pl.ds(pl.multiple_of(blk * block, block), block)
        grad = (dot_nt(dm[rows], wd[...]) * slope[rows].astype(F32)).astype(BF)
        slope[rows] = grad
        part[blk] = dot_nt(grad, wu[...]).astype(BF)
        sends(t, scatter_a)
        pl.when(t == 0)(lambda: ledger.step(ends=(3,), middles=(2,), turns=(1,), backs=(0,)))
        return carry

    lax.fori_loop(0, 4, feed_back, 0)
    gathers[1].finish()
    for copy in facts:
        copy.wait_recv()
    pooled_all = jnp.concatenate([a_in[j, 0] for j in range(4)], 0)
    da_all = jnp.concatenate([a_in[j, 1] for j in range(4)], 0)
    dq_all = jnp.concatenate([s_in[j, 1] for j in range(4)], 0)
    do_all = jnp.concatenate([s_in[j, 2] for j in range(4)], 0)
    out_all = jnp.concatenate([s_in[j, 3] for j in range(4)], 0)
    grads[2, 0:local] = dot_tn(dq_all, pooled_all).astype(BF)
    grads[2, local : 2 * local] = dot_tn(
        jnp.concatenate([stack(s_in[j, 0]) for j in range(4)], 0),
        jnp.concatenate([f_in[j, 1] for j in range(4)], 0),
    ).astype(BF)
    grads[2, 2 * local : 3 * local] = dot_tn(
        jnp.concatenate([stack(s_in[j, 2]) for j in range(4)], 0),
        jnp.concatenate([f_in[j, 0] for j in range(4)], 0),
    ).astype(BF)
    grads[2, 3 * local :] = dot_tn(out_all, da_all).astype(BF)
    ledger.open(4, 5)
    vec[20:21, 0:local] = rows_sum(dq_all.astype(F32))
    vec[21:22, 0:local] = rows_sum(do_all.astype(F32))
    ledger.step(middles=(3,), turns=(2,), backs=(1,))
    scatter_a.second()
    grads[3] = dot_tn(hid[...], dm[...]).astype(BF)
    ledger.open(6, 7)
    ledger.step(ends=(4, 5), turns=(3,), backs=(2,))
    grads[4] = dot_tn(n2[...], slope[...]).astype(BF)
    ledger.open(8, 9)
    vec[16:17] = rows_sum(slope[...].astype(F32))
    ledger.step(ends=(6,), middles=(4,), backs=(3,))
    scatter_a.wait()
    dn2 = scatter_a.total()
    scatter_a.finish()
    hat, rstd = norm_stats(r1[...])
    back = z[...] + norm_back(dn2, hat, rstd, vector(g2))
    r1[...] = back
    da[own] = back.astype(BF)
    gathers[2].start()
    vec[2:3] = rows_sum(back)
    vec[3:4] = rows_sum(dn2 * hat)
    vec[4:5] = rows_sum(dn2)

    ledger.step(ends=(7,), middles=(5,), turns=(4,))
    scatter_b = scatters[3]

    def attend_back(t, carry):
        waits(t, gathers[2])
        blk = block_of(t)
        rows = pl.ds(pl.multiple_of(blk * block, block), block)
        d_out = dot_nt(da[rows], wo[...]).astype(BF)
        query, keys, values = q[rows], k[rows], v[rows]
        parts = [[], [], []]
        for m in range(block // sub):
            cut = slice(m * sub, (m + 1) * sub)
            index = blk * (block // sub) + m
            dq = jnp.zeros((sub, local), F32)
            dk = jnp.zeros((sub, local), F32)
            dv = jnp.zeros((sub, local), F32)
            for i in range(heads):
                probs_low = p[index, i]
                probs = probs_low.astype(F32)
                d_probs = dot_nt(d_out[cut] * low_masks[i], values[cut])
                d_scores = probs * (d_probs - jnp.sum(probs * d_probs, -1, keepdims=True))
                d_scores = d_scores.astype(BF)
                dq = dq + dot(d_scores, keys[cut]) * masks[i]
                dk = dk + dot_tn(d_scores, query[cut]) * masks[i]
                dv = dv + dot_tn(probs_low, d_out[cut]) * masks[i]
            parts[0].append((dq * scale).astype(BF))
            parts[1].append((dk * scale).astype(BF))
            parts[2].append(dv.astype(BF))
        total = None
        for i in range(3):
            whole = jnp.concatenate(parts[i], 0)
            (q, k, v)[i][rows] = whole
            term = dot(whole, wqkv[i])
            total = term if total is None else total + term
        part[blk] = total.astype(BF)
        sends(t, scatter_b)
        pl.when(t == 0)(lambda: ledger.step(ends=(8,), middles=(6,), turns=(5,), backs=(4,)))
        pl.when(t == 2)(lambda: ledger.step(ends=(9,), middles=(7,), turns=(6,), backs=(5,)))
        return carry

    lax.fori_loop(0, 4, attend_back, 0)
    for i in range(2):
        grads[5, i * local : (i + 1) * local] = dot_tn((q, k)[i][...], n1[...]).astype(BF)
    ledger.open(10)
    ledger.step(middles=(8,), turns=(7,), backs=(6,))
    scatter_b.second()
    grads[5, 2 * local : 3 * local] = dot_tn(v[...], n1[...]).astype(BF)
    grads[5, 3 * local :] = dot_tn(o[...], da[...]).astype(BF)
    ledger.open(11)
    vec[18:19, 0:local] = rows_sum(q[...].astype(F32))
    vec[19:20, 0:local] = rows_sum(v[...].astype(F32))
    ledger.step(ends=(10, 11), middles=(9,), turns=(8,), backs=(7,))
    scatter_b.wait()
    dn1 = scatter_b.total()
    hat, rstd = norm_stats(x[own].astype(F32))
    dy[own] = (r1[...] + norm_back(dn1, hat, rstd, vector(g1))).astype(BF)
    gathers[3].start()
    vec[0:1] = rows_sum(dn1 * hat)
    vec[1:2] = rows_sum(dn1)

    vh_in[at.h] = vec[0:16]
    tops = [
        same_place(vh_in.at[at.h], v_sems, i, at.head(j)) for i, j in enumerate(head_peers)
    ]
    for copy in tops:
        copy.start()
    ledger.step(middles=(10,), turns=(9,), backs=(8,))
    for copy in tops:
        copy.wait_recv()
    vec[0:16] = vh_in[0] + vh_in[1] + vh_in[2] + vh_in[3]
    ledger.open(12)
    gathers[3].forward()
    ledger.step(ends=(12,), middles=(11, 12), turns=(10,), backs=(9,))
    gathers[3].wait_x()
    gathers[3].wait_y()
    ledger.step(turns=(11, 12), backs=(10,))
    gathers[3].wait_d()
    ledger.step(backs=(11, 12))
    ledger.close()
    scatter_b.finish()
    for i in (0, 2, 3):
        gathers[i].finish()
    for copy in hop1 + hop_b + hop2 + hop3 + pics + [core_pics]:
        copy.wait_send()
    for copy in rings + sums + tells + backs + facts + tops:
        copy.wait_send()


def run_kernel(dp, section, slots, x, lens, image, base, top):
    tokens, width = x.shape
    local = base[4].shape[0]
    ff = base[8].shape[1]
    block = tokens // 4
    heads = local // HEAD_DIM
    captions = image.shape[0]
    own_caps = captions // 4
    per = heads * own_caps
    everyone = dp * section * captions
    batch = min(dp, 4)
    others = dp * section - 1
    vmem = pl.BlockSpec(memory_space=pltpu.VMEM)
    shape = jax.ShapeDtypeStruct
    outs = [
        shape((tokens, width), BF),
        shape((6, width, width), BF),
        shape((32, width), F32),
    ]
    assert ff == width and 4 * local == width
    sems = pltpu.SemaphoreType.DMA
    ram = pltpu.VMEM
    half_piece = width // 4
    scratch = [
        ram((tokens, width), BF),
        ram((tokens, local), BF),
        ram((tokens, local), BF),
        ram((tokens, local), BF),
        ram((tokens // 128, heads, 128, 128), BF),
        ram((tokens, local), BF),
        ram((tokens, width), BF),
        ram((tokens, ff), BF),
        ram((tokens, ff), BF),
        ram((block, width), F32),
        ram((block, width), F32),
        ram((4, 4, local, width), BF),
        ram((4, 2, local), F32),
        ram((dp, section, captions, width), BF),
        ram((4, block, width), BF),
        ram((6, block // 2, width), BF),
        ram((4, own_caps, width), F32),
        ram((4, captions, width), BF),
        ram((dp * section, dp // batch, 8, everyone // (dp // batch) // 4), F32),
        ram((captions, everyone), F32),
        ram((captions, width), F32),
        ram((captions, width), BF),
        ram((4, own_caps, width), BF),
        ram((4, 2, per, width), BF),
        ram((4, 2, per, width), BF),
        ram((4, 4, own_caps, local), BF),
        ram((4, 4, own_caps, local), BF),
        ram((4, 2, own_caps, width), BF),
        ram((tokens, width), BF),
        ram((12, half_piece, width), BF),
        ram((12, half_piece, width), BF),
        ram((12, half_piece, width), BF),
        ram((4, 16, width), F32),
        ram((16, width), F32),
        ram((16, width), F32),
        ram((16, width), F32),
    ]
    for count in ((4, 6), (4, 6), (12,), (3,), (dp,), (others,), (18,), (3,)):
        scratch += [sems(count), sems(count)]
    scratch += [sems((13,))] * 8 + [pltpu.SemaphoreType.REGULAR((13,))]
    return pl.pallas_call(
        functools.partial(kernel, dp, section, slots),
        out_shape=outs,
        in_specs=[vmem] * 27,
        out_specs=[vmem] * 3,
        scratch_shapes=scratch,
        compiler_params=pltpu.CompilerParams(
            collective_id=0, has_side_effects=True, vmem_limit_bytes=VMEM_LIMIT
        ),
        cost_estimate=pl.CostEstimate(
            flops=14 * 10**9, bytes_accessed=40 * 10**6, transcendentals=4 * 10**6
        ),
    )(x, lens, image, *base, *top)


def on_device(dp, section, text_in, lengths, image_embed, *params):
    base, top = params[:12], params[12:]
    captions, slots, width = text_in.shape
    tokens = captions * slots
    local = base[4].shape[0]

    def layout(layer):
        return layer[:2] + (layer[2].transpose(1, 2, 0),) + layer[3:]

    dy, grads, vec = run_kernel(
        dp,
        section,
        slots,
        text_in.reshape(tokens, width),
        lengths,
        image_embed,
        layout(base),
        layout(top),
    )

    def unpack(start, rows, bu, bqv):
        down, up, attention = (grads[start + i] for i in range(3))
        return (
            vec[rows],
            vec[rows + 1],
            attention[: 3 * local].reshape(3, local, width).transpose(2, 0, 1).astype(F32),
            vec[bqv : bqv + 2, :local],
            attention[3 * local :].astype(F32),
            vec[rows + 2],
            vec[rows + 3],
            vec[rows + 4],
            up.astype(F32),
            vec[bu],
            down.astype(F32),
            vec[rows + 5],
        )

    loss = vec[22, 0] * (0.5 / (dp * section * captions))
    return (
        (loss, dy.astype(F32).reshape(captions, slots, width))
        + unpack(3, 0, 16, 18)
        + unpack(0, 6, 17, 20)
    )


def solution(mesh):
    layer_in = (
        P(),
        P(),
        P(None, None, "head"),
        P(None, "head"),
        P("head", None),
        P(),
        P(),
        P(),
        P(None, "head"),
        P("head"),
        P("head", None),
        P(),
    )
    rows = P(("dp", "section"), None, None)
    return jax.shard_map(
        functools.partial(on_device, mesh.shape["dp"], mesh.shape["section"]),
        mesh=mesh,
        in_specs=(rows, P(("dp", "section")), P(("dp", "section"), None)) + layer_in * 2,
        out_specs=(P(), rows) + layer_in * 2,
        check_vma=False,
    )
```

time: 421 us -> 228 us (0.54)
  waiting for transfers between devices: 94.9 us -> 0 us
  blocking collectives: 66.2 us -> 0 us
  local copies, waits for them, and re-layouts: 31.5 us -> 7.28 us
  between operations: 16 us -> 2.49 us
  Pallas kernels: 198 us -> 209 us
  other arithmetic: 13.6 us -> 9.12 us
    psum x1 -> x0, waiting for transfers between devices: 94.9 us -> none  [on_device(): base_big = lax.psum(tuple(firsts[1:5]), axes)]
    psum x2 -> x0, blocking collectives: 66.2 us -> none  [the longest x1 38.8 us: on_device(): vec = lax.psum(jnp.stack([firsts[5], seconds[6]], 0), axes + ('head',))]
    reshape x16 -> x0, local copies, waits for them, and re-layouts: 19.6 us -> none  [the longest x14 17.7 us: line(): return vector.reshape(1, -1)]
    pallas_call x3 -> x1, Pallas kernels: 198 us -> 209 us  [run_kernel(): pl.pallas_call(functools.partial(kernel, dp, section, slots), out_shape=o...]
    unnamed x37 -> x4, local copies, waits for them, and re-layouts: 8.91 us -> 0.98 us
    slice x1 -> x4, local copies, waits for them, and re-layouts: 0.69 us -> 6.3 us  [the longest x1 2.05 us: unpack(): vec[rows + 5]]
    convert_element_type x8 -> x3, other arithmetic: 8.69 us -> 7.04 us  [the longest x1 3.84 us: unpack(): down.astype(F32)]
  transfers between devices with their start and end apart: 1 -> 0, of which waited for: 1 -> 0; matrix products, arithmetic and copies ran while one was open for 1% -> 0% of each run, Pallas kernels for 0% -> 0%
where the time goes in v2:
time: 228 us
  Pallas kernels  209 us (92%)
  other arithmetic  9.12 us (4%)
  local copies, waits for them, and re-layouts  7.28 us (3%)
  between operations  2.49 us (1%)
    pallas_call x1, Pallas kernels, run_kernel(): pl.pallas_call(functools.partial(kernel, dp, section, slots), out_shape=o...  209 us

profile of v2, /device:TPU:0, one launch (start us, length us, event | category | flops | bytes accessed | tf_op | source)
XLA Modules:
  0.0 228.1 jit_solution(15640803013208627713)
XLA Ops:
  0.7 209.2 %shard_map.458 = (bf16[1024,768]{1,0:T(8,128)(2,1)}, bf16[6,768,768]{2,1,0:T(8,128)(2,1)}, f32[32,768]{1,0:T(8,128)}) custom-call(bf16[1024,768]{1,0:T(8,128)(2,1)} %bitcast.35, s32[64]{0:T(128)} %refs_1_.1, bf16[64,768]{1,0:T(8,128)(2,1)} %refs_2_.1, f32[768]{0:T(1024)} %refs_3_.1, f32[768]{0:T(1024)} %refs_4_.1, bf16[3,192,768]{2,1,0:T(8,128)(2,1)} %bitcast.36, ...), custom_call_target="tpu_custom_call" | custom-call | flops 14000000000 | bytes 40000000 | tf_op jit(solution)/shard_map/pallas_call | solution.py:972
  209.9 2.1 slice_reduce_fusion
  211.9 0.0 copy-start
  211.9 1.7 fusion
  213.6 2.1 convert_bitcast_fusion
  215.7 1.0 copy-done
  216.7 3.8 %bitcast_convert_fusion = (f32[768,768]{1,0:T(8,128)}, f32[768,768]{1,0:T(8,128)}, f32[768,768]{1,0:T(8,128)}, f32[768,768]{1,0:T(8,128)}) fusion(bf16[6,768,768]{2,1,0:T(8,128)(2,1)S(1)} %copy-done), kind=kLoop, calls=%fused_computation.2 | loop fusion | flops 2359296 | bytes 14155776 | tf_op jit(solution)/shard_map/convert_element_type | solution.py:1020
  220.6 0.0 copy-start.1
  220.6 1.1 bitcast_convert_fusion.4
  221.6 1.4 fusion.1
  223.0 1.2 slice.85
  224.8 0.0 copy-done.1
  224.9 2.1 convert.11
Async XLA Ops:
  211.9 4.8 %copy-start = (bf16[6,768,768]{2,1,0:T(8,128)(2,1)S(1)}, bf16[6,768,768]{2,1,0:T(8,128)(2,1)}, u32[]{:S(2)}) copy-start(bf16[6,768,768]{2,1,0:T(8,128)(2,1)} %get-tuple-element.31) | copy-start | bytes 21233668
  220.6 4.3 %copy-start.1 = (bf16[1024,768]{1,0:T(8,128)(2,1)S(1)}, bf16[1024,768]{1,0:T(8,128)(2,1)}, u32[]{:S(2)}) copy-start(bf16[1024,768]{1,0:T(8,128)(2,1)} %get-tuple-element.30) | copy-start | bytes 4718596

commit v3 on v2

--- a/solution.py
+++ b/solution.py
@@ -88,7 +88,7 @@
         barrier = pltpu.get_barrier_semaphore()
         for device in devices:
             pl.semaphore_signal(barrier, inc=1, device_id=device, device_id_type=MESH)
-        pl.semaphore_wait(barrier, len(devices))
+        return lambda: pl.semaphore_wait(barrier, len(devices))
 
 
 def remote(src, dst, send_sem, recv_sem, device):
@@ -306,11 +306,38 @@
                 pl.when(jnp.logical_not(self.outermost))(lambda: self.outward(i).start())
                 self.finish(i)
 
-    def close(self):
-        for i in range(len(self.pieces)):
-            self.last(i).wait_recv()
-            self.last(i).wait_send()
-            pl.when(jnp.logical_not(self.outermost))(lambda: self.outward(i).wait_send())
+    def close(self, i):
+        self.last(i).wait_recv()
+        self.last(i).wait_send()
+        pl.when(jnp.logical_not(self.outermost))(lambda: self.outward(i).wait_send())
+
+
+PER_ARRAY = 2
+SCHEDULE = (
+    ((0,), (), (), (), ()),
+    ((), (), (), (), ()),
+    ((1,), (), (), (), ()),
+    ((), (0,), (), (), ()),
+    ((2, 3), (1,), (0,), (), ()),
+    ((), (), (), (), ()),
+    ((), (2,), (1,), (), ()),
+    ((), (3,), (), (0,), ()),
+    ((4,), (), (), (), ()),
+    ((), (), (2,), (), (0,)),
+    ((5,), (4,), (), (1,), (1,)),
+    ((), (), (3,), (), ()),
+    ((6, 7), (5,), (4,), (2, 3), (2,)),
+    ((), (6,), (), (), (3,)),
+    ((8,), (), (5,), (4,), ()),
+    ((9,), (7,), (6,), (), (4,)),
+    ((), (), (), (5,), ()),
+    ((10,), (8,), (7,), (), (5,)),
+    ((11,), (9,), (8,), (6,), (6,)),
+    ((), (10,), (9,), (7,), (7,)),
+    ((), (), (), (8,), ()),
+    ((), (11,), (), (), ()),
+    ((), (), (10, 11), (9, 10, 11), (8, 9, 10, 11)),
+)
 
 
 def kernel(dp, section, slots, *refs):
@@ -321,10 +348,11 @@
         del refs[:count]
         return out
 
-    x, lens, image = take(3)
-    g1, c1, wqkv, bqv, wo, bo, g2, c2, wu, bu, wd, bd = take(12)
-    tg1, tc1, tqkv, tbqv, two, tbo, tg2, tc2, twu, tbu, twd, tbd = take(12)
-    dy, grads, vec = take(3)
+    far_x, lens, image = take(3)
+    g1, c1, far_qkv, bqv, far_o, bo, g2, c2, far_u, bu, far_d, bd = take(12)
+    tg1, tc1, tqkv, tbqv, two, tbo, tg2, tc2, far_tu, tbu, far_td, tbd = take(12)
+    far_dy, far_grads, vec = take(3)
+    x, wqkv, wo, wu, wd, twu, twd, dy, grads = take(9)
     n1, q, k, v, p, o, n2, hid, slope, r1, z = take(11)
     w2, b2, images = take(3)
     part, got = take(2)
@@ -337,6 +365,7 @@
         take(2) for _ in range(8)
     )
     ledger_sems = take(9)
+    in_sems, out_sems = take(2)
     assert not refs
 
     at = Place()
@@ -365,14 +394,29 @@
     def vector(ref):
         return ref[...].reshape(1, -1)
 
+    arrive = at.greet([at.head(j) for j in head_peers] + others)
+    loads = [
+        pltpu.make_async_copy(source, target, in_sems.at[i])
+        for i, (source, target) in enumerate(
+            (
+                (tqkv, w2.at[at.h, 0:3]),
+                (two, w2.at[at.h, 3]),
+                (far_x, x),
+                (far_qkv, wqkv),
+                (far_o, wo),
+                (far_u, wu),
+                (far_d, wd),
+                (far_tu, twu),
+                (far_td, twd),
+            )
+        )
+    ]
+    for copy in loads:
+        copy.start()
     pic = image[...].astype(F32)
     pic = pic * lax.rsqrt(jnp.mean(pic * pic, -1, keepdims=True) + NORM_EPS) * width ** (-0.5)
     images[at.z, at.s] = pic.astype(BF)
-    w2[at.h, 0:3] = tqkv[...]
-    w2[at.h, 3] = two[...]
     b2[at.h] = tbqv[...]
-
-    at.greet([at.head(j) for j in head_peers] + others)
 
     quarter = local // 4
     mine = lax.rem(at.z, 2) * 2 + at.s
@@ -400,6 +444,9 @@
         same_place(images.at[at.z, at.s], i_sems, i, device) for i, device in enumerate(zs)
     ]
     core_pics = same_place(images.at[:, at.s], i_sems, dp - 1, other_core)
+    for copy in loads[:2]:
+        copy.wait()
+    arrive()
     for copy in hop1 + hop_b + pics:
         copy.start()
 
@@ -464,6 +511,8 @@
         pl.when(t == 2)(scatter.send_x)
         return carry
 
+    for copy in loads[2:5]:
+        copy.wait()
     lax.fori_loop(0, 4, attend, 0)
     scatter.second()
     for i in range(3):
@@ -491,6 +540,8 @@
         pl.when(t == 3)(scatter.send_d)
 
     gathers[0].start()
+    for copy in loads[5:7]:
+        copy.wait()
 
     def feed(t, carry):
         waits(t, gathers[0])
@@ -585,8 +636,13 @@
             at.head(j),
         )
 
+    for copy in loads[7:]:
+        copy.wait()
     rings = [small(ring.at[at.h], i, j) for i, j in enumerate(head_peers)]
-    for copy in rings:
+    early = [
+        small(f_out.at[j, 0], 18 + i, j, f_in.at[at.h, 0]) for i, j in enumerate(head_peers)
+    ]
+    for copy in rings + early:
         copy.start()
     for copy in rings:
         copy.wait_recv()
@@ -672,7 +728,7 @@
     d_pool = (unit_r * width ** (-0.5)) * (text_grad - pooled * (unit_r * unit_r * inner))
     dpool[...] = d_pool
 
-    per_array = 2
+    per_array = PER_ARRAY
     span = width // per_array
     pieces = []
     for a in range(6):
@@ -681,8 +737,24 @@
             pieces.append(
                 (grads.at[a, pl.ds(n * span, span)], c_in.at[i], l_in.at[i], b_in.at[i])
             )
+    count = len(pieces)
     pieces.append((vec, vc_in, vl_in, vb_in))
     ledger = Ledger(at, dp, pieces, ledger_sems)
+
+    def opened(a):
+        ledger.open(*range(a * per_array, (a + 1) * per_array))
+
+    def flush(i):
+        a, n = divmod(i, per_array)
+        rows = pl.ds(n * span, span)
+        return pltpu.make_async_copy(grads.at[a, rows], far_grads.at[a, rows], out_sems.at[i])
+
+    def slot(number):
+        ends, middles, turns, backs, done = SCHEDULE[number]
+        ledger.step(ends, middles, turns, backs)
+        for i in done:
+            ledger.close(i)
+            flush(i).start()
 
     low = d_pool.astype(BF)
     du_top = (dot_nt(low, twd[...]) * steep).astype(BF)
@@ -695,14 +767,14 @@
     for copy in backs:
         copy.start()
     grads[0] = dot_tn(value, low).astype(BF)
-    ledger.open(0, 1)
+    opened(0)
     grads[1] = dot_tn(n2_top, du_top).astype(BF)
-    ledger.open(2, 3)
+    opened(1)
     vec[...] = jnp.zeros_like(vec)
     vec[22:23, 0:128] = jnp.broadcast_to(lost, (1, 128))
     vec[17:18] = rows_sum(du_top.astype(F32))
     rsb[at.h] = dn2b[own_rows]
-    ledger.step(ends=(0,))
+    slot(0)
     for copy in backs:
         copy.wait_recv()
     dn2 = rsb[0].astype(F32)
@@ -716,6 +788,8 @@
     vec[10:11] = rows_sum(dn2)
     vec[11:12] = rows_sum(dpool_own)
 
+    slot(1)
+
     da_top = dr1_top.astype(BF)
     a_in[at.h, 1] = da_top
     ws = []
@@ -728,7 +802,7 @@
     d_scores = probs * (d_probs - jnp.sum(probs * d_probs, -1, keepdims=True))
     scores_low = d_scores.astype(BF)
     g_rows = (dot(scores_low, normed) * scale).astype(BF)
-    ledger.step(ends=(1,), middles=(0,))
+    slot(2)
     d_pooled_low = jnp.zeros((own_caps, width), F32)
     for j in range(4):
         piece = g_rows[j * per : (j + 1) * per]
@@ -738,7 +812,7 @@
         d_pooled_low = d_pooled_low + dot(d_query, w2[j, 0])
     facts = []
     for i, j in enumerate(head_peers):
-        facts.append(small(f_out.at[j], 9 + i, j, f_in.at[at.h]))
+        facts.append(small(f_out.at[j, 1], 9 + i, j, f_in.at[at.h, 1]))
         facts.append(small(s_out.at[j], 12 + i, j, s_in.at[at.h]))
         facts.append(small(a_in.at[at.h], 15 + i, j))
     dn = dot_tn(scores_low, u_all) * scale + dot_tn(probs_low, w_all)
@@ -760,7 +834,7 @@
 
     f_in[at.h] = f_out[at.h]
     s_in[at.h] = s_out[at.h]
-    ledger.step(ends=(2,), middles=(1,), turns=(0,))
+    slot(3)
     scatter_a = scatters[2]
 
     def feed_back(t, carry):
@@ -771,12 +845,13 @@
         slope[rows] = grad
         part[blk] = dot_nt(grad, wu[...]).astype(BF)
         sends(t, scatter_a)
-        pl.when(t == 0)(lambda: ledger.step(ends=(3,), middles=(2,), turns=(1,), backs=(0,)))
+        for i in range(3):
+            pl.when(t == i)(lambda: slot(4 + i))
         return carry
 
     lax.fori_loop(0, 4, feed_back, 0)
     gathers[1].finish()
-    for copy in facts:
+    for copy in early + facts:
         copy.wait_recv()
     pooled_all = jnp.concatenate([a_in[j, 0] for j in range(4)], 0)
     da_all = jnp.concatenate([a_in[j, 1] for j in range(4)], 0)
@@ -793,18 +868,19 @@
         jnp.concatenate([f_in[j, 0] for j in range(4)], 0),
     ).astype(BF)
     grads[2, 3 * local :] = dot_tn(out_all, da_all).astype(BF)
-    ledger.open(4, 5)
+    opened(2)
     vec[20:21, 0:local] = rows_sum(dq_all.astype(F32))
     vec[21:22, 0:local] = rows_sum(do_all.astype(F32))
-    ledger.step(middles=(3,), turns=(2,), backs=(1,))
+    slot(7)
+    grads[3] = dot_tn(hid[...], dm[...]).astype(BF)
+    opened(3)
+    slot(8)
+    grads[4] = dot_tn(n2[...], slope[...]).astype(BF)
+    opened(4)
+    slot(9)
     scatter_a.second()
-    grads[3] = dot_tn(hid[...], dm[...]).astype(BF)
-    ledger.open(6, 7)
-    ledger.step(ends=(4, 5), turns=(3,), backs=(2,))
-    grads[4] = dot_tn(n2[...], slope[...]).astype(BF)
-    ledger.open(8, 9)
     vec[16:17] = rows_sum(slope[...].astype(F32))
-    ledger.step(ends=(6,), middles=(4,), backs=(3,))
+    slot(10)
     scatter_a.wait()
     dn2 = scatter_a.total()
     scatter_a.finish()
@@ -817,7 +893,7 @@
     vec[3:4] = rows_sum(dn2 * hat)
     vec[4:5] = rows_sum(dn2)
 
-    ledger.step(ends=(7,), middles=(5,), turns=(4,))
+    slot(11)
     scatter_b = scatters[3]
 
     def attend_back(t, carry):
@@ -853,22 +929,22 @@
             total = term if total is None else total + term
         part[blk] = total.astype(BF)
         sends(t, scatter_b)
-        pl.when(t == 0)(lambda: ledger.step(ends=(8,), middles=(6,), turns=(5,), backs=(4,)))
-        pl.when(t == 2)(lambda: ledger.step(ends=(9,), middles=(7,), turns=(6,), backs=(5,)))
+        for i in range(3):
+            pl.when(t == i)(lambda: slot(12 + i))
         return carry
 
     lax.fori_loop(0, 4, attend_back, 0)
     for i in range(2):
         grads[5, i * local : (i + 1) * local] = dot_tn((q, k)[i][...], n1[...]).astype(BF)
-    ledger.open(10)
-    ledger.step(middles=(8,), turns=(7,), backs=(6,))
-    scatter_b.second()
+    slot(15)
     grads[5, 2 * local : 3 * local] = dot_tn(v[...], n1[...]).astype(BF)
     grads[5, 3 * local :] = dot_tn(o[...], da[...]).astype(BF)
-    ledger.open(11)
+    opened(5)
+    slot(16)
+    scatter_b.second()
     vec[18:19, 0:local] = rows_sum(q[...].astype(F32))
     vec[19:20, 0:local] = rows_sum(v[...].astype(F32))
-    ledger.step(ends=(10, 11), middles=(9,), turns=(8,), backs=(7,))
+    slot(17)
     scatter_b.wait()
     dn1 = scatter_b.total()
     hat, rstd = norm_stats(x[own].astype(F32))
@@ -883,25 +959,34 @@
     ]
     for copy in tops:
         copy.start()
-    ledger.step(middles=(10,), turns=(9,), backs=(8,))
+    slot(18)
     for copy in tops:
         copy.wait_recv()
     vec[0:16] = vh_in[0] + vh_in[1] + vh_in[2] + vh_in[3]
-    ledger.open(12)
+    ledger.open(count)
     gathers[3].forward()
-    ledger.step(ends=(12,), middles=(11, 12), turns=(10,), backs=(9,))
+    slot(19)
+    ledger.step(ends=(count,), middles=(count,))
     gathers[3].wait_x()
     gathers[3].wait_y()
-    ledger.step(turns=(11, 12), backs=(10,))
+    slot(20)
+    ledger.step(turns=(count,))
     gathers[3].wait_d()
-    ledger.step(backs=(11, 12))
-    ledger.close()
+    spill = pltpu.make_async_copy(dy, far_dy, out_sems.at[count])
+    spill.start()
+    slot(21)
+    ledger.step(backs=(count,))
+    slot(22)
+    ledger.close(count)
+    for i in range(count):
+        flush(i).wait()
+    spill.wait()
     scatter_b.finish()
     for i in (0, 2, 3):
         gathers[i].finish()
     for copy in hop1 + hop_b + hop2 + hop3 + pics + [core_pics]:
         copy.wait_send()
-    for copy in rings + sums + tells + backs + facts + tops:
+    for copy in rings + early + sums + tells + backs + facts + tops:
         copy.wait_send()
 
 
@@ -918,6 +1003,8 @@
     batch = min(dp, 4)
     others = dp * section - 1
     vmem = pl.BlockSpec(memory_space=pltpu.VMEM)
+    hbm = pl.BlockSpec(memory_space=pl.ANY)
+    big = (0, 5, 7, 11, 13, 17, 19, 23, 25)
     shape = jax.ShapeDtypeStruct
     outs = [
         shape((tokens, width), BF),
@@ -927,8 +1014,18 @@
     assert ff == width and 4 * local == width
     sems = pltpu.SemaphoreType.DMA
     ram = pltpu.VMEM
-    half_piece = width // 4
+    half_piece = width // (2 * PER_ARRAY)
+    count = 6 * PER_ARRAY
     scratch = [
+        ram((tokens, width), BF),
+        ram((3, local, width), BF),
+        ram((local, width), BF),
+        ram((width, ff), BF),
+        ram((ff, width), BF),
+        ram((width, ff), BF),
+        ram((ff, width), BF),
+        ram((tokens, width), BF),
+        ram((6, width, width), BF),
         ram((tokens, width), BF),
         ram((tokens, local), BF),
         ram((tokens, local), BF),
@@ -958,22 +1055,23 @@
         ram((4, 4, own_caps, local), BF),
         ram((4, 2, own_caps, width), BF),
         ram((tokens, width), BF),
-        ram((12, half_piece, width), BF),
-        ram((12, half_piece, width), BF),
-        ram((12, half_piece, width), BF),
+        ram((count, half_piece, width), BF),
+        ram((count, half_piece, width), BF),
+        ram((count, half_piece, width), BF),
         ram((4, 16, width), F32),
         ram((16, width), F32),
         ram((16, width), F32),
         ram((16, width), F32),
     ]
-    for count in ((4, 6), (4, 6), (12,), (3,), (dp,), (others,), (18,), (3,)):
-        scratch += [sems(count), sems(count)]
-    scratch += [sems((13,))] * 8 + [pltpu.SemaphoreType.REGULAR((13,))]
+    for many in ((4, 6), (4, 6), (12,), (3,), (dp,), (others,), (21,), (3,)):
+        scratch += [sems(many), sems(many)]
+    scratch += [sems((count + 1,))] * 8 + [pltpu.SemaphoreType.REGULAR((count + 1,))]
+    scratch += [sems((9,)), sems((count + 1,))]
     return pl.pallas_call(
         functools.partial(kernel, dp, section, slots),
         out_shape=outs,
-        in_specs=[vmem] * 27,
-        out_specs=[vmem] * 3,
+        in_specs=[hbm if i in big else vmem for i in range(27)],
+        out_specs=[hbm, hbm, vmem],
         scratch_shapes=scratch,
         compiler_params=pltpu.CompilerParams(
             collective_id=0, has_side_effects=True, vmem_limit_bytes=VMEM_LIMIT
@@ -982,6 +1080,106 @@
             flops=14 * 10**9, bytes_accessed=40 * 10**6, transcendentals=4 * 10**6
         ),
     )(x, lens, image, *base, *top)
+
+
+def widen_kernel(local, scale, far_dy, far_grads, vec, *refs):
+    loss, text, base, top = refs[0], refs[1], refs[2:14], refs[14:26]
+    near_dy, near_grads, wide_text, wide_grads, dy_in, dy_out, g_in, g_out = refs[26:]
+    rows = wide_text.shape[0] // 4
+    width = wide_text.shape[1]
+    incoming = []
+    for a in (3, 4, 5, 0, 1, 2):
+        for n in range(4):
+            span = pl.ds(n * local, local)
+            incoming.append(
+                pltpu.make_async_copy(
+                    far_grads.at[a, span], near_grads.at[a, span], g_in.at[4 * a + n]
+                )
+            )
+    texts = []
+    for n in range(4):
+        span = pl.ds(n * rows, rows)
+        texts.append(pltpu.make_async_copy(far_dy.at[span], near_dy.at[span], dy_in.at[n]))
+    for copy in incoming + texts:
+        copy.start()
+    loss[...] = vec[22:23, 0:1] * scale
+    for layer, row, bu, bqv in ((base, 0, 16, 18), (top, 6, 17, 20)):
+        layer[0][...] = vec[row]
+        layer[1][...] = vec[row + 1]
+        layer[3][...] = vec[bqv : bqv + 2, 0:local]
+        layer[5][...] = vec[row + 2]
+        layer[6][...] = vec[row + 3]
+        layer[7][...] = vec[row + 4]
+        layer[9][...] = vec[bu]
+        layer[11][...] = vec[row + 5]
+    outgoing = []
+    for i, copy in enumerate(incoming):
+        a, n = (3, 4, 5, 0, 1, 2)[i // 4], i % 4
+        layer = base if a >= 3 else top
+        span = pl.ds(n * local, local)
+        copy.wait()
+        wide_grads[a, span] = near_grads[a, span].astype(F32)
+        if a % 3 == 2:
+            target = layer[2].at[n] if n < 3 else layer[4]
+        else:
+            target = layer[10 if a % 3 == 0 else 8].at[span]
+        outgoing.append(
+            pltpu.make_async_copy(wide_grads.at[a, span], target, g_out.at[4 * a + n])
+        )
+        outgoing[-1].start()
+    for n, copy in enumerate(texts):
+        span = pl.ds(n * rows, rows)
+        copy.wait()
+        wide_text[span] = near_dy[span].astype(F32)
+        outgoing.append(pltpu.make_async_copy(wide_text.at[span], text.at[span], dy_out.at[n]))
+        outgoing[-1].start()
+    for copy in outgoing:
+        copy.wait()
+
+
+def widen(local, scale, dy, grads, vec):
+    tokens, width = dy.shape
+    vmem = pl.BlockSpec(memory_space=pltpu.VMEM)
+    hbm = pl.BlockSpec(memory_space=pl.ANY)
+    shape = jax.ShapeDtypeStruct
+    line = (shape((width,), F32), vmem)
+    square = (shape((width, width), F32), hbm)
+    layer = [
+        line,
+        line,
+        (shape((3, local, width), F32), hbm),
+        (shape((2, local), F32), vmem),
+        (shape((local, width), F32), hbm),
+        line,
+        line,
+        line,
+        square,
+        line,
+        square,
+        line,
+    ]
+    outs = [(shape((1, 1), F32), vmem), (shape((tokens, width), F32), hbm)] + layer * 2
+    sems = pltpu.SemaphoreType.DMA
+    return pl.pallas_call(
+        functools.partial(widen_kernel, local, scale),
+        out_shape=[item[0] for item in outs],
+        in_specs=[hbm, hbm, vmem],
+        out_specs=[item[1] for item in outs],
+        scratch_shapes=[
+            pltpu.VMEM((tokens, width), BF),
+            pltpu.VMEM((6, width, width), BF),
+            pltpu.VMEM((tokens, width), F32),
+            pltpu.VMEM((6, width, width), F32),
+            sems((4,)),
+            sems((4,)),
+            sems((24,)),
+            sems((24,)),
+        ],
+        compiler_params=pltpu.CompilerParams(vmem_limit_bytes=VMEM_LIMIT),
+        cost_estimate=pl.CostEstimate(
+            flops=10**7, bytes_accessed=26 * 10**6, transcendentals=0
+        ),
+    )(dy, grads, vec)
 
 
 def on_device(dp, section, text_in, lengths, image_embed, *params):
@@ -1003,30 +1201,10 @@
         layout(base),
         layout(top),
     )
-
-    def unpack(start, rows, bu, bqv):
-        down, up, attention = (grads[start + i] for i in range(3))
-        return (
-            vec[rows],
-            vec[rows + 1],
-            attention[: 3 * local].reshape(3, local, width).transpose(2, 0, 1).astype(F32),
-            vec[bqv : bqv + 2, :local],
-            attention[3 * local :].astype(F32),
-            vec[rows + 2],
-            vec[rows + 3],
-            vec[rows + 4],
-            up.astype(F32),
-            vec[bu],
-            down.astype(F32),
-            vec[rows + 5],
-        )
-
-    loss = vec[22, 0] * (0.5 / (dp * section * captions))
-    return (
-        (loss, dy.astype(F32).reshape(captions, slots, width))
-        + unpack(3, 0, 16, 18)
-        + unpack(0, 6, 17, 20)
-    )
+    outs = list(widen(local, 0.5 / (dp * section * captions), dy, grads, vec))
+    for i in (4, 16):
+        outs[i] = outs[i].transpose(2, 0, 1)
+    return (outs[0][0, 0], outs[1].reshape(captions, slots, width)) + tuple(outs[2:])
 
 
 def solution(mesh):

time: 228 us -> 208 us (0.912)
  other arithmetic: 9.12 us -> 0 us
  local copies, waits for them, and re-layouts: 7.28 us -> 0 us
    pallas_call x1, Pallas kernels: 209 us -> 196 us  [run_kernel(): pl.pallas_call(functools.partial(kernel, dp, section, slots), out_shape=o...]
    pallas_call x0 -> x1, Pallas kernels: none -> 10.6 us  [widen(): pl.pallas_call(functools.partial(widen_kernel, local, scale), out_shape=[...]
    convert_element_type x3 -> x0, other arithmetic: 7.04 us -> none  [the longest x1 3.84 us: unpack(): down.astype(F32)]
    slice x4 -> x0, local copies, waits for them, and re-layouts: 6.3 us -> none  [the longest x1 2.05 us: unpack(): vec[rows + 5]]
where the time goes in v3:
time: 208 us
  Pallas kernels  207 us (100%)
    pallas_call x1, Pallas kernels, run_kernel(): pl.pallas_call(functools.partial(kernel, dp, section, slots), out_shape=o...  196 us
    pallas_call x1, Pallas kernels, widen(): pl.pallas_call(functools.partial(widen_kernel, local, scale), out_shape=[...  10.6 us

profile of v3, /device:TPU:0, one launch (start us, length us, event | category | flops | bytes accessed | tf_op | source)
XLA Modules:
  0.0 207.9 jit_solution(1725501543531698606)
XLA Ops:
  0.7 196.4 %shard_map.458 = (bf16[1024,768]{1,0:T(8,128)(2,1)}, bf16[6,768,768]{2,1,0:T(8,128)(2,1)}, f32[32,768]{1,0:T(8,128)}) custom-call(bf16[1024,768]{1,0:T(8,128)(2,1)} %bitcast.10, s32[64]{0:T(128)} %refs_1_.1, bf16[64,768]{1,0:T(8,128)(2,1)} %refs_2_.1, f32[768]{0:T(1024)} %refs_3_.1, f32[768]{0:T(1024)} %refs_4_.1, bf16[3,192,768]{2,1,0:T(8,128)(2,1)} %bitcast.11, ...), custom_call_target="tpu_custom_call" | custom-call | flops 14000000000 | bytes 40000000 | tf_op jit(solution)/shard_map/pallas_call | solution.py:1070
  197.1 10.6 %shard_map.459 = (f32[1,1]{1,0:T(1,128)}, f32[1024,768]{1,0:T(8,128)}, f32[768]{0:T(1024)}, f32[768]{0:T(1024)}, f32[3,192,768]{2,1,0:T(8,128)}, /*index=5*/f32[...) custom-call(bf16[1024,768]{1,0:T(8,128)(2,1)} %get-tuple-element.55., ...), custom_call_target="tpu_custom_call" | custom-call | flops 10000000 | bytes 26000000 | tf_op jit(solution)/shard_map/pallas_call | solution.py:1163

commit v4 on v3

--- a/solution.py
+++ b/solution.py
@@ -312,7 +312,10 @@
         pl.when(jnp.logical_not(self.outermost))(lambda: self.outward(i).wait_send())
 
 
-PER_ARRAY = 2
+PIECES = ((0, 0, 2), (0, 2, 2), (1, 0, 2), (1, 2, 2), (2, 0, 2), (2, 2, 2), (3, 0, 2), (3, 2, 2), (4, 0, 2), (4, 2, 2), (5, 0, 1), (5, 1, 1), (5, 2, 1), (5, 3, 1))
+RING = 8
+HOP_AT, CORE_AT = 3, 2
+VECTORS = (14, 15, 18, 19)
 SCHEDULE = (
     ((0,), (), (), (), ()),
     ((), (), (), (), ()),
@@ -330,13 +333,14 @@
     ((), (6,), (), (), (3,)),
     ((8,), (), (5,), (4,), ()),
     ((9,), (7,), (6,), (), (4,)),
-    ((), (), (), (5,), ()),
-    ((10,), (8,), (7,), (), (5,)),
-    ((11,), (9,), (8,), (6,), (6,)),
-    ((), (10,), (9,), (7,), (7,)),
-    ((), (), (), (8,), ()),
-    ((), (11,), (), (), ()),
-    ((), (), (10, 11), (9, 10, 11), (8, 9, 10, 11)),
+    ((10,), (), (), (5,), ()),
+    ((11,), (), (), (), ()),
+    ((12, 13), (8, 9), (7,), (), (5,)),
+    ((), (10,), (8,), (6,), (6,)),
+    ((), (11, 12), (9, 10), (7, 8), (7,)),
+    ((), (13,), (11, 12), (9, 10), (8, 9)),
+    ((), (), (13,), (11, 12), (10,)),
+    ((), (), (), (13,), (11, 12, 13)),
 )
 
 
@@ -352,17 +356,17 @@
     g1, c1, far_qkv, bqv, far_o, bo, g2, c2, far_u, bu, far_d, bd = take(12)
     tg1, tc1, tqkv, tbqv, two, tbo, tg2, tc2, far_tu, tbu, far_td, tbd = take(12)
     far_dy, far_grads, vec = take(3)
-    x, wqkv, wo, wu, wd, twu, twd, dy, grads = take(9)
+    x, wqkv, wo_all, wu, wd, twu, twd, dy, grads, o_all = take(10)
     n1, q, k, v, p, o, n2, hid, slope, r1, z = take(11)
     w2, b2, images = take(3)
     part, got = take(2)
-    ring, arb, stats, scored, dpool, dn2b, rsb = take(7)
+    ring, arb, stats, scored, dn2b, rsb = take(6)
     f_out, f_in, s_out, s_in, a_in = take(5)
     (da,) = take(1)
     dm = dy
-    c_in, l_in, b_in, vh_in, vc_in, vl_in, vb_in = take(7)
-    ag_sems, rs_sems, w_sems, h_sems, i_sems, st_sems, sm_sems, v_sems = (
-        take(2) for _ in range(8)
+    c_in, l_in, b_in, vh_in, vc_in, vl_in, vb_in, late, late_in, late_all = take(10)
+    ag_sems, rs_sems, w_sems, h_sems, i_sems, st_sems, sm_sems, v_sems, sp_sems, o_sems, wo_sems = (
+        take(2) for _ in range(11)
     )
     ledger_sems = take(9)
     in_sems, out_sems = take(2)
@@ -371,7 +375,7 @@
     at = Place()
     tokens, width = x.shape
     block = tokens // 4
-    local = wo.shape[0]
+    local = far_o.shape[0]
     heads = local // HEAD_DIM
     sub = 128
     captions = tokens // slots
@@ -403,7 +407,7 @@
                 (two, w2.at[at.h, 3]),
                 (far_x, x),
                 (far_qkv, wqkv),
-                (far_o, wo),
+                (far_o, wo_all.at[at.h]),
                 (far_u, wu),
                 (far_d, wd),
                 (far_tu, twu),
@@ -444,14 +448,23 @@
         same_place(images.at[at.z, at.s], i_sems, i, device) for i, device in enumerate(zs)
     ]
     core_pics = same_place(images.at[:, at.s], i_sems, dp - 1, other_core)
-    for copy in loads[:2]:
+    half = pl.ds(pl.multiple_of(at.s * (local // 2), local // 2), local // 2)
+    wo_hop = [
+        same_place(wo_all.at[at.h, half], wo_sems, i, at.head(j)) for i, j in enumerate(head_peers)
+    ]
+    wo_core = [
+        same_place(wo_all.at[j, half], wo_sems, 3 + i, other_core)
+        for i, j in enumerate(head_peers)
+    ]
+    loads[4].wait()
+    arrive()
+    for copy in wo_hop + hop_b + pics:
+        copy.start()
+    for copy in loads[:4]:
         copy.wait()
-    arrive()
-    for copy in hop1 + hop_b + pics:
-        copy.start()
 
     scatters = [
-        Scatter(at, part, got, rs_sems[0].at[i], rs_sems[1].at[i], block) for i in range(4)
+        Scatter(at, part, got, rs_sems[0].at[i], rs_sems[1].at[i], block) for i in range(3)
     ]
     gathers = [
         Gather(at, ref, ag_sems[0].at[i], ag_sems[1].at[i], block)
@@ -476,7 +489,16 @@
     row_id = lax.broadcasted_iota(jnp.int32, (sub, sub), 0) // slots
     col_id = lax.broadcasted_iota(jnp.int32, (sub, sub), 1) // slots
     same = row_id == col_id
-    scatter = scatters[0]
+    mixes = [
+        remote(
+            o.at[pl.ds(pl.multiple_of(j * block, block), block)],
+            o_all.at[at.h],
+            o_sems[0].at[i],
+            o_sems[1].at[i],
+            at.head(j),
+        )
+        for i, j in enumerate((at.hd, at.hy, at.hx))
+    ]
 
     def attend(t, carry):
         blk = block_of(3 - t)
@@ -505,22 +527,33 @@
             mixed.append(total.astype(BF))
         mixed = jnp.concatenate(mixed, 0)
         o[rows] = mixed
-        part[blk] = dot(mixed, wo[...]).astype(BF)
-        pl.when(t == 0)(scatter.send_d)
-        pl.when(t == 1)(scatter.send_y)
-        pl.when(t == 2)(scatter.send_x)
+        for i in range(3):
+            pl.when(t == i)(mixes[i].start)
+
+        @pl.when(t == HOP_AT)
+        def _():
+            for copy in hop1:
+                copy.start()
+
+        @pl.when(t == CORE_AT)
+        def _():
+            for copy in wo_hop:
+                copy.wait_recv()
+            for copy in wo_core:
+                copy.start()
+
+        @pl.when(t == 3)
+        def _():
+            o_all[at.h] = mixed
+
         return carry
 
-    for copy in loads[2:5]:
-        copy.wait()
     lax.fori_loop(0, 4, attend, 0)
-    scatter.second()
-    for i in range(3):
-        hop1[i].wait_recv()
-        hop2[i].start()
-    scatter.wait()
-    resid = x[own].astype(F32) + scatter.total() + vector(bo)
-    scatter.finish()
+    for copy in mixes + wo_core:
+        copy.wait_recv()
+    resid = x[own].astype(F32) + vector(bo)
+    for j in range(4):
+        resid = resid + dot(o_all[j], wo_all[j])
     r1[...] = resid
     hat, _ = norm_stats(resid)
     n2[own] = (hat * vector(g2) + vector(c2)).astype(BF)
@@ -540,6 +573,9 @@
         pl.when(t == 3)(scatter.send_d)
 
     gathers[0].start()
+    for i in range(3):
+        hop1[i].wait_recv()
+        hop2[i].start()
     for copy in loads[5:7]:
         copy.wait()
 
@@ -552,7 +588,7 @@
         hid[rows] = value
         slope[rows] = steep.astype(BF)
         part[blk] = dot(value, wd[...]).astype(BF)
-        sends(t, scatters[1])
+        sends(t, scatters[0])
         return carry
 
     lax.fori_loop(0, 4, feed, 0)
@@ -563,10 +599,10 @@
     for copy in pics:
         copy.wait_recv()
     core_pics.start()
-    scatters[1].second()
-    scatters[1].wait()
-    zv = r1[...] + scatters[1].total() + vector(bd)
-    scatters[1].finish()
+    scatters[0].second()
+    scatters[0].wait()
+    zv = r1[...] + scatters[0].total() + vector(bd)
+    scatters[0].finish()
     z[...] = zv
     for copy in hop_b + hop3 + [core_pics]:
         copy.wait_recv()
@@ -726,31 +762,33 @@
     text_grad = LOGIT_SCALE * text_grad
     inner = jnp.mean(pooled * text_grad, -1, keepdims=True)
     d_pool = (unit_r * width ** (-0.5)) * (text_grad - pooled * (unit_r * unit_r * inner))
-    dpool[...] = d_pool
-
-    per_array = PER_ARRAY
-    span = width // per_array
+    z[:caps] = d_pool
+
     pieces = []
-    for a in range(6):
-        for n in range(per_array):
-            i = a * per_array + n
-            pieces.append(
-                (grads.at[a, pl.ds(n * span, span)], c_in.at[i], l_in.at[i], b_in.at[i])
-            )
+    taken = 0
+    for i, (a, first, many) in enumerate(PIECES):
+        first, many = first * width // 4, many * width // 4
+        here = pl.ds(taken, many // 2)
+        lane = pl.ds(0, many // 2)
+        pieces.append(
+            (grads.at[a, pl.ds(first, many)], c_in.at[here], l_in.at[i % RING, lane], b_in.at[here])
+        )
+        taken += many // 2
     count = len(pieces)
     pieces.append((vec, vc_in, vl_in, vb_in))
     ledger = Ledger(at, dp, pieces, ledger_sems)
 
-    def opened(a):
-        ledger.open(*range(a * per_array, (a + 1) * per_array))
-
     def flush(i):
-        a, n = divmod(i, per_array)
-        rows = pl.ds(n * span, span)
+        a, first, many = PIECES[i]
+        rows = pl.ds(first * width // 4, many * width // 4)
         return pltpu.make_async_copy(grads.at[a, rows], far_grads.at[a, rows], out_sems.at[i])
 
     def slot(number):
         ends, middles, turns, backs, done = SCHEDULE[number]
+        if number in VECTORS:
+            chosen = [()] * 4
+            chosen[VECTORS.index(number)] = (count,)
+            ledger.step(*chosen)
         ledger.step(ends, middles, turns, backs)
         for i in done:
             ledger.close(i)
@@ -767,9 +805,9 @@
     for copy in backs:
         copy.start()
     grads[0] = dot_tn(value, low).astype(BF)
-    opened(0)
+    ledger.open(0, 1)
     grads[1] = dot_tn(n2_top, du_top).astype(BF)
-    opened(1)
+    ledger.open(2, 3)
     vec[...] = jnp.zeros_like(vec)
     vec[22:23, 0:128] = jnp.broadcast_to(lost, (1, 128))
     vec[17:18] = rows_sum(du_top.astype(F32))
@@ -781,7 +819,7 @@
     for j in range(1, 4):
         dn2 = dn2 + rsb[j].astype(F32)
     hat2, rstd2 = norm_stats(ring[at.h])
-    dpool_own = dpool[own_rows]
+    dpool_own = z[own_rows]
     dr1_top = dpool_own + norm_back(dn2, hat2, rstd2, vector(tg2))
     vec[8:9] = rows_sum(dr1_top)
     vec[9:10] = rows_sum(dn2 * hat2)
@@ -835,7 +873,7 @@
     f_in[at.h] = f_out[at.h]
     s_in[at.h] = s_out[at.h]
     slot(3)
-    scatter_a = scatters[2]
+    scatter_a = scatters[1]
 
     def feed_back(t, carry):
         waits(t, gathers[1])
@@ -868,15 +906,15 @@
         jnp.concatenate([f_in[j, 0] for j in range(4)], 0),
     ).astype(BF)
     grads[2, 3 * local :] = dot_tn(out_all, da_all).astype(BF)
-    opened(2)
+    ledger.open(4, 5)
     vec[20:21, 0:local] = rows_sum(dq_all.astype(F32))
     vec[21:22, 0:local] = rows_sum(do_all.astype(F32))
     slot(7)
     grads[3] = dot_tn(hid[...], dm[...]).astype(BF)
-    opened(3)
+    ledger.open(6, 7)
     slot(8)
     grads[4] = dot_tn(n2[...], slope[...]).astype(BF)
-    opened(4)
+    ledger.open(8, 9)
     slot(9)
     scatter_a.second()
     vec[16:17] = rows_sum(slope[...].astype(F32))
@@ -893,14 +931,18 @@
     vec[3:4] = rows_sum(dn2 * hat)
     vec[4:5] = rows_sum(dn2)
 
+    vh_in[at.h] = vec[0:16]
+    tops = [same_place(vh_in.at[at.h], v_sems, i, at.head(j)) for i, j in enumerate(head_peers)]
+    for copy in tops:
+        copy.start()
     slot(11)
-    scatter_b = scatters[3]
+    scatter_b = scatters[2]
 
     def attend_back(t, carry):
         waits(t, gathers[2])
         blk = block_of(t)
         rows = pl.ds(pl.multiple_of(blk * block, block), block)
-        d_out = dot_nt(da[rows], wo[...]).astype(BF)
+        d_out = dot_nt(da[rows], wo_all[at.h]).astype(BF)
         query, keys, values = q[rows], k[rows], v[rows]
         parts = [[], [], []]
         for m in range(block // sub):
@@ -931,62 +973,84 @@
         sends(t, scatter_b)
         for i in range(3):
             pl.when(t == i)(lambda: slot(12 + i))
+
+        @pl.when(t == 1)
+        def _():
+            for copy in tops:
+                copy.wait_recv()
+            vec[0:16] = vh_in[0] + vh_in[1] + vh_in[2] + vh_in[3]
+            ledger.open(count)
+
         return carry
 
     lax.fori_loop(0, 4, attend_back, 0)
-    for i in range(2):
-        grads[5, i * local : (i + 1) * local] = dot_tn((q, k)[i][...], n1[...]).astype(BF)
+    grads[5, 0:local] = dot_tn(q[...], n1[...]).astype(BF)
+    ledger.open(10)
+    grads[5, local : 2 * local] = dot_tn(k[...], n1[...]).astype(BF)
+    ledger.open(11)
     slot(15)
     grads[5, 2 * local : 3 * local] = dot_tn(v[...], n1[...]).astype(BF)
+    ledger.open(12)
+    slot(16)
     grads[5, 3 * local :] = dot_tn(o[...], da[...]).astype(BF)
-    opened(5)
-    slot(16)
+    ledger.open(13)
+    slot(17)
     scatter_b.second()
-    vec[18:19, 0:local] = rows_sum(q[...].astype(F32))
-    vec[19:20, 0:local] = rows_sum(v[...].astype(F32))
-    slot(17)
+    late[...] = jnp.zeros_like(late)
+    late[2:3, 0:local] = rows_sum(q[...].astype(F32))
+    late[3:4, 0:local] = rows_sum(v[...].astype(F32))
+    slot(18)
     scatter_b.wait()
     dn1 = scatter_b.total()
     hat, rstd = norm_stats(x[own].astype(F32))
     dy[own] = (r1[...] + norm_back(dn1, hat, rstd, vector(g1))).astype(BF)
     gathers[3].start()
-    vec[0:1] = rows_sum(dn1 * hat)
-    vec[1:2] = rows_sum(dn1)
-
-    vh_in[at.h] = vec[0:16]
-    tops = [
-        same_place(vh_in.at[at.h], v_sems, i, at.head(j)) for i, j in enumerate(head_peers)
-    ]
-    for copy in tops:
+    late[0:1] = rows_sum(dn1 * hat)
+    late[1:2] = rows_sum(dn1)
+
+    late_in[at.h] = late[...]
+    lates = [
+        same_place(late_in.at[at.h], v_sems, 3 + i, at.head(j)) for i, j in enumerate(head_peers)
+    ]
+    for copy in lates:
         copy.start()
-    slot(18)
-    for copy in tops:
+    slot(19)
+    for copy in lates:
         copy.wait_recv()
-    vec[0:16] = vh_in[0] + vh_in[1] + vh_in[2] + vh_in[3]
-    ledger.open(count)
+    late_all[place, 0:2] = late_in[0, 0:2] + late_in[1, 0:2] + late_in[2, 0:2] + late_in[3, 0:2]
+    late_all[place, 2:8] = late[2:8]
+    spreads = [
+        same_place(late_all.at[place], sp_sems, i, device) for i, device in enumerate(others)
+    ]
+    for copy in spreads:
+        copy.start()
+    slot(20)
     gathers[3].forward()
-    slot(19)
-    ledger.step(ends=(count,), middles=(count,))
+    slot(21)
     gathers[3].wait_x()
     gathers[3].wait_y()
-    slot(20)
-    ledger.step(turns=(count,))
+    slot(22)
     gathers[3].wait_d()
     spill = pltpu.make_async_copy(dy, far_dy, out_sems.at[count])
     spill.start()
-    slot(21)
-    ledger.step(backs=(count,))
-    slot(22)
+    slot(23)
+    for copy in spreads:
+        copy.wait_recv()
+    total = late_all[0]
+    for i in range(1, dp * section):
+        total = total + late_all[i]
     ledger.close(count)
+    vec[0:2] = total[0:2]
+    vec[18:20] = total[2:4]
     for i in range(count):
         flush(i).wait()
     spill.wait()
     scatter_b.finish()
     for i in (0, 2, 3):
         gathers[i].finish()
-    for copy in hop1 + hop_b + hop2 + hop3 + pics + [core_pics]:
+    for copy in hop1 + hop_b + hop2 + hop3 + pics + [core_pics] + wo_hop + wo_core + mixes:
         copy.wait_send()
-    for copy in rings + early + sums + tells + backs + facts + tops:
+    for copy in rings + early + sums + tells + backs + facts + tops + lates + spreads:
         copy.wait_send()
 
 
@@ -1014,18 +1078,19 @@
     assert ff == width and 4 * local == width
     sems = pltpu.SemaphoreType.DMA
     ram = pltpu.VMEM
-    half_piece = width // (2 * PER_ARRAY)
-    count = 6 * PER_ARRAY
+    count = len(PIECES)
+    rows = sum(piece[2] for piece in PIECES) * width // 8
     scratch = [
         ram((tokens, width), BF),
         ram((3, local, width), BF),
-        ram((local, width), BF),
+        ram((4, local, width), BF),
         ram((width, ff), BF),
         ram((ff, width), BF),
         ram((width, ff), BF),
         ram((ff, width), BF),
         ram((tokens, width), BF),
         ram((6, width, width), BF),
+        ram((4, block, local), BF),
         ram((tokens, width), BF),
         ram((tokens, local), BF),
         ram((tokens, local), BF),
@@ -1046,7 +1111,6 @@
         ram((4, captions, width), BF),
         ram((dp * section, dp // batch, 8, everyone // (dp // batch) // 4), F32),
         ram((captions, everyone), F32),
-        ram((captions, width), F32),
         ram((captions, width), BF),
         ram((4, own_caps, width), BF),
         ram((4, 2, per, width), BF),
@@ -1055,15 +1119,18 @@
         ram((4, 4, own_caps, local), BF),
         ram((4, 2, own_caps, width), BF),
         ram((tokens, width), BF),
-        ram((count, half_piece, width), BF),
-        ram((count, half_piece, width), BF),
-        ram((count, half_piece, width), BF),
+        ram((rows, width), BF),
+        ram((RING, width // 4, width), BF),
+        ram((rows, width), BF),
         ram((4, 16, width), F32),
         ram((16, width), F32),
         ram((16, width), F32),
         ram((16, width), F32),
-    ]
-    for many in ((4, 6), (4, 6), (12,), (3,), (dp,), (others,), (21,), (3,)):
+        ram((8, width), F32),
+        ram((4, 8, width), F32),
+        ram((dp * section, 8, width), F32),
+    ]
+    for many in ((4, 6), (3, 6), (12,), (3,), (dp,), (others,), (21,), (6,), (others,), (3,), (6,)):
         scratch += [sems(many), sems(many)]
     scratch += [sems((count + 1,))] * 8 + [pltpu.SemaphoreType.REGULAR((count + 1,))]
     scratch += [sems((9,)), sems((count + 1,))]

time: 208 us -> 206 us (level)
  no operation moved by 1% of the time
where the time goes in v4:
time: 206 us
  Pallas kernels  205 us (100%)
    pallas_call x1, Pallas kernels, run_kernel(): pl.pallas_call(functools.partial(kernel, dp, section, slots), out_shape=o...  194 us
    pallas_call x1, Pallas kernels, widen(): pl.pallas_call(functools.partial(widen_kernel, local, scale), out_shape=[...  10.6 us

profile of v4, /device:TPU:0, one launch (start us, length us, event | category | flops | bytes accessed | tf_op | source)
XLA Modules:
  0.0 205.8 jit_solution(2957255211258303853)
XLA Ops:
  0.7 194.3 %shard_map.458 = (bf16[1024,768]{1,0:T(8,128)(2,1)}, bf16[6,768,768]{2,1,0:T(8,128)(2,1)}, f32[32,768]{1,0:T(8,128)}) custom-call(bf16[1024,768]{1,0:T(8,128)(2,1)} %bitcast.10, s32[64]{0:T(128)} %refs_1_.1, bf16[64,768]{1,0:T(8,128)(2,1)} %refs_2_.1, f32[768]{0:T(1024)} %refs_3_.1, f32[768]{0:T(1024)} %refs_4_.1, bf16[3,192,768]{2,1,0:T(8,128)(2,1)} %bitcast.11, ...), custom_call_target="tpu_custom_call" | custom-call | flops 14000000000 | bytes 40000000 | tf_op jit(solution)/shard_map/pallas_call | solution.py:1137
  195.0 10.6 %shard_map.459 = (f32[1,1]{1,0:T(1,128)}, f32[1024,768]{1,0:T(8,128)}, f32[768]{0:T(1024)}, f32[768]{0:T(1024)}, f32[3,192,768]{2,1,0:T(8,128)}, /*index=5*/f32[...) custom-call(bf16[1024,768]{1,0:T(8,128)(2,1)} %get-tuple-element.55., ...), custom_call_target="tpu_custom_call" | custom-call | flops 10000000 | bytes 26000000 | tf_op jit(solution)/shard_map/pallas_call | solution.py:1230

commit v5 on v4

--- a/solution.py
+++ b/solution.py
@@ -314,7 +314,7 @@
 
 PIECES = ((0, 0, 2), (0, 2, 2), (1, 0, 2), (1, 2, 2), (2, 0, 2), (2, 2, 2), (3, 0, 2), (3, 2, 2), (4, 0, 2), (4, 2, 2), (5, 0, 1), (5, 1, 1), (5, 2, 1), (5, 3, 1))
 RING = 8
-HOP_AT, CORE_AT = 3, 2
+HOP_AT, PASS_AT = 2, 2
 VECTORS = (14, 15, 18, 19)
 SCHEDULE = (
     ((0,), (), (), (), ()),
@@ -426,21 +426,27 @@
     mine = lax.rem(at.z, 2) * 2 + at.s
     pair = (1 - lax.rem(at.z, 2)) * 2 + at.s
 
-    def shard_part(owner, which):
-        return w2.at[owner, :, pl.ds(pl.multiple_of(which * quarter, quarter), quarter)]
+    def shard_part(owner, which, first=0, many=4):
+        rows = pl.ds(pl.multiple_of(which * quarter, quarter), quarter)
+        return w2.at[owner, pl.ds(first, many), rows]
 
     def same_place(ref, sems, i, device):
         return remote(ref, ref, sems[0].at[i], sems[1].at[i], device)
 
     hop1 = [
-        same_place(shard_part(at.h, mine), w_sems, i, at.head(j)) for i, j in enumerate(head_peers)
+        same_place(shard_part(at.h, mine), w_sems, i, at.head(j))
+        for i, j in enumerate((at.hx, at.hy))
+    ]
+    pass1 = [
+        same_place(shard_part(at.hx, mine, 0, 2), w_sems, 2, at.head(at.hy)),
+        same_place(shard_part(at.hy, mine, 2, 2), w_sems, 3, at.head(at.hx)),
     ]
     hop_b = [same_place(b2.at[at.h], h_sems, i, at.head(j)) for i, j in enumerate(head_peers)]
     hop2 = [
-        same_place(shard_part(j, mine), w_sems, 3 + i, z_pair) for i, j in enumerate(head_peers)
+        same_place(shard_part(j, mine), w_sems, 4 + i, z_pair) for i, j in enumerate(head_peers)
     ]
     hop3 = [
-        same_place(shard_part(j, which), w_sems, 6 + 3 * n + i, other_core)
+        same_place(shard_part(j, which), w_sems, 7 + 3 * n + i, other_core)
         for i, j in enumerate(head_peers)
         for n, which in enumerate((mine, pair))
     ]
@@ -450,10 +456,21 @@
     core_pics = same_place(images.at[:, at.s], i_sems, dp - 1, other_core)
     half = pl.ds(pl.multiple_of(at.s * (local // 2), local // 2), local // 2)
     wo_hop = [
-        same_place(wo_all.at[at.h, half], wo_sems, i, at.head(j)) for i, j in enumerate(head_peers)
+        same_place(wo_all.at[at.h, half], wo_sems, i, at.head(j))
+        for i, j in enumerate((at.hx, at.hy))
+    ]
+
+    def wo_part(owner, which):
+        piece = local // 4
+        first = pl.multiple_of(at.s * (local // 2) + which * piece, piece)
+        return wo_all.at[owner, pl.ds(first, piece)]
+
+    wo_pass = [
+        same_place(wo_part(at.hx, 0), wo_sems, 2, at.head(at.hy)),
+        same_place(wo_part(at.hy, 1), wo_sems, 3, at.head(at.hx)),
     ]
     wo_core = [
-        same_place(wo_all.at[j, half], wo_sems, 3 + i, other_core)
+        same_place(wo_all.at[j, half], wo_sems, 4 + i, other_core)
         for i, j in enumerate(head_peers)
     ]
     loads[4].wait()
@@ -535,12 +552,18 @@
             for copy in hop1:
                 copy.start()
 
-        @pl.when(t == CORE_AT)
+        @pl.when(t == 1)
         def _():
             for copy in wo_hop:
                 copy.wait_recv()
-            for copy in wo_core:
+            for copy in wo_pass + wo_core[:2]:
                 copy.start()
+
+        @pl.when(t == 2)
+        def _():
+            for copy in wo_pass:
+                copy.wait_recv()
+            wo_core[2].start()
 
         @pl.when(t == 3)
         def _():
@@ -573,9 +596,10 @@
         pl.when(t == 3)(scatter.send_d)
 
     gathers[0].start()
-    for i in range(3):
-        hop1[i].wait_recv()
-        hop2[i].start()
+    for copy in hop1:
+        copy.wait_recv()
+    for copy in pass1 + hop2[:2]:
+        copy.start()
     for copy in loads[5:7]:
         copy.wait()
 
@@ -589,6 +613,13 @@
         slope[rows] = steep.astype(BF)
         part[blk] = dot(value, wd[...]).astype(BF)
         sends(t, scatters[0])
+
+        @pl.when(t == PASS_AT)
+        def _():
+            for copy in pass1:
+                copy.wait_recv()
+            hop2[2].start()
+
         return carry
 
     lax.fori_loop(0, 4, feed, 0)
@@ -1048,7 +1079,9 @@
     scatter_b.finish()
     for i in (0, 2, 3):
         gathers[i].finish()
-    for copy in hop1 + hop_b + hop2 + hop3 + pics + [core_pics] + wo_hop + wo_core + mixes:
+    for copy in hop1 + pass1 + hop_b + hop2 + hop3 + pics + [core_pics]:
+        copy.wait_send()
+    for copy in wo_hop + wo_pass + wo_core + mixes:
         copy.wait_send()
     for copy in rings + early + sums + tells + backs + facts + tops + lates + spreads:
         copy.wait_send()
@@ -1130,7 +1163,7 @@
         ram((4, 8, width), F32),
         ram((dp * section, 8, width), F32),
     ]
-    for many in ((4, 6), (3, 6), (12,), (3,), (dp,), (others,), (21,), (6,), (others,), (3,), (6,)):
+    for many in ((4, 6), (3, 6), (13,), (3,), (dp,), (others,), (21,), (6,), (others,), (3,), (7,)):
         scratch += [sems(many), sems(many)]
     scratch += [sems((count + 1,))] * 8 + [pltpu.SemaphoreType.REGULAR((count + 1,))]
     scratch += [sems((9,)), sems((count + 1,))]

time: 206 us -> 203 us (0.985)
  Pallas kernels: 205 us -> 202 us
    pallas_call x1, Pallas kernels: 194 us -> 191 us  [run_kernel(): pl.pallas_call(functools.partial(kernel, dp, section, slots), out_shape=o...]
where the time goes in v5:
time: 203 us
  Pallas kernels  202 us (100%)
    pallas_call x1, Pallas kernels, run_kernel(): pl.pallas_call(functools.partial(kernel, dp, section, slots), out_shape=o...  191 us
    pallas_call x1, Pallas kernels, widen(): pl.pallas_call(functools.partial(widen_kernel, local, scale), out_shape=[...  10.6 us

profile of v5, /device:TPU:0, one launch (start us, length us, event | category | flops | bytes accessed | tf_op | source)
XLA Modules:
  0.0 202.7 jit_solution(14077887333930880085)
XLA Ops:
  0.7 191.3 %shard_map.458 = (bf16[1024,768]{1,0:T(8,128)(2,1)}, bf16[6,768,768]{2,1,0:T(8,128)(2,1)}, f32[32,768]{1,0:T(8,128)}) custom-call(bf16[1024,768]{1,0:T(8,128)(2,1)} %bitcast.10, s32[64]{0:T(128)} %refs_1_.1, bf16[64,768]{1,0:T(8,128)(2,1)} %refs_2_.1, f32[768]{0:T(1024)} %refs_3_.1, f32[768]{0:T(1024)} %refs_4_.1, bf16[3,192,768]{2,1,0:T(8,128)(2,1)} %bitcast.11, ...), custom_call_target="tpu_custom_call" | custom-call | flops 14000000000 | bytes 40000000 | tf_op jit(solution)/shard_map/pallas_call | solution.py:1170
  192.0 10.6 %shard_map.459 = (f32[1,1]{1,0:T(1,128)}, f32[1024,768]{1,0:T(8,128)}, f32[768]{0:T(1024)}, f32[768]{0:T(1024)}, f32[3,192,768]{2,1,0:T(8,128)}, /*index=5*/f32[...) custom-call(bf16[1024,768]{1,0:T(8,128)(2,1)} %get-tuple-element.55., ...), custom_call_target="tpu_custom_call" | custom-call | flops 10000000 | bytes 26000000 | tf_op jit(solution)/shard_map/pallas_call | solution.py:1263

commit v6 on v5

--- a/solution.py
+++ b/solution.py
@@ -123,8 +123,12 @@
         ]
 
     def start(self):
-        for i in range(4):
-            self.c[i].start()
+        self.c[0].start()
+        self.c[1].start()
+
+    def start_rest(self):
+        self.c[2].start()
+        self.c[3].start()
 
     def forward(self):
         self.c[0].wait_recv()
@@ -613,6 +617,7 @@
         slope[rows] = steep.astype(BF)
         part[blk] = dot(value, wd[...]).astype(BF)
         sends(t, scatters[0])
+        pl.when(t == 0)(gathers[0].start_rest)
 
         @pl.when(t == PASS_AT)
         def _():
@@ -914,6 +919,7 @@
         slope[rows] = grad
         part[blk] = dot_nt(grad, wu[...]).astype(BF)
         sends(t, scatter_a)
+        pl.when(t == 0)(gathers[1].start_rest)
         for i in range(3):
             pl.when(t == i)(lambda: slot(4 + i))
         return carry
@@ -1002,6 +1008,7 @@
             total = term if total is None else total + term
         part[blk] = total.astype(BF)
         sends(t, scatter_b)
+        pl.when(t == 0)(gathers[2].start_rest)
         for i in range(3):
             pl.when(t == i)(lambda: slot(12 + i))
 
@@ -1045,6 +1052,7 @@
     ]
     for copy in lates:
         copy.start()
+    gathers[3].start_rest()
     slot(19)
     for copy in lates:
         copy.wait_recv()

time: 203 us -> 202 us (level)
  no operation moved by 1% of the time
where the time goes in v6:
time: 202 us; the launch traced here: 201 us
  Pallas kernels  201 us (100%)
    pallas_call x1, Pallas kernels, run_kernel(): pl.pallas_call(functools.partial(kernel, dp, section, slots), out_shape=o...  190 us
    pallas_call x1, Pallas kernels, widen(): pl.pallas_call(functools.partial(widen_kernel, local, scale), out_shape=[...  10.6 us

profile of v6, /device:TPU:0, one launch (start us, length us, event | category | flops | bytes accessed | tf_op | source)
XLA Modules:
  0.0 201.4 jit_solution(3740014276458574055)
XLA Ops:
  0.7 189.9 %shard_map.458 = (bf16[1024,768]{1,0:T(8,128)(2,1)}, bf16[6,768,768]{2,1,0:T(8,128)(2,1)}, f32[32,768]{1,0:T(8,128)}) custom-call(bf16[1024,768]{1,0:T(8,128)(2,1)} %bitcast.10, s32[64]{0:T(128)} %refs_1_.1, bf16[64,768]{1,0:T(8,128)(2,1)} %refs_2_.1, f32[768]{0:T(1024)} %refs_3_.1, f32[768]{0:T(1024)} %refs_4_.1, bf16[3,192,768]{2,1,0:T(8,128)(2,1)} %bitcast.11, ...), custom_call_target="tpu_custom_call" | custom-call | flops 14000000000 | bytes 40000000 | tf_op jit(solution)/shard_map/pallas_call | solution.py:1178
  190.6 10.6 %shard_map.459 = (f32[1,1]{1,0:T(1,128)}, f32[1024,768]{1,0:T(8,128)}, f32[768]{0:T(1024)}, f32[768]{0:T(1024)}, f32[3,192,768]{2,1,0:T(8,128)}, /*index=5*/f32[...) custom-call(bf16[1024,768]{1,0:T(8,128)(2,1)} %get-tuple-element.55., ...), custom_call_target="tpu_custom_call" | custom-call | flops 10000000 | bytes 26000000 | tf_op jit(solution)/shard_map/pallas_call | solution.py:1271

commit v7 on v6

--- a/solution.py
+++ b/solution.py
@@ -695,7 +695,7 @@
         piece = mix[j * per : (j + 1) * per]
         f_out[j, 0] = piece
         out = (pick_heads(dot_nt(piece, w2[j, 2])) + b2[j, 1:2]).astype(BF)
-        s_out[j, 3] = out
+        s_out[j, 1] = out
         attended = attended + dot(out, w2[j, 3])
     ring[at.h] = z_pool + attended + vector(tbo)
 
@@ -714,6 +714,9 @@
     early = [
         small(f_out.at[j, 0], 18 + i, j, f_in.at[at.h, 0]) for i, j in enumerate(head_peers)
     ]
+    for i, j in enumerate(head_peers):
+        early.append(small(s_out.at[j, pl.ds(0, 2)], 21 + i, j, s_in.at[at.h, pl.ds(0, 2)]))
+        early.append(small(a_in.at[at.h, 0], 24 + i, j))
     for copy in rings + early:
         copy.start()
     for copy in rings:
@@ -869,7 +872,7 @@
     ws = []
     for j in range(4):
         d_out = dot_nt(da_top, w2[j, 3]).astype(BF)
-        s_out[j, 2] = d_out
+        s_out[j, 3] = d_out
         ws.append(dot(stack(d_out), w2[j, 2]).astype(BF))
     w_all = jnp.concatenate(ws, 0)
     d_probs = dot_nt(w_all, normed)
@@ -882,13 +885,13 @@
         piece = g_rows[j * per : (j + 1) * per]
         f_out[j, 1] = piece
         d_query = pick_heads(dot_nt(piece, w2[j, 1])).astype(BF)
-        s_out[j, 1] = d_query
+        s_out[j, 2] = d_query
         d_pooled_low = d_pooled_low + dot(d_query, w2[j, 0])
     facts = []
     for i, j in enumerate(head_peers):
         facts.append(small(f_out.at[j, 1], 9 + i, j, f_in.at[at.h, 1]))
-        facts.append(small(s_out.at[j], 12 + i, j, s_in.at[at.h]))
-        facts.append(small(a_in.at[at.h], 15 + i, j))
+        facts.append(small(s_out.at[j, pl.ds(2, 2)], 12 + i, j, s_in.at[at.h, pl.ds(2, 2)]))
+        facts.append(small(a_in.at[at.h, 1], 15 + i, j))
     dn = dot_tn(scores_low, u_all) * scale + dot_tn(probs_low, w_all)
 
     def widen(values):
@@ -930,16 +933,16 @@
         copy.wait_recv()
     pooled_all = jnp.concatenate([a_in[j, 0] for j in range(4)], 0)
     da_all = jnp.concatenate([a_in[j, 1] for j in range(4)], 0)
-    dq_all = jnp.concatenate([s_in[j, 1] for j in range(4)], 0)
-    do_all = jnp.concatenate([s_in[j, 2] for j in range(4)], 0)
-    out_all = jnp.concatenate([s_in[j, 3] for j in range(4)], 0)
+    dq_all = jnp.concatenate([s_in[j, 2] for j in range(4)], 0)
+    do_all = jnp.concatenate([s_in[j, 3] for j in range(4)], 0)
+    out_all = jnp.concatenate([s_in[j, 1] for j in range(4)], 0)
     grads[2, 0:local] = dot_tn(dq_all, pooled_all).astype(BF)
     grads[2, local : 2 * local] = dot_tn(
         jnp.concatenate([stack(s_in[j, 0]) for j in range(4)], 0),
         jnp.concatenate([f_in[j, 1] for j in range(4)], 0),
     ).astype(BF)
     grads[2, 2 * local : 3 * local] = dot_tn(
-        jnp.concatenate([stack(s_in[j, 2]) for j in range(4)], 0),
+        jnp.concatenate([stack(s_in[j, 3]) for j in range(4)], 0),
         jnp.concatenate([f_in[j, 0] for j in range(4)], 0),
     ).astype(BF)
     grads[2, 3 * local :] = dot_tn(out_all, da_all).astype(BF)
@@ -1171,7 +1174,7 @@
         ram((4, 8, width), F32),
         ram((dp * section, 8, width), F32),
     ]
-    for many in ((4, 6), (3, 6), (13,), (3,), (dp,), (others,), (21,), (6,), (others,), (3,), (7,)):
+    for many in ((4, 6), (3, 6), (13,), (3,), (dp,), (others,), (27,), (6,), (others,), (3,), (7,)):
         scratch += [sems(many), sems(many)]
     scratch += [sems((count + 1,))] * 8 + [pltpu.SemaphoreType.REGULAR((count + 1,))]
     scratch += [sems((9,)), sems((count + 1,))]

time: 202 us -> 202 us (level)
  no operation moved by 1% of the time
where the time goes in v7:
time: 202 us
  Pallas kernels  201 us (100%)
    pallas_call x1, Pallas kernels, run_kernel(): pl.pallas_call(functools.partial(kernel, dp, section, slots), out_shape=o...  190 us
    pallas_call x1, Pallas kernels, widen(): pl.pallas_call(functools.partial(widen_kernel, local, scale), out_shape=[...  10.6 us

profile of v7, /device:TPU:0, one launch (start us, length us, event | category | flops | bytes accessed | tf_op | source)
XLA Modules:
  0.0 201.5 jit_solution(7027158995519560903)
XLA Ops:
  0.7 190.0 %shard_map.458 = (bf16[1024,768]{1,0:T(8,128)(2,1)}, bf16[6,768,768]{2,1,0:T(8,128)(2,1)}, f32[32,768]{1,0:T(8,128)}) custom-call(bf16[1024,768]{1,0:T(8,128)(2,1)} %bitcast.10, s32[64]{0:T(128)} %refs_1_.1, bf16[64,768]{1,0:T(8,128)(2,1)} %refs_2_.1, f32[768]{0:T(1024)} %refs_3_.1, f32[768]{0:T(1024)} %refs_4_.1, bf16[3,192,768]{2,1,0:T(8,128)(2,1)} %bitcast.11, ...), custom_call_target="tpu_custom_call" | custom-call | flops 14000000000 | bytes 40000000 | tf_op jit(solution)/shard_map/pallas_call | solution.py:1181
  190.7 10.6 %shard_map.459 = (f32[1,1]{1,0:T(1,128)}, f32[1024,768]{1,0:T(8,128)}, f32[768]{0:T(1024)}, f32[768]{0:T(1024)}, f32[3,192,768]{2,1,0:T(8,128)}, /*index=5*/f32[...) custom-call(bf16[1024,768]{1,0:T(8,128)(2,1)} %get-tuple-element.55., ...), custom_call_target="tpu_custom_call" | custom-call | flops 10000000 | bytes 26000000 | tf_op jit(solution)/shard_map/pallas_call | solution.py:1274
